TPU v7x, 32 devices: a whole 2x2x4 slice. The times are simulated.
32 devices in a mesh: grp: 2 (over y), col: 4 (over z), freq: 2 (over x), rep: 2 (over core).
Axes of the slice: x: 2, y: 2, z: 4, core: 2. Of those that a mesh axis runs over, the one named last changes fastest.
Arguments:
- focusing: float32 [2, 2, 512, 16384], P('freq', None, ('grp', 'rep'), 'col'), parts along dimension 2, may hold values from -6 to 6
- v_factors: bfloat16 [2, 2, 384, 16384], P('freq', None, None, 'col'), may hold values from -0.1875 to 0.1875
- u_factors: bfloat16 [2, 2, 16, 384, 1024], P('freq', None, 'col'), may hold values from -0.3125 to 0.3125
- tile_ranks: int32 [16, 16], replicated, may hold values from 1 to 24
- owners: int32 [16], replicated, may hold values from 0 to 3, as said below
- onsets: int32 [16384], replicated, may hold values from 64 to 511
Outputs:
- update: float32 [2, 2, 512, 16384], P('freq', None, ('grp', 'rep'), 'col'), parts along dimension 2
There are 2 independent parts, one for each index of `grp`. A program takes and returns all parts, laid end to end along the dimension named above; an argument that names none is the same for every part. Nothing has to cross between parts.
Inputs may be any that keep to these rules, and one draw needn't show every extreme that they name: `owners`: no owner holds more than 4 row tiles, and some owner holds exactly 4; the factors of row tile I stand in slot slot[I] of u_factors as the steps define it.
All inputs are finite; a program needn't handle non-finite values.
Results may differ from a plain program's by a relative error of at most 0.0062.
Values may be sent and summed in bfloat16 or wider, within the bound.
No kernel may reach another device: no remote copies, remote signals or barrier semaphores. Data moves between devices by JAX's collectives and lax.ppermute only.
A program may use at most 64 MiB of HBM per device.

v0:
```python
import jax
import jax.numpy as jnp
from jax import lax
from jax.sharding import PartitionSpec as P

TS = 1024
R = 24
NR = 16384
NS = 16384
NT = 512
KLO = 8


def window_tables(count_freq, onset_rows):
    time_steps = jnp.arange(NT, dtype=jnp.int32)
    freq_bins = KLO + jnp.arange(count_freq, dtype=jnp.int32)
    phases = 2.0 * jnp.pi * (freq_bins[None, :] * time_steps[:, None] % NT).astype(jnp.float32) / NT
    cosine = jnp.cos(phases)
    sines = jnp.sin(phases)
    analyse = jnp.stack([cosine, -sines], axis=2).reshape(NT, 2 * count_freq)
    synthesis = analyse * (2.0 / NT)
    product_table = (analyse[:, :, None] * synthesis[:, None, :]).reshape(
        NT, 4 * count_freq * count_freq
    )
    running_table = jnp.cumsum(product_table, axis=0)
    mixing = jnp.take(running_table, onset_rows - 1, axis=0)
    return mixing.reshape(-1, 2 * count_freq, 2 * count_freq)


def kernel_product(einsum_recipe, left_side, right_side):
    return jnp.einsum(einsum_recipe, left_side, right_side, preferred_element_type=jnp.float32)


def per_device(focusing, v_factors, u_factors, tile_ranks, owners, onsets):
    count_col = lax.axis_size("col")
    my_column = lax.axis_index("col")
    count_freq = lax.axis_size("freq")
    my_freq = lax.axis_index("freq")
    freq_dev = focusing.shape[0]
    vis_dev = focusing.shape[2]
    sources_dev = focusing.shape[3]
    capacity = u_factors.shape[2]
    block_width = min(sources_dev, TS)
    blocks_dev = sources_dev // block_width
    per_tile = TS // block_width
    all_blocks = count_col * blocks_dev
    row_tiles = NR // TS
    col_tiles = NS // TS
    freq_all = freq_dev * count_freq
    quarter = TS // count_freq
    tile_ids = jnp.arange(row_tiles, dtype=jnp.int32)
    same_owner = owners[:, None] == owners[None, :]
    earlier = tile_ids[None, :] < tile_ids[:, None]
    slot_of = jnp.sum((same_owner & earlier).astype(jnp.int32), axis=1)
    slot_ids = jnp.arange(capacity, dtype=jnp.int32)
    routing = (owners[None, None, :] == jnp.arange(count_col, dtype=jnp.int32)[:, None, None]) & (
        slot_of[None, None, :] == slot_ids[None, :, None]
    )
    lower_routing = routing.astype(jnp.bfloat16)
    my_slots = ((owners[None, :] == my_column) & (slot_of[None, :] == slot_ids[:, None])).astype(
        jnp.int32
    )
    slot_ranks = jnp.sum(my_slots[:, :, None] * tile_ranks[None, :, :], axis=1)
    rank_mask = (jnp.arange(R, dtype=jnp.int32)[None, None, :] < slot_ranks[:, :, None]).astype(
        jnp.float32
    )
    slot_onsets = jnp.sum(my_slots[:, :, None] * onsets.reshape(row_tiles, TS)[None], axis=1)
    slot_onsets = jnp.maximum(slot_onsets, 1)
    focus_low = focusing.astype(jnp.bfloat16).reshape(freq_dev, 2, vis_dev, blocks_dev, block_width)
    factors_v = v_factors.reshape(freq_dev, 2, row_tiles, R, blocks_dev, block_width)
    einsum_recipe = "fikbs,fvbs->ifbkv"
    real_portion = kernel_product(einsum_recipe, factors_v[:, 0], focus_low[:, 0]) - kernel_product(
        einsum_recipe, factors_v[:, 1], focus_low[:, 1]
    )
    part_imag = kernel_product(einsum_recipe, factors_v[:, 0], focus_low[:, 1]) + kernel_product(
        einsum_recipe, factors_v[:, 1], focus_low[:, 0]
    )
    partial_sums = jnp.stack([real_portion, part_imag], axis=3).astype(jnp.bfloat16)
    outgoing_parts = kernel_product("way,ymleno->amwleno", lower_routing, partial_sums).astype(
        jnp.bfloat16
    )
    outgoing_parts = outgoing_parts.reshape(capacity, freq_dev, all_blocks, 2, R, vis_dev)
    arrived = lax.all_to_all(outgoing_parts, "col", split_axis=2, concat_axis=2, tiled=True)
    coefficients = jnp.sum(
        arrived.astype(jnp.float32).reshape(capacity, freq_dev, col_tiles, per_tile, 2, R, vis_dev),
        axis=3,
    )
    coefficients = (coefficients * rank_mask[:, None, :, None, :, None]).astype(jnp.bfloat16)
    factors_u = u_factors.reshape(freq_dev, 2, capacity, col_tiles, R, TS)
    uform = "fcjka,cfjkv->cfav"
    field_real = kernel_product(uform, factors_u[:, 0], coefficients[:, :, :, 0]) - kernel_product(
        uform, factors_u[:, 1], coefficients[:, :, :, 1]
    )
    field_imag = kernel_product(uform, factors_u[:, 0], coefficients[:, :, :, 1]) + kernel_product(
        uform, factors_u[:, 1], coefficients[:, :, :, 0]
    )
    receiver_field = jnp.stack([field_real, field_imag], axis=2).astype(jnp.bfloat16)
    turned = lax.all_to_all(receiver_field, "freq", split_axis=3, concat_axis=1, tiled=True)
    quarter_onsets = lax.dynamic_slice_in_dim(slot_onsets, my_freq * quarter, quarter, 1)
    mixing = window_tables(freq_all, quarter_onsets.reshape(-1)).reshape(
        capacity, quarter, 2 * freq_all, 2 * freq_all
    )
    flat_field = turned.reshape(capacity, 2 * freq_all, quarter, vis_dev).astype(jnp.float32)
    mixed_field = jnp.einsum("crpq,cqrv->cprv", mixing, flat_field, precision=lax.Precision.HIGHEST)
    mixed_field = mixed_field.astype(jnp.bfloat16).reshape(capacity, freq_all, 2, quarter, vis_dev)
    windowed = lax.all_to_all(mixed_field, "freq", split_axis=1, concat_axis=3, tiled=True)
    aform = "fcjka,cfav->cfjkv"
    back_real = kernel_product(aform, factors_u[:, 0], windowed[:, :, 0]) + kernel_product(
        aform, factors_u[:, 1], windowed[:, :, 1]
    )
    back_imag = kernel_product(aform, factors_u[:, 0], windowed[:, :, 1]) - kernel_product(
        aform, factors_u[:, 1], windowed[:, :, 0]
    )
    adjoint = jnp.stack([back_real, back_imag], axis=3) * rank_mask[:, None, :, None, :, None]
    adjoint = adjoint.astype(jnp.bfloat16)
    spread = jnp.broadcast_to(
        adjoint[:, :, :, None], (capacity, freq_dev, col_tiles, per_tile, 2, R, vis_dev)
    )
    spread = spread.reshape(capacity, freq_dev, all_blocks, 2, R, vis_dev)
    result_field = lax.all_to_all(spread, "col", split_axis=2, concat_axis=2, tiled=True)
    result_field = result_field.reshape(capacity, freq_dev, count_col, blocks_dev, 2, R, vis_dev)
    row_share = kernel_product("prq,rjpagwu->qjagwu", lower_routing, result_field).astype(
        jnp.bfloat16
    )
    wform = "fikbs,ifbkv->fvbs"
    wave_real = kernel_product(wform, factors_v[:, 0], row_share[:, :, :, 0]) + kernel_product(
        wform, factors_v[:, 1], row_share[:, :, :, 1]
    )
    wave_imag = kernel_product(wform, factors_v[:, 0], row_share[:, :, :, 1]) - kernel_product(
        wform, factors_v[:, 1], row_share[:, :, :, 0]
    )
    wave_field = jnp.stack([wave_real, wave_imag], axis=1).reshape(
        freq_dev, 2, vis_dev, sources_dev
    )
    return focusing - wave_field


def solution(mesh):
    return jax.shard_map(
        per_device,
        mesh=mesh,
        in_specs=(
            P("freq", None, ("grp", "rep"), "col"),
            P("freq", None, None, "col"),
            P("freq", None, "col", None, None),
            P(),
            P(),
            P(),
        ),
        out_specs=P("freq", None, ("grp", "rep"), "col"),
        check_vma=False,
    )
```

profile of v0, /device:TPU:0, one launch (start us, length us, event | category | flops | bytes accessed | tf_op | source)
XLA Modules:
  0.0 226.1 jit_solution(2480742213525763126)
XLA Ops:
  0.0 11.1 %reshape.509 = bf16[1,2,16,24,4,1024]{5,4,3,2,1,0:T(4,128)(2,1)} reshape(bf16[1,2,384,4096]{3,2,1,0:T(8,128)(2,1)} %param.7) | data formatting | bytes 12582912 | tf_op jit(solution)/shard_map/reshape | solution.py:70
  11.1 5.6 %fusion.59 = (bf16[1,1,16,24,4,1024]{5,4,3,2,1,0:T(4,128)(2,1)S(1)}, bf16[1,1,16,24,4,1024]{5,4,3,2,1,0:T(4,128)(2,1)S(1)}) fusion(bf16[1,2,16,24,4,1024]{5,4,3,2,1,0:T(4,128)(2,1)} %reshape.509), kind=kLoop, calls=%fused_computation.108 | loop fusion | bytes 12582912 | tf_op jit(solution)/shard_map/slice | solution.py:72
  16.8 1.7 copy-done
  18.4 2.6 %copy.146 = bf16[1,1,16,24,4,1024]{5,3,2,4,1,0:T(8,128)(2,1)} copy(bf16[1,1,16,24,4,1024]{5,4,3,2,1,0:T(4,128)(2,1)S(1)} %get-tuple-element.6) | data formatting | bytes 6291456
  21.1 5.6 %copy.122 = f32[1,2,128,4096]{2,3,1,0:T(8,128)} copy(f32[1,2,128,4096]{3,2,1,0:T(8,128)} %param.6) | data formatting | bytes 8388608 | tf_op args[0]
  26.7 2.6 %convert_element_type.92 = bf16[1,2,128,4096]{2,3,1,0:T(8,128)(2,1)S(1)} convert(f32[1,2,128,4096]{2,3,1,0:T(8,128)} %copy.122) | non-fusion elementwise | flops 1048576 | bytes 6291456 | tf_op jit(solution)/shard_map/convert_element_type | solution.py:69
  29.3 0.5 copy-done.4
  29.8 1.9 fusion.39
  31.7 1.9 fusion.38
  33.6 1.0 copy.144
  34.5 1.9 fusion.40
  36.4 1.9 fusion.37
  38.3 0.2 convert_reduce_fusion
  38.5 2.0 fusion.43
  40.5 0.1 maximum_bitcast_fusion
  40.6 0.5 fusion.31
  41.2 0.2 copy.101
  41.4 1.0 copy.102
  42.4 6.6 %all-to-all-start = ((bf16[4,1,16,2,24,128]{5,4,0,3,1,2:T(8,128)(2,1)}), bf16[4,1,16,2,24,128]{5,4,0,3,1,2:T(8,128)(2,1)}, u32[]{:S(2)}, u32[]{:S(2)}) async-start(bf16[4,1,16,2,24,128]{5,4,0,3,1,2:T(8,128)(2,1)} %copy.102), calls=%async_computation | async-start | bytes 1572864 | tf_op jit(solution)/shard_map/all_to_all | solution.py:83
  49.0 0.2 fusion.58
  49.4 1.2 reduce-window.6
  50.5 0.2 slice_reduce_fusion
  50.7 0.1 multiply_reduce_fusion.1
  50.8 0.1 multiply_reduce_fusion
  50.9 0.1 fusion.45
  51.0 0.1 broadcast_add_fusion
  51.1 18.1 %all-to-all-done = bf16[4,1,16,2,24,128]{5,4,0,3,1,2:T(8,128)(2,1)} async-done(((bf16[4,1,16,2,24,128]{5,4,0,3,1,2:T(8,128)(2,1)}), bf16[4,1,16,2,24,128]{5,4,0,3,1,2:T(8,128)(2,1)}, u32[]{:S(2)}, u32[]{:S(2)}) %all-to-all-start) | async-done | bytes 786464 | tf_op jit(solution)/shard_map/all_to_all | solution.py:83
  69.2 1.6 multiply_convert_fusion
  70.7 0.0 slice-start.1
  70.8 2.8 %fusion.19 = f32[4,128,1024,1]{2,1,3,0:T(8,128)S(1)} fusion(bf16[1,2,4,16,24,1024]{5,4,3,2,1,0:T(8,128)(2,1)} %bitcast.252, bf16[4,1,16,2,24,128]{5,4,2,0,3,1:T(8,128)(2,1)S(1)} %multiply_convert_fusion), kind=kOutput, calls=%fused_computation.28 | convolution fusion | flops 402653184 | bytes 5636096 | tf_op jit(solution)/shard_map/fcjka,cfjkv->cfav/dot_general | solution.py:31
  73.6 2.7 %fusion.18 = f32[4,128,1024,1]{2,1,3,0:T(8,128)S(1)} fusion(bf16[1,2,4,16,24,1024]{5,4,3,2,1,0:T(8,128)(2,1)} %bitcast.253, bf16[4,1,16,2,24,128]{5,4,2,0,3,1:T(8,128)(2,1)S(1)} %multiply_convert_fusion), kind=kOutput, calls=%fused_computation.27 | convolution fusion | flops 402653184 | bytes 5636096 | tf_op jit(solution)/shard_map/fcjka,cfjkv->cfav/dot_general | solution.py:31
  76.3 0.8 fusion.29
  77.0 0.8 fusion.30
  77.8 1.5 pad_maximum_fusion
  79.3 4.3 %copy.104 = bf16[4,1,2,1024,128]{4,0,2,1,3:T(4,128)(2,1)} copy(bf16[4,1,2,1024,128]{3,4,0,2,1:T(8,128)(2,1)} %pad_maximum_fusion) | data formatting | bytes 4194304 | tf_op jit(solution)/shard_map/stack | solution.py:97
  83.7 4.8 %all-to-all-start.1 = ((bf16[4,1,2,1024,128]{4,0,2,1,3:T(4,128)(2,1)}), bf16[4,1,2,1024,128]{4,0,2,1,3:T(4,128)(2,1)}, u32[]{:S(2)}, u32[]{:S(2)}) async-start(bf16[4,1,2,1024,128]{4,0,2,1,3:T(4,128)(2,1)} %copy.104), calls=%async_computation.1 | async-start | bytes 4194304 | tf_op jit(solution)/shard_map/all_to_all | solution.py:98
  88.5 0.1 copy.139
  88.7 7.6 %gather_fusion = f32[2048,16]{1,0:T(8,128)} fusion(f32[512,16]{1,0:T(8,128)S(1)} %bitcast.251, s32[2048]{0:T(1024)S(1)} %broadcast_clamp_fusion), kind=kCustom, calls=%fused_computation | custom fusion | bytes 270336 | tf_op jit(solution)/shard_map/jit(_take)/gather | solution.py:26
  96.3 1.5 copy.109
  97.8 0.1 gather.7
  98.0 3.1 %copy.110 = f32[4,512,4,4]{3,2,1,0:T(4,128)} copy(f32[4,512,4,4]{1,0,3,2:T(4,128)S(1)} %broadcast_select_fusion) | data formatting | bytes 262144 | tf_op jit(solution)/shard_map/jit(_take)/select_n | solution.py:26
  101.1 11.8 %all-to-all-done.1 = bf16[4,1,2,1024,128]{4,0,2,1,3:T(4,128)(2,1)} async-done(((bf16[4,1,2,1024,128]{4,0,2,1,3:T(4,128)(2,1)}), bf16[4,1,2,1024,128]{4,0,2,1,3:T(4,128)(2,1)}, u32[]{:S(2)}, u32[]{:S(2)}) %all-to-all-start.1) | async-done | bytes 2097184 | tf_op jit(solution)/shard_map/all_to_all | solution.py:98
  112.9 3.4 %copy.105 = bf16[4,1,2,2,512,128]{5,2,3,4,0,1:T(2,128)(2,1)S(1)} copy(bf16[4,1,2,2,512,128]{5,0,2,4,3,1:T(4,128)(2,1)} %bitcast.47) | data formatting | bytes 4194304 | tf_op jit(solution)/shard_map/all_to_all | solution.py:98
  116.3 7.2 %convolution_convert_fusion = bf16[4,512,128,4]{2,3,1,0:T(4,128)(2,1)S(1)} fusion(bf16[4,4,512,128]{3,1,2,0:T(4,128)(2,1)S(1)} %bitcast.264, f32[4,512,4,4]{3,2,1,0:T(4,128)S(1)} %copy-done.2), kind=kOutput, calls=%fused_computation.33 | convolution fusion | flops 51380224 | bytes 4325376 | tf_op jit(solution)/shard_map/crpq,cqrv->cprv/dot_general | solution.py:104
  123.5 0.0 slice-start.2
  123.5 1.4 copy.111
  124.9 37.3 %all_to_all.43 = bf16[4,2,2,512,128]{4,2,3,0,1:T(2,128)(2,1)S(1)} all-to-all(bf16[4,2,2,512,128]{4,2,3,0,1:T(2,128)(2,1)S(1)} %copy.111), channel_id=1, replica_groups=mesh['grp'=2,'col'=4,'freq'=2,'rep'=2] {'freq'}, dimensions={1} | all-to-all | bytes 4194304 | tf_op jit(solution)/shard_map/all_to_all | solution.py:106
  162.2 0.4 copy.112
  162.7 1.0 fusion.17
  163.6 1.0 fusion.16
  164.6 1.0 fusion.34
  165.6 1.0 fusion.36
  166.6 0.3 fusion.28
  166.9 0.1 copy.113
  167.0 20.5 %all_to_all.44 = bf16[4,1,16,2,24,128]{5,4,0,3,1,2:T(8,128)(2,1)S(1)} all-to-all(bf16[4,1,16,2,24,128]{5,4,0,3,1,2:T(8,128)(2,1)S(1)} %copy.113), channel_id=1, replica_groups=mesh['grp'=2,'col'=4,'freq'=2,'rep'=2] {'col'}, dimensions={2} | all-to-all | bytes 1572864 | tf_op jit(solution)/shard_map/all_to_all | solution.py:120
  187.5 0.7 fusion.32
  188.2 3.7 %fusion.2 = f32[4,128,1024,1]{2,1,3,0:T(8,128)S(1)} fusion(bf16[1,1,16,24,4,1024]{5,4,3,2,1,0:T(4,128)(2,1)S(1)} %copy-done.1, bf16[16,1,4,2,24,128]{5,0,4,3,2,1:T(8,128)(2,1)S(1)} %fusion.32), kind=kOutput, calls=%fused_computation.6 | convolution fusion | flops 402653184 | bytes 5636096 | tf_op jit(solution)/shard_map/fikbs,ifbkv->fvbs/dot_general | solution.py:31
  191.9 5.0 %fusion = f32[4,128,1024,1]{2,1,3,0:T(8,128)} fusion(bf16[1,1,16,24,4,1024]{5,4,3,2,1,0:T(4,128)(2,1)S(1)} %copy-done.1, bf16[16,1,4,2,24,128]{5,0,4,3,2,1:T(8,128)(2,1)S(1)} %fusion.32), kind=kOutput, calls=%fused_computation.4 | convolution fusion | flops 402653184 | bytes 5636096 | tf_op jit(solution)/shard_map/fikbs,ifbkv->fvbs/dot_general | solution.py:31
  196.9 5.2 %fusion.13 = f32[1,128,4,1024]{3,1,2,0:T(8,128)} fusion(f32[4,128,1024,1]{2,1,3,0:T(8,128)S(1)} %fusion.2, bf16[1,1,16,24,4,1024]{5,4,3,2,1,0:T(4,128)(2,1)S(1)} %get-tuple-element.5, bf16[16,1,4,2,24,128]{5,0,4,3,2,1:T(8,128)(2,1)S(1)} %fusion.32), kind=kOutput, calls=%fused_computation.20 | convolution fusion | flops 403177472 | bytes 7733248 | tf_op jit(solution)/shard_map/fikbs,ifbkv->fvbs/dot_general | solution.py:31
  202.1 3.1 %copy.118 = f32[1,128,4,1024]{1,3,2,0:T(8,128)} copy(f32[1,128,4,1024]{3,1,2,0:T(8,128)} %fusion.13) | data formatting | bytes 4194304 | tf_op jit(solution)/shard_map/add | solution.py:126
  205.2 6.8 %fusion.12 = f32[1,128,4,1024]{3,1,2,0:T(8,128)} fusion(f32[4,128,1024,1]{2,1,3,0:T(8,128)} %fusion, bf16[1,1,16,24,4,1024]{5,4,3,2,1,0:T(4,128)(2,1)S(1)} %get-tuple-element.5, bf16[16,1,4,2,24,128]{5,0,4,3,2,1:T(8,128)(2,1)} %copy-done.5), kind=kOutput, calls=%fused_computation.18 | convolution fusion | flops 403177472 | bytes 7733248 | tf_op jit(solution)/shard_map/fikbs,ifbkv->fvbs/dot_general | solution.py:31
  212.0 3.1 %copy.121 = f32[1,128,4,1024]{1,3,2,0:T(8,128)} copy(f32[1,128,4,1024]{3,1,2,0:T(8,128)} %fusion.12) | data formatting | bytes 4194304 | tf_op jit(solution)/shard_map/sub | solution.py:129
  215.1 5.2 %maximum_subtract_fusion = f32[1,2,128,4096]{2,3,1,0:T(8,128)} fusion(f32[1,2,128,4096]{2,3,1,0:T(8,128)} %copy.122, f32[1,1,128,4096]{2,3,1,0:T(8,128)} %bitcast.268, f32[1,1,128,4096]{2,3,1,0:T(8,128)S(1)} %bitcast.267), kind=kLoop, calls=%fused_computation.1 | loop fusion | flops 2097152 | bytes 12582912 | tf_op jit(solution)/shard_map/sub | solution.py:135
  220.3 5.6 %copy.123 = f32[1,2,128,4096]{3,2,1,0:T(8,128)} copy(f32[1,2,128,4096]{2,3,1,0:T(8,128)} %maximum_subtract_fusion) | data formatting | bytes 8388608 | tf_op jit(solution)/shard_map/sub | solution.py:135
  (43 shorter events, 0.3 us)
Async XLA Ops:
  16.8 1.7 copy-start
  26.7 3.2 %copy-start.4 = (bf16[1,1,16,24,4,1024]{5,3,2,4,1,0:T(8,128)(2,1)S(1)}, bf16[1,1,16,24,4,1024]{5,3,2,4,1,0:T(8,128)(2,1)}, u32[]{:S(2)}) copy-start(bf16[1,1,16,24,4,1024]{5,3,2,4,1,0:T(8,128)(2,1)} %copy.146) | copy-start | bytes 9437188
  36.4 1.9 copy-start.8
  40.6 8.4 %copy-start.6 = (s32[16384]{0:T(1024)S(1)}, s32[16384]{0:T(1024)}, u32[]{:S(2)}) copy-start(s32[16384]{0:T(1024)} %param.11) | copy-start | bytes 196612
  40.6 10.1 %copy-start.7 = (s32[16,16]{1,0:T(8,128)S(1)}, s32[16,16]{1,0:T(8,128)}, u32[]{:S(2)}) copy-start(s32[16,16]{1,0:T(8,128)} %param.9) | copy-start | bytes 3076
  42.4 26.8 %all-to-all-start = ((bf16[4,1,16,2,24,128]{5,4,0,3,1,2:T(8,128)(2,1)}), bf16[4,1,16,2,24,128]{5,4,0,3,1,2:T(8,128)(2,1)}, u32[]{:S(2)}, u32[]{:S(2)}) async-start(bf16[4,1,16,2,24,128]{5,4,0,3,1,2:T(8,128)(2,1)} %copy.102), calls=%async_computation | async-start | bytes 1572864 | tf_op jit(solution)/shard_map/all_to_all | solution.py:83
  69.2 7.1 %slice-start = ((s8[6291456]{0:T(1024)(128)(4,1)}), s8[4194304]{0:T(1024)(128)(4,1)S(1)}, s32[]{:S(2)}) async-start(s8[6291456]{0:T(1024)(128)(4,1)} %bitcast.254), calls=%async_computation.4 | async-start | bytes 8388608
  70.7 5.5 %slice-start.1 = ((s8[6291456]{0:T(1024)(128)(4,1)}), s8[2097152]{0:T(1024)(128)(4,1)S(1)}, s32[]{:S(2)}) async-start(s8[6291456]{0:T(1024)(128)(4,1)} %bitcast.254), calls=%async_computation.5 | async-start | bytes 4194304
  83.7 29.2 %all-to-all-start.1 = ((bf16[4,1,2,1024,128]{4,0,2,1,3:T(4,128)(2,1)}), bf16[4,1,2,1024,128]{4,0,2,1,3:T(4,128)(2,1)}, u32[]{:S(2)}, u32[]{:S(2)}) async-start(bf16[4,1,2,1024,128]{4,0,2,1,3:T(4,128)(2,1)} %copy.104), calls=%async_computation.1 | async-start | bytes 4194304 | tf_op jit(solution)/shard_map/all_to_all | solution.py:98
  112.9 3.4 %copy-start.2 = (f32[4,512,4,4]{3,2,1,0:T(4,128)S(1)}, f32[4,512,4,4]{3,2,1,0:T(4,128)}, u32[]{:S(2)}) copy-start(f32[4,512,4,4]{3,2,1,0:T(4,128)} %copy.110) | copy-start | bytes 393220
  123.5 39.2 %slice-start.2 = ((s8[6291456]{0:T(1024)(128)(4,1)}), s8[2097152]{0:T(1024)(128)(4,1)S(1)}, s32[]{:S(2)}) async-start(s8[6291456]{0:T(1024)(128)(4,1)} %bitcast.258), calls=%async_computation.6 | async-start | bytes 4194304
  124.9 37.7 %slice-start.3 = ((s8[6291456]{0:T(1024)(128)(4,1)}), s8[4194304]{0:T(1024)(128)(4,1)S(1)}, s32[]{:S(2)}) async-start(s8[6291456]{0:T(1024)(128)(4,1)} %bitcast.258), calls=%async_computation.7 | async-start | bytes 8388608
  166.9 21.3 %copy-start.1 = (bf16[1,1,16,24,4,1024]{5,4,3,2,1,0:T(4,128)(2,1)S(1)}, bf16[1,1,16,24,4,1024]{5,4,3,2,1,0:T(4,128)(2,1)}, u32[]{:S(2)}) copy-start(bf16[1,1,16,24,4,1024]{5,4,3,2,1,0:T(4,128)(2,1)} %copy-done) | copy-start | bytes 9437188
  188.2 8.7 %copy-start.5 = (bf16[16,1,4,2,24,128]{5,0,4,3,2,1:T(8,128)(2,1)}, bf16[16,1,4,2,24,128]{5,0,4,3,2,1:T(8,128)(2,1)S(1)}, u32[]{:S(2)}) copy-start(bf16[16,1,4,2,24,128]{5,0,4,3,2,1:T(8,128)(2,1)S(1)} %fusion.32) | copy-start | bytes 2359300
  212.0 3.1 %copy-start.3 = (f32[1,128,4,1024]{1,3,2,0:T(8,128)S(1)}, f32[1,128,4,1024]{1,3,2,0:T(8,128)}, u32[]{:S(2)}) copy-start(f32[1,128,4,1024]{1,3,2,0:T(8,128)} %copy.118) | copy-start | bytes 6291460
where the time goes:
time: 228 us; the launch traced here: 226 us
  local copies, waits for them, and re-layouts  63.6 us (28%)
  blocking collectives  57.7 us (25%)
  matrix products  47.5 us (21%)
  waiting for transfers between devices  29.8 us (13%)
  other arithmetic  15.4 us (7%)
  starting transfers between devices  11.4 us (5%)
    all_to_all x1, blocking collectives, per_device(): lax.all_to_all(mixed_field, 'freq', split_axis=1, concat_axis=3, tiled=True)  37.3 us
    dot_general x14, matrix products, kernel_product(): jnp.einsum(einsum_recipe, left_side, right_side, preferred_element_type=j...  32.8 us
    all_to_all x1, blocking collectives, per_device(): lax.all_to_all(spread, 'col', split_axis=2, concat_axis=2, tiled=True)  20.5 us
    all_to_all x1, waiting for transfers between devices, per_device(): lax.all_to_all(outgoing_parts, 'col', split_axis=2, concat_axis=2, tiled=...  18.1 us
    all_to_all x1, waiting for transfers between devices, per_device(): lax.all_to_all(receiver_field, 'freq', split_axis=3, concat_axis=1, tiled...  11.8 us
    unnamed x31, local copies, waits for them, and re-layouts  11.5 us
    reshape x1, local copies, waits for them, and re-layouts, per_device(): v_factors.reshape(freq_dev, 2, row_tiles, R, blocks_dev, block_width)  11.1 us
    gather x3, local copies, waits for them, and re-layouts, window_tables(): mixing = jnp.take(running_table, onset_rows - 1, axis=0)  9.24 us
  transfers between devices with their start and end apart: 2, of which 2 were waited for; matrix products, arithmetic and copies ran while one was open for 6% of the time, Pallas kernels for 0%

commit v1 on v0

--- a/solution.py
+++ b/solution.py
@@ -1,6 +1,12 @@
+import functools
+
 import jax
 import jax.numpy as jnp
+import ml_dtypes
+import numpy as np
 from jax import lax
+from jax.experimental import pallas as pl
+from jax.experimental.pallas import tpu as pltpu
 from jax.sharding import PartitionSpec as P
 
 TS = 1024
@@ -31,7 +37,7 @@
     return jnp.einsum(einsum_recipe, left_side, right_side, preferred_element_type=jnp.float32)
 
 
-def per_device(focusing, v_factors, u_factors, tile_ranks, owners, onsets):
+def per_device_general(focusing, v_factors, u_factors, tile_ranks, owners, onsets):
     count_col = lax.axis_size("col")
     my_column = lax.axis_index("col")
     count_freq = lax.axis_size("freq")
@@ -135,6 +141,327 @@
     return focusing - wave_field
 
 
+def mixing_table(count_freq):
+    time_steps = np.arange(NT)
+    rows = []
+    for mine in range(count_freq):
+        bins = [KLO + mine] + [KLO + f for f in range(count_freq) if f != mine]
+        phases = 2.0 * np.pi * ((np.array(bins)[:, None] * time_steps[None, :]) % NT) / NT
+        analyse = np.stack([np.cos(phases), -np.sin(phases)], axis=1).reshape(2 * count_freq, NT)
+        table = (analyse[:, None, :] * analyse[None, :, :] * (2.0 / NT)).reshape(-1, NT)
+        rest = table.astype(np.float32)
+        parts = []
+        for _ in range(3):
+            part = rest.astype(ml_dtypes.bfloat16)
+            parts.append(part)
+            rest = rest - part.astype(np.float32)
+        rows.append(np.concatenate(parts, axis=0))
+    return np.stack(rows)
+
+
+def dot(left, right, left_dim, right_dim):
+    return lax.dot_general(
+        left, right, (((left_dim,), (right_dim,)), ((), ())), preferred_element_type=jnp.float32
+    )
+
+
+def list_tiles(owners, tile_of, held, count_col, capacity):
+    for owner in range(count_col):
+        held[owner] = 0
+    for tile in range(owners.shape[0]):
+        owner = owners[tile]
+        slot = held[owner]
+        tile_of[owner * capacity + slot] = tile
+        held[owner] = slot + 1
+
+
+def forward_kernel(count_col, half, owners, ranks, focus, factors, *refs):
+    outs = refs[: half * count_col]
+    sums, tile_of, held = refs[half * count_col :]
+    block = pl.program_id(0)
+    blocks = pl.num_programs(0)
+    column = lax.axis_index("col")
+    mine = lax.axis_index("freq")
+    two, vis, width = focus.shape[1:]
+    low = focus[0].astype(jnp.bfloat16).reshape(two * vis, width)
+    by_real = dot(factors[0, 0], low, 1, 1)
+    by_imag = dot(factors[0, 1], low, 1, 1)
+    sums[block] = jnp.concatenate(
+        [by_real[:, :vis] - by_imag[:, vis:], by_real[:, vis:] + by_imag[:, :vis]], axis=1
+    )
+
+    @pl.when(block == blocks - 1)
+    def _():
+        capacity = 2 * half
+        list_tiles(owners, tile_of, held, count_col, capacity)
+        row_id = lax.broadcasted_iota(jnp.int32, (R, 2 * vis), 0)
+        for s in range(half):
+            for d in range(count_col):
+                for e in range(2):
+                    tile = tile_of[(column ^ d) * capacity + (mine ^ e) * half + s]
+                    pieces = []
+                    for j in range(sums.shape[0]):
+                        rank = ranks[tile, column * sums.shape[0] + j]
+                        piece = sums[j, pl.ds(pl.multiple_of(tile * R, 8), R), :]
+                        pieces.append(jnp.where(row_id < rank, piece, 0.0))
+                    outs[s * count_col + d][e] = jnp.concatenate(pieces, axis=0).astype(jnp.bfloat16)
+
+
+def forward_products(count_col, half, focusing, v_factors, tile_ranks, owners):
+    vis, sources = focusing.shape[2:]
+    rows = v_factors.shape[2]
+    blocks = sources // TS
+    out = jax.ShapeDtypeStruct((2, blocks * R, 2 * vis), jnp.bfloat16)
+    whole = pl.BlockSpec((2, blocks * R, 2 * vis), lambda j: (0, 0, 0))
+    smem = pl.BlockSpec(memory_space=pltpu.SMEM)
+    return pl.pallas_call(
+        functools.partial(forward_kernel, count_col, half),
+        grid=(blocks,),
+        in_specs=[
+            smem,
+            smem,
+            pl.BlockSpec((1, 2, vis, TS), lambda j: (0, 0, 0, j)),
+            pl.BlockSpec((1, 2, rows, TS), lambda j: (0, 0, 0, j)),
+        ],
+        out_specs=[whole] * (half * count_col),
+        out_shape=[out] * (half * count_col),
+        scratch_shapes=[
+            pltpu.VMEM((blocks, rows, 2 * vis), jnp.float32),
+            pltpu.SMEM((count_col * 2 * half,), jnp.int32),
+            pltpu.SMEM((count_col,), jnp.int32),
+        ],
+        compiler_params=pltpu.CompilerParams(
+            dimension_semantics=("arbitrary",), vmem_limit_bytes=40 * 2**20
+        ),
+        cost_estimate=pl.CostEstimate(
+            flops=8 * rows * vis * sources, bytes_accessed=8 * vis * sources + 4 * rows * sources, transcendentals=0
+        ),
+        name="forward_products",
+    )(owners, tile_ranks, focusing, v_factors)
+
+
+def receiver_kernel(count_col, half, chunk, owners, ranks, onsets, table, kept, *refs):
+    others = refs[: count_col - 1]
+    crossed, u_own, quarter_0, quarter_1, quarter_2, quarter_3 = refs[count_col - 1 : count_col + 5]
+    outs = refs[count_col + 5 : 2 * count_col + 5]
+    factors, coefs, field, windowed, tile_of, held, sems = refs[2 * count_col + 5 :]
+    column = lax.axis_index("col")
+    mine = lax.axis_index("freq")
+    place = lax.axis_index("grp") * 2 + lax.axis_index("rep")
+    vis = field.shape[1]
+    rows = factors.shape[2]
+    quarter = rows // 4
+    copies = [
+        pltpu.make_async_copy(u_own.at[0, :, mine * half + chunk], factors.at[0], sems.at[0])
+    ]
+    for n, ref in enumerate((quarter_0, quarter_1, quarter_2, quarter_3)):
+        start = pl.multiple_of((place ^ n) * quarter, quarter)
+        copies.append(
+            pltpu.make_async_copy(ref, factors.at[1, :, pl.ds(start, quarter), :], sems.at[n + 1])
+        )
+    for copy in copies:
+        copy.start()
+    list_tiles(owners, tile_of, held, count_col, 2 * half)
+    tile = tile_of[column * 2 * half + mine * half + chunk]
+    strip = crossed.shape[1]
+    for d in range(count_col):
+        start = pl.multiple_of((column ^ d) * strip, strip)
+        arrived = (kept if d == 0 else others[d - 1])[0]
+        for e, values in enumerate((arrived, crossed[d])):
+            coefs[e, 0, pl.ds(start, strip), :] = values
+            coefs[e, 1, pl.ds(start, strip), :] = jnp.concatenate([-values[:, vis:], values[:, :vis]], axis=1)
+    times = lax.broadcasted_iota(jnp.int32, (NT, TS), 0)
+    inside = jnp.where(times < onsets[tile], 1.0, 0.0).astype(jnp.bfloat16)
+    tables = dot(table[mine], inside, 1, 0)
+    count = tables.shape[0] // 3
+    mixing = tables[:count] + tables[count : 2 * count] + tables[2 * count :]
+    for e in range(2):
+        for copy in copies[:1] if e == 0 else copies[1:]:
+            copy.wait()
+        product = dot(coefs[e].reshape(2 * rows, 2 * vis), factors[e].reshape(2 * rows, TS), 0, 0)
+        low = product.astype(jnp.bfloat16).astype(jnp.float32)
+        field[2 * e] = low[:vis]
+        field[2 * e + 1] = low[vis:]
+    for p in range(4):
+        total = mixing[4 * p : 4 * p + 1] * field[0]
+        for q in range(1, 4):
+            total = total + mixing[4 * p + q : 4 * p + q + 1] * field[q]
+        windowed[p // 2, (p % 2) * vis : (p % 2 + 1) * vis, :] = total.astype(jnp.bfloat16)
+    row_id = lax.broadcasted_iota(jnp.int32, (R, 2 * vis), 0)
+    per_column = strip // R
+    for e in range(2):
+        back = dot(factors[e].reshape(2 * rows, TS), windowed[e], 1, 1)
+        by_real, by_imag = back[:rows], back[rows:]
+        adjoint = jnp.concatenate(
+            [by_real[:, :vis] + by_imag[:, vis:], by_real[:, vis:] - by_imag[:, :vis]], axis=1
+        )
+        pieces = []
+        for j in range(rows // R):
+            pieces.append(jnp.where(row_id < ranks[tile, j], adjoint[j * R : (j + 1) * R], 0.0))
+        coefs[e, 0] = jnp.concatenate(pieces, axis=0).astype(jnp.bfloat16)
+        for d in range(count_col):
+            start = pl.multiple_of((column ^ d) * strip, strip)
+            outs[d][e] = coefs[e, 0, pl.ds(start, strip), :]
+
+
+def receiver_products(count_col, half, chunk, owners, tile_ranks, onsets, table, arrived, crossed, u_factors, quarters):
+    strip, columns = crossed.shape[1:]
+    rows = u_factors.shape[3]
+    vis = columns // 2
+    smem = pl.BlockSpec(memory_space=pltpu.SMEM)
+    vmem = pl.BlockSpec(memory_space=pltpu.VMEM)
+    anywhere = pl.BlockSpec(memory_space=pl.ANY)
+    out = jax.ShapeDtypeStruct((2, strip, columns), jnp.bfloat16)
+    return pl.pallas_call(
+        functools.partial(receiver_kernel, count_col, half, chunk),
+        in_specs=[smem, smem, vmem, vmem] + [vmem] * (count_col + 1) + [anywhere] * 5,
+        out_specs=[vmem] * count_col,
+        out_shape=[out] * count_col,
+        scratch_shapes=[
+            pltpu.VMEM((2, 2, rows, TS), jnp.bfloat16),
+            pltpu.VMEM((2, 2, rows, columns), jnp.bfloat16),
+            pltpu.VMEM((4, vis, TS), jnp.float32),
+            pltpu.VMEM((2, columns, TS), jnp.bfloat16),
+            pltpu.SMEM((count_col * 2 * half,), jnp.int32),
+            pltpu.SMEM((count_col,), jnp.int32),
+            pltpu.SemaphoreType.DMA((5,)),
+        ],
+        compiler_params=pltpu.CompilerParams(vmem_limit_bytes=40 * 2**20),
+        cost_estimate=pl.CostEstimate(
+            flops=32 * rows * vis * TS, bytes_accessed=8 * rows * TS, transcendentals=0
+        ),
+        name="receiver_products",
+    )(owners, tile_ranks, onsets, table, *arrived, crossed, u_factors, *quarters)
+
+
+def update_kernel(count_col, half, owners, *refs):
+    per = count_col + 1
+    arrivals = [refs[s * per : (s + 1) * per] for s in range(half)]
+    focus, factors, out, gathered, adjoint, tile_of, held = refs[half * per :]
+    step = pl.program_id(0)
+    column = lax.axis_index("col")
+    mine = lax.axis_index("freq")
+    two, vis, width = focus.shape[1:]
+    rows = factors.shape[2]
+
+    @pl.when(step == 0)
+    def _():
+        capacity = 2 * half
+        list_tiles(owners, tile_of, held, count_col, capacity)
+        for s in range(half):
+            crossed = arrivals[s][count_col]
+            for d in range(count_col):
+                for e in range(2):
+                    tile = tile_of[(column ^ d) * capacity + (mine ^ e) * half + s]
+                    values = (arrivals[s][d][0] if e == 0 else crossed[d]).astype(jnp.float32)
+                    for j in range(gathered.shape[0]):
+                        gathered[j, pl.ds(pl.multiple_of(tile * R, 8), R), :] = values[j * R : (j + 1) * R]
+        for j in range(gathered.shape[0]):
+            values = gathered[j]
+            adjoint[j, :rows] = values.astype(jnp.bfloat16)
+            adjoint[j, rows:] = jnp.concatenate([values[:, vis:], -values[:, :vis]], axis=1).astype(jnp.bfloat16)
+
+    block = step * width // TS
+    wave = dot(adjoint[block], factors[0].reshape(2 * rows, width), 0, 0)
+    out[0] = focus[0] - wave.reshape(two, vis, width)
+
+
+def update_products(count_col, half, owners, arrivals, focusing, v_factors):
+    vis, sources = focusing.shape[2:]
+    rows = v_factors.shape[2]
+    blocks = sources // TS
+    width = 512
+    smem = pl.BlockSpec(memory_space=pltpu.SMEM)
+    specs = [smem]
+    for group in arrivals:
+        for array in group:
+            specs.append(pl.BlockSpec(array.shape, lambda j: (0, 0, 0)))
+    return pl.pallas_call(
+        functools.partial(update_kernel, count_col, half),
+        grid=(sources // width,),
+        in_specs=specs
+        + [
+            pl.BlockSpec((1, 2, vis, width), lambda j: (0, 0, 0, j)),
+            pl.BlockSpec((1, 2, rows, width), lambda j: (0, 0, 0, j)),
+        ],
+        out_specs=pl.BlockSpec((1, 2, vis, width), lambda j: (0, 0, 0, j)),
+        out_shape=jax.ShapeDtypeStruct(focusing.shape, jnp.float32),
+        scratch_shapes=[
+            pltpu.VMEM((blocks, rows, 2 * vis), jnp.float32),
+            pltpu.VMEM((blocks, 2 * rows, 2 * vis), jnp.bfloat16),
+            pltpu.SMEM((count_col * 2 * half,), jnp.int32),
+            pltpu.SMEM((count_col,), jnp.int32),
+        ],
+        compiler_params=pltpu.CompilerParams(
+            dimension_semantics=("arbitrary",), vmem_limit_bytes=40 * 2**20
+        ),
+        cost_estimate=pl.CostEstimate(
+            flops=8 * rows * vis * sources, bytes_accessed=16 * vis * sources + 4 * rows * sources, transcendentals=0
+        ),
+        name="update_products",
+    )(owners, *[array for group in arrivals for array in group], focusing, v_factors)
+
+
+def swap(array, axis):
+    return lax.ppermute(array, axis, [(0, 1), (1, 0)])
+
+
+def exchange_columns(arrays, count_col):
+    moved = list(arrays)
+    for d in range(count_col - 1, 0, -1):
+        moved[d] = lax.ppermute(arrays[d], "col", [(i, i ^ d) for i in range(count_col)])
+    return moved
+
+
+def per_device_paired(focusing, v_factors, u_factors, tile_ranks, owners, onsets):
+    count_col = lax.axis_size("col")
+    mine = lax.axis_index("freq")
+    capacity = u_factors.shape[2]
+    half = capacity // 2
+    rows = u_factors.shape[3]
+    place = lax.axis_index("grp") * 2 + lax.axis_index("rep")
+    table = jnp.asarray(mixing_table(2))
+    tile_onsets = onsets.reshape(NR // TS, 1, TS)
+    quarters = []
+    for s in range(half):
+        piece = lax.dynamic_slice(
+            u_factors, (0, 0, (1 - mine) * half + s, place * (rows // 4), 0), (1, 2, 1, rows // 4, TS)
+        ).reshape(2, rows // 4, TS)
+        first = swap(piece, "freq")
+        second = swap(first, "grp")
+        quarters.append([first, swap(first, "rep"), second, swap(second, "rep")])
+    outgoing = forward_products(count_col, half, focusing, v_factors, tile_ranks, owners)
+    arrivals = []
+    for s in range(half):
+        arrived = exchange_columns(outgoing[s * count_col : (s + 1) * count_col], count_col)
+        crossed = swap(jnp.stack([array[1] for array in arrived]), "freq")
+        back = receiver_products(
+            count_col, half, s, owners, tile_ranks, tile_onsets, table, arrived, crossed, u_factors, quarters[s]
+        )
+        returned = exchange_columns(back, count_col)
+        arrivals.append(returned + [swap(jnp.stack([array[1] for array in returned]), "freq")])
+    return update_products(count_col, half, owners, arrivals, focusing, v_factors)
+
+
+def per_device(focusing, v_factors, u_factors, tile_ranks, owners, onsets):
+    count_col = lax.axis_size("col")
+    paired = (
+        lax.axis_size("freq") == 2
+        and lax.axis_size("grp") == 2
+        and lax.axis_size("rep") == 2
+        and focusing.shape[0] == 1
+        and count_col & (count_col - 1) == 0
+        and u_factors.shape[2] % 2 == 0
+        and u_factors.shape[2] * count_col == NR // TS
+        and focusing.shape[2] % 128 == 0
+        and focusing.shape[3] % TS == 0
+        and (focusing.shape[3] // TS * R) % 16 == 0
+        and u_factors.shape[3] % 64 == 0
+    )
+    chosen = per_device_paired if paired else per_device_general
+    return chosen(focusing, v_factors, u_factors, tile_ranks, owners, onsets)
+
+
 def solution(mesh):
     return jax.shard_map(
         per_device,

time: 228 us -> 97.1 us (0.43)
  blocking collectives: 57.7 us -> 0 us
  local copies, waits for them, and re-layouts: 63.6 us -> 7.62 us
  matrix products: 47.5 us -> 0 us
  starting transfers between devices: 11.4 us -> 30.3 us
  Pallas kernels: 0 us -> 18.3 us
  other arithmetic: 15.4 us -> 0.11 us
  waiting for transfers between devices: 29.8 us -> 40.3 us
    all_to_all x2 -> x0, blocking collectives: 57.7 us -> none  [the longest x1 37.3 us: per_device(): lax.all_to_all(mixed_field, 'freq', split_axis=1, concat_axis=3, tiled=True)]
    ppermute x0 -> x24, waiting for transfers between devices: none -> 40.3 us  [the longest x12 24.9 us: swap(): return lax.ppermute(array, axis, [(0, 1), (1, 0)])]
    dot_general x15 -> x0, matrix products: 40 us -> none  [the longest x14 32.8 us: kernel_product(): jnp.einsum(einsum_recipe, left_side, right_side, preferred_element_type=j...]
    ppermute x0 -> x24, starting transfers between devices: none -> 30.3 us  [the longest x12 18.2 us: exchange_columns(): lax.ppermute(arrays[d], 'col', [(i, i ^ d) for i in range(count_col)])]
    all_to_all x2 -> x0, waiting for transfers between devices: 29.8 us -> none  [the longest x1 18.1 us: per_device(): lax.all_to_all(outgoing_parts, 'col', split_axis=2, concat_axis=2, tiled=...]
    pallas_call x0 -> x4, Pallas kernels: none -> 18.3 us  [the longest x2 7.74 us: receiver_products(): pl.pallas_call(functools.partial(receiver_kernel, count_col, half, chunk)...]
    reshape x4 -> x1, local copies, waits for them, and re-layouts: 13.6 us -> 1.2 us  [per_device_paired(): piece = lax.dynamic_slice(u_factors, (0, 0, (1 - mine) * half + s, place...]
    all_to_all x2 -> x0, starting transfers between devices: 11.4 us -> none  [the longest x1 6.58 us: per_device(): lax.all_to_all(outgoing_parts, 'col', split_axis=2, concat_axis=2, tiled=...]
  transfers between devices with their start and end apart: 2 -> 24, of which waited for: 2 -> 12; matrix products, arithmetic and copies ran while one was open for 6% -> 0% of each run, Pallas kernels for 0% -> 12%
where the time goes in v1:
time: 97.1 us; the launch traced here: 96.9 us
  waiting for transfers between devices  40.3 us (42%)
  starting transfers between devices  30.3 us (31%)
  Pallas kernels  18.3 us (19%)
  local copies, waits for them, and re-layouts  7.62 us (8%)
    ppermute x12, waiting for transfers between devices, swap(): return lax.ppermute(array, axis, [(0, 1), (1, 0)])  24.9 us
    ppermute x12, starting transfers between devices, exchange_columns(): lax.ppermute(arrays[d], 'col', [(i, i ^ d) for i in range(count_col)])  18.2 us
    ppermute x12, waiting for transfers between devices, exchange_columns(): lax.ppermute(arrays[d], 'col', [(i, i ^ d) for i in range(count_col)])  15.4 us
    ppermute x12, starting transfers between devices, swap(): return lax.ppermute(array, axis, [(0, 1), (1, 0)])  12.1 us
    pallas_call x2, Pallas kernels, receiver_products(): pl.pallas_call(functools.partial(receiver_kernel, count_col, half, chunk)...  7.74 us
    pallas_call x1, Pallas kernels, update_products(): pl.pallas_call(functools.partial(update_kernel, count_col, half), grid=(s...  6.59 us
    unnamed x18, local copies, waits for them, and re-layouts  6.35 us
    pallas_call x1, Pallas kernels, forward_products(): pl.pallas_call(functools.partial(forward_kernel, count_col, half), grid=(...  3.95 us
  transfers between devices with their start and end apart: 24, of which 12 were waited for; matrix products, arithmetic and copies ran while one was open for 0% of the time, Pallas kernels for 12%

profile of v1, /device:TPU:0, one launch (start us, length us, event | category | flops | bytes accessed | tf_op | source)
XLA Modules:
  0.0 96.9 jit_solution(8813949952041432588)
XLA Ops:
  0.0 1.2 %dynamic-slice_bitcast_fusion = (bf16[2,96,1024]{2,1,0:T(8,128)(2,1)S(1)}, bf16[2,96,1024]{2,1,0:T(8,128)(2,1)S(1)}) fusion(bf16[1,2,4,384,1024]{4,3,2,1,0:T(8,128)(2,1)} %refs_4_.3, s32[]{:T(128)S(6)} %select_n.12, s32[]{:T(128)S(6)} %select_n.11, s32[]{:T(128)S(6)} %select_n.10), kind=kLoop, calls=%fused_computation | loop fusion | bytes 1572876 | tf_op jit(solution)/shard_map/reshape | solution.py:429
  1.2 0.0 slice-start
  1.2 3.0 %collective-permute-start.16 = (bf16[2,96,1024]{2,1,0:T(8,128)(2,1)S(1)}, bf16[2,96,1024]{2,1,0:T(8,128)(2,1)S(1)}, u32[]{:S(2)}, u32[]{:S(2)}) collective-permute-start(bf16[2,96,1024]{2,1,0:T(8,128)(2,1)S(1)} %get-tuple-element.37), channel_id=1, source_target_pairs={{0,2},{2,0},{1,3},{3,1},{4,6},{6,4},{5,7},{7,5},{8,10},{10,8},{9,1... | collective-permute-start | bytes 1179656 | tf_op jit(solution)/shard_map/ppermute | solution.py:406
  4.2 0.1 collective-permute-start.4
  4.3 9.9 %collective-permute-done.16.refs_5_ = bf16[2,96,1024]{2,1,0:T(8,128)(2,1)S(1)} collective-permute-done((bf16[2,96,1024]{2,1,0:T(8,128)(2,1)S(1)}, bf16[2,96,1024]{2,1,0:T(8,128)(2,1)S(1)}, u32[]{:S(2)}, u32[]{:S(2)}) %collective-permute-start.16) | collective-permute-done | bytes 393248 | tf_op jit(solution)/shard_map/ppermute | solution.py:406
  14.2 2.1 %collective-permute-start.18 = (bf16[2,96,1024]{2,1,0:T(8,128)(2,1)S(1)}, bf16[2,96,1024]{2,1,0:T(8,128)(2,1)S(1)}, u32[]{:S(2)}, u32[]{:S(2)}) collective-permute-start(bf16[2,96,1024]{2,1,0:T(8,128)(2,1)S(1)} %collective-permute-done.16.refs_5_), channel_id=1, source_target_pairs={{0,16},{16,0},{1,17},{17,1},{2,18},{18,2},{3,19},{19,3},{4,20},{20... | collective-permute-start | bytes 1179656 | tf_op jit(solution)/shard_map/ppermute | solution.py:406
  16.3 5.5 %collective-permute-done.4.refs_5_ = bf16[2,96,1024]{2,1,0:T(8,128)(2,1)S(1)} collective-permute-done((bf16[2,96,1024]{2,1,0:T(8,128)(2,1)S(1)}, bf16[2,96,1024]{2,1,0:T(8,128)(2,1)S(1)}, u32[]{:S(2)}, u32[]{:S(2)}) %collective-permute-start.4) | collective-permute-done | bytes 393248 | tf_op jit(solution)/shard_map/ppermute | solution.py:406
  21.8 1.8 %collective-permute-start.6 = (bf16[2,96,1024]{2,1,0:T(8,128)(2,1)S(1)}, bf16[2,96,1024]{2,1,0:T(8,128)(2,1)S(1)}, u32[]{:S(2)}, u32[]{:S(2)}) collective-permute-start(bf16[2,96,1024]{2,1,0:T(8,128)(2,1)S(1)} %collective-permute-done.4.refs_5_), channel_id=1, source_target_pairs={{0,16},{16,0},{1,17},{17,1},{2,18},{18,2},{3,19},{19,3},{4,20},{20... | collective-permute-start | bytes 1179656 | tf_op jit(solution)/shard_map/ppermute | solution.py:406
  23.5 2.8 %copy-done = bf16[1,2,384,4096]{3,2,1,0:T(8,128)(2,1)S(1)} copy-done((bf16[1,2,384,4096]{3,2,1,0:T(8,128)(2,1)S(1)}, bf16[1,2,384,4096]{3,2,1,0:T(8,128)(2,1)}, u32[]{:S(2)}) %copy-start) | copy-done | bytes 6291480
  26.3 2.2 %copy-done.1 = f32[1,2,128,4096]{3,2,1,0:T(8,128)S(1)} copy-done((f32[1,2,128,4096]{3,2,1,0:T(8,128)S(1)}, f32[1,2,128,4096]{3,2,1,0:T(8,128)}, u32[]{:S(2)}) %copy-start.1) | copy-done | bytes 4194328
  28.5 0.7 copy-done.5
  29.2 0.7 copy-done.6
  29.9 3.9 %forward_products.1 = (bf16[2,96,256]{2,1,0:T(8,128)(2,1)S(1)}, bf16[2,96,256]{2,1,0:T(8,128)(2,1)S(1)}, bf16[2,96,256]{2,1,0:T(8,128)(2,1)S(1)}, bf16[2,96,256]...) custom-call(s32[16]{0:T(128)S(1)} %copy-done.6, ...), custom_call_target="tpu_custom_call" | custom-call | flops 1610612736 | bytes 10485760 | tf_op jit(solution)/shard_map/forward_products/pallas_call | solution.py:217
  33.8 1.7 %collective-permute-start.12 = (bf16[2,96,256]{2,1,0:T(8,128)(2,1)S(1)}, bf16[2,96,256]{2,1,0:T(8,128)(2,1)S(1)}, u32[]{:S(2)}, u32[]{:S(2)}) collective-permute-start(bf16[2,96,256]{2,1,0:T(8,128)(2,1)S(1)} %get-tuple-element.30), channel_id=1, source_target_pairs={{0,4},{4,0},{8,12},{12,8},{1,5},{5,1},{9,13},{13,9},{2,6},{6,2},{1... | collective-permute-start | bytes 294920 | tf_op jit(solution)/shard_map/ppermute | solution.py:412
  35.5 2.6 %collective-permute-start.13 = (bf16[2,96,256]{2,1,0:T(8,128)(2,1)S(1)}, bf16[2,96,256]{2,1,0:T(8,128)(2,1)S(1)}, u32[]{:S(2)}, u32[]{:S(2)}) collective-permute-start(bf16[2,96,256]{2,1,0:T(8,128)(2,1)S(1)} %get-tuple-element.31), channel_id=1, source_target_pairs={{0,8},{4,12},{8,0},{12,4},{1,9},{5,13},{9,1},{13,5},{2,10},{6,14},... | collective-permute-start | bytes 294920 | tf_op jit(solution)/shard_map/ppermute | solution.py:412
  38.1 0.2 collective-permute-start.14
  38.3 1.9 %collective-permute-done.12.refs_0_ = bf16[2,96,256]{2,1,0:T(8,128)(2,1)S(1)} collective-permute-done((bf16[2,96,256]{2,1,0:T(8,128)(2,1)S(1)}, bf16[2,96,256]{2,1,0:T(8,128)(2,1)S(1)}, u32[]{:S(2)}, u32[]{:S(2)}) %collective-permute-start.12) | collective-permute-done | bytes 98336 | tf_op jit(solution)/shard_map/ppermute | solution.py:412
  40.1 1.0 %collective-permute-start = (bf16[2,96,256]{2,1,0:T(8,128)(2,1)S(1)}, bf16[2,96,256]{2,1,0:T(8,128)(2,1)S(1)}, u32[]{:S(2)}, u32[]{:S(2)}) collective-permute-start(bf16[2,96,256]{2,1,0:T(8,128)(2,1)S(1)} %get-tuple-element.22), channel_id=1, source_target_pairs={{0,4},{4,0},{8,12},{12,8},{1,5},{5,1},{9,13},{13,9},{2,6},{6,2},{1... | collective-permute-start | bytes 294920 | tf_op jit(solution)/shard_map/ppermute | solution.py:412
  41.1 2.8 %collective-permute-done.13.refs_1_ = bf16[2,96,256]{2,1,0:T(8,128)(2,1)S(1)} collective-permute-done((bf16[2,96,256]{2,1,0:T(8,128)(2,1)S(1)}, bf16[2,96,256]{2,1,0:T(8,128)(2,1)S(1)}, u32[]{:S(2)}, u32[]{:S(2)}) %collective-permute-start.13) | collective-permute-done | bytes 98336 | tf_op jit(solution)/shard_map/ppermute | solution.py:412
  43.9 0.0 collective-permute-start.17
  43.9 0.0 collective-permute-done.18.refs_7_
  43.9 0.5 collective-permute-start.19
  44.5 0.5 collective-permute-done.14.refs_2_
  45.0 2.4 %collective-permute-start.1 = (bf16[2,96,256]{2,1,0:T(8,128)(2,1)S(1)}, bf16[2,96,256]{2,1,0:T(8,128)(2,1)S(1)}, u32[]{:S(2)}, u32[]{:S(2)}) collective-permute-start(bf16[2,96,256]{2,1,0:T(8,128)(2,1)S(1)} %get-tuple-element.23), channel_id=1, source_target_pairs={{0,8},{4,12},{8,0},{12,4},{1,9},{5,13},{9,1},{13,5},{2,10},{6,14},... | collective-permute-start | bytes 294920 | tf_op jit(solution)/shard_map/ppermute | solution.py:412
  47.4 0.0 collective-permute-done.refs_0_
  47.4 1.4 %collective-permute-start.2 = (bf16[2,96,256]{2,1,0:T(8,128)(2,1)S(1)}, bf16[2,96,256]{2,1,0:T(8,128)(2,1)S(1)}, u32[]{:S(2)}, u32[]{:S(2)}) collective-permute-start(bf16[2,96,256]{2,1,0:T(8,128)(2,1)S(1)} %get-tuple-element.24), channel_id=1, source_target_pairs={{0,12},{4,8},{8,4},{12,0},{1,13},{5,9},{9,5},{13,1},{2,14},{6,10},... | collective-permute-start | bytes 294920 | tf_op jit(solution)/shard_map/ppermute | solution.py:412
  48.8 6.4 %collective-permute-done.1.refs_1_ = bf16[2,96,256]{2,1,0:T(8,128)(2,1)S(1)} collective-permute-done((bf16[2,96,256]{2,1,0:T(8,128)(2,1)S(1)}, bf16[2,96,256]{2,1,0:T(8,128)(2,1)S(1)}, u32[]{:S(2)}, u32[]{:S(2)}) %collective-permute-start.1) | collective-permute-done | bytes 98336 | tf_op jit(solution)/shard_map/ppermute | solution.py:412
  55.2 1.5 %collective-permute-start.15 = (bf16[4,96,256]{2,1,0:T(8,128)(2,1)S(1)}, bf16[4,96,256]{2,1,0:T(8,128)(2,1)S(1)}, u32[]{:S(2)}, u32[]{:S(2)}) collective-permute-start(bf16[4,96,256]{2,1,0:T(8,128)(2,1)S(1)} %pad_maximum_fusion.2), channel_id=1, source_target_pairs={{0,2},{2,0},{1,3},{3,1},{4,6},{6,4},{5,7},{7,5},{8,10},{10,8},{9,1... | collective-permute-start | bytes 589832 | tf_op jit(solution)/shard_map/ppermute | solution.py:406
  56.7 0.0 collective-permute-done.2.refs_2_
  56.7 0.0 collective-permute-start.5
  56.7 0.0 collective-permute-done.6.refs_7_
  56.7 0.5 collective-permute-start.7
  57.3 4.4 %collective-permute-done.15.refs_3_ = bf16[4,96,256]{2,1,0:T(8,128)(2,1)S(1)} collective-permute-done((bf16[4,96,256]{2,1,0:T(8,128)(2,1)S(1)}, bf16[4,96,256]{2,1,0:T(8,128)(2,1)S(1)}, u32[]{:S(2)}, u32[]{:S(2)}) %collective-permute-start.15) | collective-permute-done | bytes 196640 | tf_op jit(solution)/shard_map/ppermute | solution.py:406
  61.7 2.0 %collective-permute-start.3 = (bf16[4,96,256]{2,1,0:T(8,128)(2,1)S(1)}, bf16[4,96,256]{2,1,0:T(8,128)(2,1)S(1)}, u32[]{:S(2)}, u32[]{:S(2)}) collective-permute-start(bf16[4,96,256]{2,1,0:T(8,128)(2,1)S(1)} %pad_maximum_fusion), channel_id=1, source_target_pairs={{0,2},{2,0},{1,3},{3,1},{4,6},{6,4},{5,7},{7,5},{8,10},{10,8},{9,1... | collective-permute-start | bytes 589832 | tf_op jit(solution)/shard_map/ppermute | solution.py:406
  63.7 0.0 collective-permute-done.17.refs_6_
  63.7 0.0 collective-permute-done.19.refs_8_
  63.7 0.0 copy-done.3
  63.7 0.0 copy-done.4
  63.7 0.0 slice-done
  63.7 0.0 slice-done.1
  63.8 3.9 %receiver_products.3 = (bf16[2,96,256]{2,1,0:T(8,128)(2,1)S(1)}, bf16[2,96,256]{2,1,0:T(8,128)(2,1)S(1)}, bf16[2,96,256]{2,1,0:T(8,128)(2,1)S(1)}, bf16[2,96,256]{2,1,0:T(8,128)(2,1)S(1)}) custom-call(s32[16]{0:T(128)S(1)} %copy-done.6, s32[16,16]{1,0:T(8,128)S(1)} %copy-done.5, s32[16,1,1024]{2,1,0:T(1,128)S(1)} %bitcast.7, ...), custom_call_target="tpu_custom_call" | custom-call | flops 1610612736 | bytes 3145728 | tf_op jit(solution)/shard_map/receiver_products/pallas_call | solution.py:315
  67.6 0.0 copy-start.2
  67.7 0.1 collective-permute-start.20
  67.7 1.9 %collective-permute-start.21 = (bf16[2,96,256]{2,1,0:T(8,128)(2,1)S(1)}, bf16[2,96,256]{2,1,0:T(8,128)(2,1)S(1)}, u32[]{:S(2)}, u32[]{:S(2)}) collective-permute-start(bf16[2,96,256]{2,1,0:T(8,128)(2,1)S(1)} %get-tuple-element.35), channel_id=1, source_target_pairs={{0,8},{4,12},{8,0},{12,4},{1,9},{5,13},{9,1},{13,5},{2,10},{6,14},... | collective-permute-start | bytes 294920 | tf_op jit(solution)/shard_map/ppermute | solution.py:412
  69.6 0.0 collective-permute-done.3.refs_3_
  69.6 2.5 %collective-permute-start.22 = (bf16[2,96,256]{2,1,0:T(8,128)(2,1)S(1)}, bf16[2,96,256]{2,1,0:T(8,128)(2,1)S(1)}, u32[]{:S(2)}, u32[]{:S(2)}) collective-permute-start(bf16[2,96,256]{2,1,0:T(8,128)(2,1)S(1)} %get-tuple-element.36), channel_id=1, source_target_pairs={{0,12},{4,8},{8,4},{12,0},{1,13},{5,9},{9,5},{13,1},{2,14},{6,10},... | collective-permute-start | bytes 294920 | tf_op jit(solution)/shard_map/ppermute | solution.py:412
  72.1 0.0 collective-permute-done.5.refs_6_
  72.1 0.0 collective-permute-done.7.refs_8_
  72.1 3.9 %receiver_products.2 = (bf16[2,96,256]{2,1,0:T(8,128)(2,1)S(1)}, bf16[2,96,256]{2,1,0:T(8,128)(2,1)S(1)}, bf16[2,96,256]{2,1,0:T(8,128)(2,1)S(1)}, bf16[2,96,256]{2,1,0:T(8,128)(2,1)S(1)}) custom-call(s32[16]{0:T(128)S(1)} %copy-done.6, s32[16,16]{1,0:T(8,128)S(1)} %copy-done.5, s32[16,1,1024]{2,1,0:T(1,128)S(1)} %bitcast.8, ...), custom_call_target="tpu_custom_call" | custom-call | flops 1610612736 | bytes 3145728 | tf_op jit(solution)/shard_map/receiver_products/pallas_call | solution.py:315
  76.0 0.1 collective-permute-start.8
  76.1 1.9 %collective-permute-start.9 = (bf16[2,96,256]{2,1,0:T(8,128)(2,1)S(1)}, bf16[2,96,256]{2,1,0:T(8,128)(2,1)S(1)}, u32[]{:S(2)}, u32[]{:S(2)}) collective-permute-start(bf16[2,96,256]{2,1,0:T(8,128)(2,1)S(1)} %get-tuple-element.27), channel_id=1, source_target_pairs={{0,8},{4,12},{8,0},{12,4},{1,9},{5,13},{9,1},{13,5},{2,10},{6,14},... | collective-permute-start | bytes 294920 | tf_op jit(solution)/shard_map/ppermute | solution.py:412
  78.0 0.0 collective-permute-done.20.refs_6_
  78.0 2.5 %collective-permute-start.10 = (bf16[2,96,256]{2,1,0:T(8,128)(2,1)S(1)}, bf16[2,96,256]{2,1,0:T(8,128)(2,1)S(1)}, u32[]{:S(2)}, u32[]{:S(2)}) collective-permute-start(bf16[2,96,256]{2,1,0:T(8,128)(2,1)S(1)} %get-tuple-element.28), channel_id=1, source_target_pairs={{0,12},{4,8},{8,4},{12,0},{1,13},{5,9},{9,5},{13,1},{2,14},{6,10},... | collective-permute-start | bytes 294920 | tf_op jit(solution)/shard_map/ppermute | solution.py:412
  80.5 0.0 collective-permute-done.21.refs_7_
  80.5 0.0 collective-permute-done.22.refs_8_
  80.6 0.1 collective-permute-start.23
  80.7 0.1 collective-permute-done.8.refs_1_
  80.8 1.0 %collective-permute-done.9.refs_2_ = bf16[2,96,256]{2,1,0:T(8,128)(2,1)S(1)} collective-permute-done((bf16[2,96,256]{2,1,0:T(8,128)(2,1)S(1)}, bf16[2,96,256]{2,1,0:T(8,128)(2,1)S(1)}, u32[]{:S(2)}, u32[]{:S(2)}) %collective-permute-start.9) | collective-permute-done | bytes 98336 | tf_op jit(solution)/shard_map/ppermute | solution.py:412
  81.8 2.7 %collective-permute-done.10.refs_3_ = bf16[2,96,256]{2,1,0:T(8,128)(2,1)S(1)} collective-permute-done((bf16[2,96,256]{2,1,0:T(8,128)(2,1)S(1)}, bf16[2,96,256]{2,1,0:T(8,128)(2,1)S(1)}, u32[]{:S(2)}, u32[]{:S(2)}) %collective-permute-start.10) | collective-permute-done | bytes 98336 | tf_op jit(solution)/shard_map/ppermute | solution.py:412
  84.5 0.6 collective-permute-start.11
  85.1 1.3 %collective-permute-done.23.refs_9_ = bf16[4,96,256]{2,1,0:T(8,128)(2,1)S(1)} collective-permute-done((bf16[4,96,256]{2,1,0:T(8,128)(2,1)S(1)}, bf16[4,96,256]{2,1,0:T(8,128)(2,1)S(1)}, u32[]{:S(2)}, u32[]{:S(2)}) %collective-permute-start.23) | collective-permute-done | bytes 196640 | tf_op jit(solution)/shard_map/ppermute | solution.py:406
  86.4 3.8 %collective-permute-done.11.refs_4_ = bf16[4,96,256]{2,1,0:T(8,128)(2,1)S(1)} collective-permute-done((bf16[4,96,256]{2,1,0:T(8,128)(2,1)S(1)}, bf16[4,96,256]{2,1,0:T(8,128)(2,1)S(1)}, u32[]{:S(2)}, u32[]{:S(2)}) %collective-permute-start.11) | collective-permute-done | bytes 196640 | tf_op jit(solution)/shard_map/ppermute | solution.py:406
  90.3 0.0 copy-done.2
  90.3 6.6 %update_products.1 = f32[1,2,128,4096]{3,2,1,0:T(8,128)} custom-call(s32[16]{0:T(128)S(1)} %copy-done.6, bf16[2,96,256]{2,1,0:T(8,128)(2,1)S(1)} %get-tuple-element.25.refs_0_, bf16[2,96,256]{2,1,0:T(8,128)(2,1)S(1)} %collective-permute-done.8.refs_1_, bf16[2,96,256]{2,1,0:T(8,128)(2,1)S(1)} %collective-permute-done.9.refs_2_, ...), custom_call_target="tpu_custom_call" | custom-call | flops 1610612736 | bytes 14680064 | tf_op jit(solution)/shard_map/update_products/pallas_call | solution.py:379
  (28 shorter events, 0.2 us)
Async XLA Ops:
  0.0 63.7 %copy-start.3 = (bf16[2,48,512]{2,1,0:T(8,128)(2,1)S(1)}, bf16[2,48,512]{2,1,0:T(8,128)(2,1)}, u32[]{:S(2)}) copy-start(bf16[2,48,512]{2,1,0:T(8,128)(2,1)} %constant.26.clone.table) | copy-start | bytes 294916
  0.0 63.7 %copy-start.4 = (s32[16384]{0:T(1024)S(1)}, s32[16384]{0:T(1024)}, u32[]{:S(2)}) copy-start(s32[16384]{0:T(1024)} %param.12) | copy-start | bytes 196612
  1.2 62.5 %slice-start = ((s8[6291456]{0:T(1024)(128)(4,1)}), s8[4194304]{0:T(1024)(128)(4,1)S(1)}, s32[]{:S(2)}) async-start(s8[6291456]{0:T(1024)(128)(4,1)} %bitcast.5), calls=%async_computation | async-start | bytes 8388608
  1.2 12.9 %collective-permute-start.16 = (bf16[2,96,1024]{2,1,0:T(8,128)(2,1)S(1)}, bf16[2,96,1024]{2,1,0:T(8,128)(2,1)S(1)}, u32[]{:S(2)}, u32[]{:S(2)}) collective-permute-start(bf16[2,96,1024]{2,1,0:T(8,128)(2,1)S(1)} %get-tuple-element.37), channel_id=1, source_target_pairs={{0,2},{2,0},{1,3},{3,1},{4,6},{6,4},{5,7},{7,5},{8,10},{10,8},{9,1... | collective-permute-start | bytes 1179656 | tf_op jit(solution)/shard_map/ppermute | solution.py:406
  4.2 59.5 %slice-start.1 = ((s8[6291456]{0:T(1024)(128)(4,1)}), s8[2097152]{0:T(1024)(128)(4,1)S(1)}, s32[]{:S(2)}) async-start(s8[6291456]{0:T(1024)(128)(4,1)} %bitcast.5), calls=%async_computation.1 | async-start | bytes 4194304
  4.2 17.5 %collective-permute-start.4 = (bf16[2,96,1024]{2,1,0:T(8,128)(2,1)S(1)}, bf16[2,96,1024]{2,1,0:T(8,128)(2,1)S(1)}, u32[]{:S(2)}, u32[]{:S(2)}) collective-permute-start(bf16[2,96,1024]{2,1,0:T(8,128)(2,1)S(1)} %get-tuple-element.38), channel_id=1, source_target_pairs={{0,2},{2,0},{1,3},{3,1},{4,6},{6,4},{5,7},{7,5},{8,10},{10,8},{9,1... | collective-permute-start | bytes 1179656 | tf_op jit(solution)/shard_map/ppermute | solution.py:406
  14.2 29.7 %collective-permute-start.18 = (bf16[2,96,1024]{2,1,0:T(8,128)(2,1)S(1)}, bf16[2,96,1024]{2,1,0:T(8,128)(2,1)S(1)}, u32[]{:S(2)}, u32[]{:S(2)}) collective-permute-start(bf16[2,96,1024]{2,1,0:T(8,128)(2,1)S(1)} %collective-permute-done.16.refs_5_), channel_id=1, source_target_pairs={{0,16},{16,0},{1,17},{17,1},{2,18},{18,2},{3,19},{19,3},{4,20},{20... | collective-permute-start | bytes 1179656 | tf_op jit(solution)/shard_map/ppermute | solution.py:406
  21.8 35.0 %collective-permute-start.6 = (bf16[2,96,1024]{2,1,0:T(8,128)(2,1)S(1)}, bf16[2,96,1024]{2,1,0:T(8,128)(2,1)S(1)}, u32[]{:S(2)}, u32[]{:S(2)}) collective-permute-start(bf16[2,96,1024]{2,1,0:T(8,128)(2,1)S(1)} %collective-permute-done.4.refs_5_), channel_id=1, source_target_pairs={{0,16},{16,0},{1,17},{17,1},{2,18},{18,2},{3,19},{19,3},{4,20},{20... | collective-permute-start | bytes 1179656 | tf_op jit(solution)/shard_map/ppermute | solution.py:406
  23.5 2.8 %copy-start = (bf16[1,2,384,4096]{3,2,1,0:T(8,128)(2,1)S(1)}, bf16[1,2,384,4096]{3,2,1,0:T(8,128)(2,1)}, u32[]{:S(2)}) copy-start(bf16[1,2,384,4096]{3,2,1,0:T(8,128)(2,1)} %refs_11_.1) | copy-start | bytes 18874372
  26.3 2.2 %copy-start.1 = (f32[1,2,128,4096]{3,2,1,0:T(8,128)S(1)}, f32[1,2,128,4096]{3,2,1,0:T(8,128)}, u32[]{:S(2)}) copy-start(f32[1,2,128,4096]{3,2,1,0:T(8,128)} %refs_10_.1) | copy-start | bytes 12582916
  28.5 0.7 copy-start.5
  29.2 0.7 copy-start.6
  33.8 6.3 %collective-permute-start.12 = (bf16[2,96,256]{2,1,0:T(8,128)(2,1)S(1)}, bf16[2,96,256]{2,1,0:T(8,128)(2,1)S(1)}, u32[]{:S(2)}, u32[]{:S(2)}) collective-permute-start(bf16[2,96,256]{2,1,0:T(8,128)(2,1)S(1)} %get-tuple-element.30), channel_id=1, source_target_pairs={{0,4},{4,0},{8,12},{12,8},{1,5},{5,1},{9,13},{13,9},{2,6},{6,2},{1... | collective-permute-start | bytes 294920 | tf_op jit(solution)/shard_map/ppermute | solution.py:412
  35.5 8.4 %collective-permute-start.13 = (bf16[2,96,256]{2,1,0:T(8,128)(2,1)S(1)}, bf16[2,96,256]{2,1,0:T(8,128)(2,1)S(1)}, u32[]{:S(2)}, u32[]{:S(2)}) collective-permute-start(bf16[2,96,256]{2,1,0:T(8,128)(2,1)S(1)} %get-tuple-element.31), channel_id=1, source_target_pairs={{0,8},{4,12},{8,0},{12,4},{1,9},{5,13},{9,1},{13,5},{2,10},{6,14},... | collective-permute-start | bytes 294920 | tf_op jit(solution)/shard_map/ppermute | solution.py:412
  38.1 6.9 %collective-permute-start.14 = (bf16[2,96,256]{2,1,0:T(8,128)(2,1)S(1)}, bf16[2,96,256]{2,1,0:T(8,128)(2,1)S(1)}, u32[]{:S(2)}, u32[]{:S(2)}) collective-permute-start(bf16[2,96,256]{2,1,0:T(8,128)(2,1)S(1)} %get-tuple-element.32), channel_id=1, source_target_pairs={{0,12},{4,8},{8,4},{12,0},{1,13},{5,9},{9,5},{13,1},{2,14},{6,10},... | collective-permute-start | bytes 294920 | tf_op jit(solution)/shard_map/ppermute | solution.py:412
  40.1 7.3 %collective-permute-start = (bf16[2,96,256]{2,1,0:T(8,128)(2,1)S(1)}, bf16[2,96,256]{2,1,0:T(8,128)(2,1)S(1)}, u32[]{:S(2)}, u32[]{:S(2)}) collective-permute-start(bf16[2,96,256]{2,1,0:T(8,128)(2,1)S(1)} %get-tuple-element.22), channel_id=1, source_target_pairs={{0,4},{4,0},{8,12},{12,8},{1,5},{5,1},{9,13},{13,9},{2,6},{6,2},{1... | collective-permute-start | bytes 294920 | tf_op jit(solution)/shard_map/ppermute | solution.py:412
  43.9 19.8 %collective-permute-start.17 = (bf16[2,96,1024]{2,1,0:T(8,128)(2,1)S(1)}, bf16[2,96,1024]{2,1,0:T(8,128)(2,1)S(1)}, u32[]{:S(2)}, u32[]{:S(2)}) collective-permute-start(bf16[2,96,1024]{2,1,0:T(8,128)(2,1)S(1)} %collective-permute-done.16.refs_5_), channel_id=1, source_target_pairs={{0,1},{1,0},{2,3},{3,2},{4,5},{5,4},{6,7},{7,6},{8,9},{9,8},{10,11... | collective-permute-start | bytes 1179656 | tf_op jit(solution)/shard_map/ppermute | solution.py:406
  43.9 19.8 %collective-permute-start.19 = (bf16[2,96,1024]{2,1,0:T(8,128)(2,1)S(1)}, bf16[2,96,1024]{2,1,0:T(8,128)(2,1)S(1)}, u32[]{:S(2)}, u32[]{:S(2)}) collective-permute-start(bf16[2,96,1024]{2,1,0:T(8,128)(2,1)S(1)} %collective-permute-done.18.refs_7_), channel_id=1, source_target_pairs={{0,1},{1,0},{2,3},{3,2},{4,5},{5,4},{6,7},{7,6},{8,9},{9,8},{10,11... | collective-permute-start | bytes 1179656 | tf_op jit(solution)/shard_map/ppermute | solution.py:406
  45.0 10.3 %collective-permute-start.1 = (bf16[2,96,256]{2,1,0:T(8,128)(2,1)S(1)}, bf16[2,96,256]{2,1,0:T(8,128)(2,1)S(1)}, u32[]{:S(2)}, u32[]{:S(2)}) collective-permute-start(bf16[2,96,256]{2,1,0:T(8,128)(2,1)S(1)} %get-tuple-element.23), channel_id=1, source_target_pairs={{0,8},{4,12},{8,0},{12,4},{1,9},{5,13},{9,1},{13,5},{2,10},{6,14},... | collective-permute-start | bytes 294920 | tf_op jit(solution)/shard_map/ppermute | solution.py:412
  47.4 9.3 %collective-permute-start.2 = (bf16[2,96,256]{2,1,0:T(8,128)(2,1)S(1)}, bf16[2,96,256]{2,1,0:T(8,128)(2,1)S(1)}, u32[]{:S(2)}, u32[]{:S(2)}) collective-permute-start(bf16[2,96,256]{2,1,0:T(8,128)(2,1)S(1)} %get-tuple-element.24), channel_id=1, source_target_pairs={{0,12},{4,8},{8,4},{12,0},{1,13},{5,9},{9,5},{13,1},{2,14},{6,10},... | collective-permute-start | bytes 294920 | tf_op jit(solution)/shard_map/ppermute | solution.py:412
  55.2 6.5 %collective-permute-start.15 = (bf16[4,96,256]{2,1,0:T(8,128)(2,1)S(1)}, bf16[4,96,256]{2,1,0:T(8,128)(2,1)S(1)}, u32[]{:S(2)}, u32[]{:S(2)}) collective-permute-start(bf16[4,96,256]{2,1,0:T(8,128)(2,1)S(1)} %pad_maximum_fusion.2), channel_id=1, source_target_pairs={{0,2},{2,0},{1,3},{3,1},{4,6},{6,4},{5,7},{7,5},{8,10},{10,8},{9,1... | collective-permute-start | bytes 589832 | tf_op jit(solution)/shard_map/ppermute | solution.py:406
  56.7 15.4 %collective-permute-start.5 = (bf16[2,96,1024]{2,1,0:T(8,128)(2,1)S(1)}, bf16[2,96,1024]{2,1,0:T(8,128)(2,1)S(1)}, u32[]{:S(2)}, u32[]{:S(2)}) collective-permute-start(bf16[2,96,1024]{2,1,0:T(8,128)(2,1)S(1)} %collective-permute-done.4.refs_5_), channel_id=1, source_target_pairs={{0,1},{1,0},{2,3},{3,2},{4,5},{5,4},{6,7},{7,6},{8,9},{9,8},{10,11... | collective-permute-start | bytes 1179656 | tf_op jit(solution)/shard_map/ppermute | solution.py:406
  56.7 15.4 %collective-permute-start.7 = (bf16[2,96,1024]{2,1,0:T(8,128)(2,1)S(1)}, bf16[2,96,1024]{2,1,0:T(8,128)(2,1)S(1)}, u32[]{:S(2)}, u32[]{:S(2)}) collective-permute-start(bf16[2,96,1024]{2,1,0:T(8,128)(2,1)S(1)} %collective-permute-done.6.refs_7_), channel_id=1, source_target_pairs={{0,1},{1,0},{2,3},{3,2},{4,5},{5,4},{6,7},{7,6},{8,9},{9,8},{10,11... | collective-permute-start | bytes 1179656 | tf_op jit(solution)/shard_map/ppermute | solution.py:406
  61.7 7.9 %collective-permute-start.3 = (bf16[4,96,256]{2,1,0:T(8,128)(2,1)S(1)}, bf16[4,96,256]{2,1,0:T(8,128)(2,1)S(1)}, u32[]{:S(2)}, u32[]{:S(2)}) collective-permute-start(bf16[4,96,256]{2,1,0:T(8,128)(2,1)S(1)} %pad_maximum_fusion), channel_id=1, source_target_pairs={{0,2},{2,0},{1,3},{3,1},{4,6},{6,4},{5,7},{7,5},{8,10},{10,8},{9,1... | collective-permute-start | bytes 589832 | tf_op jit(solution)/shard_map/ppermute | solution.py:406
  67.6 22.6 %copy-start.2 = (f32[1,2,128,4096]{3,2,1,0:T(8,128)S(1)}, f32[1,2,128,4096]{3,2,1,0:T(8,128)}, u32[]{:S(2)}) copy-start(f32[1,2,128,4096]{3,2,1,0:T(8,128)} %refs_10_.1) | copy-start | bytes 12582916
  67.7 10.4 %collective-permute-start.20 = (bf16[2,96,256]{2,1,0:T(8,128)(2,1)S(1)}, bf16[2,96,256]{2,1,0:T(8,128)(2,1)S(1)}, u32[]{:S(2)}, u32[]{:S(2)}) collective-permute-start(bf16[2,96,256]{2,1,0:T(8,128)(2,1)S(1)} %get-tuple-element.34), channel_id=1, source_target_pairs={{0,4},{4,0},{8,12},{12,8},{1,5},{5,1},{9,13},{13,9},{2,6},{6,2},{1... | collective-permute-start | bytes 294920 | tf_op jit(solution)/shard_map/ppermute | solution.py:412
  67.7 12.7 %collective-permute-start.21 = (bf16[2,96,256]{2,1,0:T(8,128)(2,1)S(1)}, bf16[2,96,256]{2,1,0:T(8,128)(2,1)S(1)}, u32[]{:S(2)}, u32[]{:S(2)}) collective-permute-start(bf16[2,96,256]{2,1,0:T(8,128)(2,1)S(1)} %get-tuple-element.35), channel_id=1, source_target_pairs={{0,8},{4,12},{8,0},{12,4},{1,9},{5,13},{9,1},{13,5},{2,10},{6,14},... | collective-permute-start | bytes 294920 | tf_op jit(solution)/shard_map/ppermute | solution.py:412
  69.6 10.9 %collective-permute-start.22 = (bf16[2,96,256]{2,1,0:T(8,128)(2,1)S(1)}, bf16[2,96,256]{2,1,0:T(8,128)(2,1)S(1)}, u32[]{:S(2)}, u32[]{:S(2)}) collective-permute-start(bf16[2,96,256]{2,1,0:T(8,128)(2,1)S(1)} %get-tuple-element.36), channel_id=1, source_target_pairs={{0,12},{4,8},{8,4},{12,0},{1,13},{5,9},{9,5},{13,1},{2,14},{6,10},... | collective-permute-start | bytes 294920 | tf_op jit(solution)/shard_map/ppermute | solution.py:412
  76.0 4.8 %collective-permute-start.8 = (bf16[2,96,256]{2,1,0:T(8,128)(2,1)S(1)}, bf16[2,96,256]{2,1,0:T(8,128)(2,1)S(1)}, u32[]{:S(2)}, u32[]{:S(2)}) collective-permute-start(bf16[2,96,256]{2,1,0:T(8,128)(2,1)S(1)} %get-tuple-element.26), channel_id=1, source_target_pairs={{0,4},{4,0},{8,12},{12,8},{1,5},{5,1},{9,13},{13,9},{2,6},{6,2},{1... | collective-permute-start | bytes 294920 | tf_op jit(solution)/shard_map/ppermute | solution.py:412
  76.1 5.7 %collective-permute-start.9 = (bf16[2,96,256]{2,1,0:T(8,128)(2,1)S(1)}, bf16[2,96,256]{2,1,0:T(8,128)(2,1)S(1)}, u32[]{:S(2)}, u32[]{:S(2)}) collective-permute-start(bf16[2,96,256]{2,1,0:T(8,128)(2,1)S(1)} %get-tuple-element.27), channel_id=1, source_target_pairs={{0,8},{4,12},{8,0},{12,4},{1,9},{5,13},{9,1},{13,5},{2,10},{6,14},... | collective-permute-start | bytes 294920 | tf_op jit(solution)/shard_map/ppermute | solution.py:412
  78.0 6.5 %collective-permute-start.10 = (bf16[2,96,256]{2,1,0:T(8,128)(2,1)S(1)}, bf16[2,96,256]{2,1,0:T(8,128)(2,1)S(1)}, u32[]{:S(2)}, u32[]{:S(2)}) collective-permute-start(bf16[2,96,256]{2,1,0:T(8,128)(2,1)S(1)} %get-tuple-element.28), channel_id=1, source_target_pairs={{0,12},{4,8},{8,4},{12,0},{1,13},{5,9},{9,5},{13,1},{2,14},{6,10},... | collective-permute-start | bytes 294920 | tf_op jit(solution)/shard_map/ppermute | solution.py:412
  80.6 5.9 %collective-permute-start.23 = (bf16[4,96,256]{2,1,0:T(8,128)(2,1)S(1)}, bf16[4,96,256]{2,1,0:T(8,128)(2,1)S(1)}, u32[]{:S(2)}, u32[]{:S(2)}) collective-permute-start(bf16[4,96,256]{2,1,0:T(8,128)(2,1)S(1)} %pad_maximum_fusion.3), channel_id=1, source_target_pairs={{0,2},{2,0},{1,3},{3,1},{4,6},{6,4},{5,7},{7,5},{8,10},{10,8},{9,1... | collective-permute-start | bytes 589832 | tf_op jit(solution)/shard_map/ppermute | solution.py:406
  84.5 5.7 %collective-permute-start.11 = (bf16[4,96,256]{2,1,0:T(8,128)(2,1)S(1)}, bf16[4,96,256]{2,1,0:T(8,128)(2,1)S(1)}, u32[]{:S(2)}, u32[]{:S(2)}) collective-permute-start(bf16[4,96,256]{2,1,0:T(8,128)(2,1)S(1)} %pad_maximum_fusion.1), channel_id=1, source_target_pairs={{0,2},{2,0},{1,3},{3,1},{4,6},{6,4},{5,7},{7,5},{8,10},{10,8},{9,1... | collective-permute-start | bytes 589832 | tf_op jit(solution)/shard_map/ppermute | solution.py:406

commit v2 on v1

--- a/solution.py
+++ b/solution.py
@@ -175,64 +175,81 @@
         held[owner] = slot + 1
 
 
-def forward_kernel(count_col, half, owners, ranks, focus, factors, *refs):
-    outs = refs[: half * count_col]
-    sums, tile_of, held = refs[half * count_col :]
-    block = pl.program_id(0)
-    blocks = pl.num_programs(0)
+def forward_kernel(count_col, half, owners_far, ranks_far, focus, factors, *refs):
+    outs = refs[: 2 * count_col]
+    focus_here, factors_here, sums, owners, ranks, tile_of, held, sems = refs[2 * count_col :]
     column = lax.axis_index("col")
     mine = lax.axis_index("freq")
-    two, vis, width = focus.shape[1:]
-    low = focus[0].astype(jnp.bfloat16).reshape(two * vis, width)
-    by_real = dot(factors[0, 0], low, 1, 1)
-    by_imag = dot(factors[0, 1], low, 1, 1)
-    sums[block] = jnp.concatenate(
-        [by_real[:, :vis] - by_imag[:, vis:], by_real[:, vis:] + by_imag[:, :vis]], axis=1
-    )
-
-    @pl.when(block == blocks - 1)
-    def _():
-        capacity = 2 * half
-        list_tiles(owners, tile_of, held, count_col, capacity)
-        row_id = lax.broadcasted_iota(jnp.int32, (R, 2 * vis), 0)
-        for s in range(half):
-            for d in range(count_col):
-                for e in range(2):
-                    tile = tile_of[(column ^ d) * capacity + (mine ^ e) * half + s]
-                    pieces = []
-                    for j in range(sums.shape[0]):
-                        rank = ranks[tile, column * sums.shape[0] + j]
-                        piece = sums[j, pl.ds(pl.multiple_of(tile * R, 8), R), :]
-                        pieces.append(jnp.where(row_id < rank, piece, 0.0))
-                    outs[s * count_col + d][e] = jnp.concatenate(pieces, axis=0).astype(jnp.bfloat16)
+    two, vis, sources = focus_here.shape
+    blocks = sources // TS
+    copies = []
+    for j in range(blocks):
+        at = pl.ds(j * TS, TS)
+        copies.append(
+            [
+                pltpu.make_async_copy(focus.at[0, :, :, at], focus_here.at[:, :, at], sems.at[0, j]),
+                pltpu.make_async_copy(factors.at[0, :, :, at], factors_here.at[:, :, at], sems.at[1, j]),
+            ]
+        )
+        for copy in copies[j]:
+            copy.start()
+    small = [
+        pltpu.make_async_copy(owners_far, owners, sems.at[2, 0]),
+        pltpu.make_async_copy(ranks_far, ranks, sems.at[2, 1]),
+    ]
+    for copy in small:
+        copy.start()
+    for copy in small:
+        copy.wait()
+    capacity = 2 * half
+    list_tiles(owners, tile_of, held, count_col, capacity)
+    for j in range(blocks):
+        for copy in copies[j]:
+            copy.wait()
+        at = pl.ds(j * TS, TS)
+        low = focus_here[:, :, at].astype(jnp.bfloat16).reshape(two * vis, TS)
+        by_real = dot(factors_here[0, :, at], low, 1, 1)
+        by_imag = dot(factors_here[1, :, at], low, 1, 1)
+        sums[j, :, :vis] = by_real[:, :vis] - by_imag[:, vis:]
+        sums[j, :, vis:] = by_real[:, vis:] + by_imag[:, :vis]
+    row_id = lax.broadcasted_iota(jnp.int32, (R, 2 * vis), 0)
+    for d in range(count_col):
+        for e in range(2):
+            for s in range(half):
+                tile = tile_of[(column ^ d) * capacity + (mine ^ e) * half + s]
+                pieces = []
+                for j in range(blocks):
+                    rank = ranks[tile, column * blocks + j]
+                    piece = sums[j, pl.ds(pl.multiple_of(tile * R, 8), R), :]
+                    pieces.append(jnp.where(row_id < rank, piece, 0.0))
+                outs[2 * d + e][s] = jnp.concatenate(pieces, axis=0).astype(jnp.bfloat16)
 
 
 def forward_products(count_col, half, focusing, v_factors, tile_ranks, owners):
     vis, sources = focusing.shape[2:]
     rows = v_factors.shape[2]
     blocks = sources // TS
-    out = jax.ShapeDtypeStruct((2, blocks * R, 2 * vis), jnp.bfloat16)
-    whole = pl.BlockSpec((2, blocks * R, 2 * vis), lambda j: (0, 0, 0))
-    smem = pl.BlockSpec(memory_space=pltpu.SMEM)
+    out = jax.ShapeDtypeStruct((half, blocks * R, 2 * vis), jnp.bfloat16)
+    vmem = pl.BlockSpec(memory_space=pltpu.VMEM)
+    anywhere = pl.BlockSpec(memory_space=pl.ANY)
     return pl.pallas_call(
         functools.partial(forward_kernel, count_col, half),
-        grid=(blocks,),
-        in_specs=[
-            smem,
-            smem,
-            pl.BlockSpec((1, 2, vis, TS), lambda j: (0, 0, 0, j)),
-            pl.BlockSpec((1, 2, rows, TS), lambda j: (0, 0, 0, j)),
+        in_specs=[anywhere] * 4,
+        out_specs=[vmem] * (2 * count_col + 2),
+        out_shape=[out] * (2 * count_col)
+        + [
+            jax.ShapeDtypeStruct(focusing.shape[1:], jnp.float32),
+            jax.ShapeDtypeStruct(v_factors.shape[1:], jnp.bfloat16),
         ],
-        out_specs=[whole] * (half * count_col),
-        out_shape=[out] * (half * count_col),
         scratch_shapes=[
             pltpu.VMEM((blocks, rows, 2 * vis), jnp.float32),
+            pltpu.SMEM(owners.shape, jnp.int32),
+            pltpu.SMEM(tile_ranks.shape, jnp.int32),
             pltpu.SMEM((count_col * 2 * half,), jnp.int32),
             pltpu.SMEM((count_col,), jnp.int32),
+            pltpu.SemaphoreType.DMA((3, blocks)),
         ],
-        compiler_params=pltpu.CompilerParams(
-            dimension_semantics=("arbitrary",), vmem_limit_bytes=40 * 2**20
-        ),
+        compiler_params=pltpu.CompilerParams(vmem_limit_bytes=46 * 2**20),
         cost_estimate=pl.CostEstimate(
             flops=8 * rows * vis * sources, bytes_accessed=8 * vis * sources + 4 * rows * sources, transcendentals=0
         ),
@@ -240,34 +257,55 @@
     )(owners, tile_ranks, focusing, v_factors)
 
 
-def receiver_kernel(count_col, half, chunk, owners, ranks, onsets, table, kept, *refs):
-    others = refs[: count_col - 1]
-    crossed, u_own, quarter_0, quarter_1, quarter_2, quarter_3 = refs[count_col - 1 : count_col + 5]
-    outs = refs[count_col + 5 : 2 * count_col + 5]
-    factors, coefs, field, windowed, tile_of, held, sems = refs[2 * count_col + 5 :]
+def load_kernel(half, u_factors, u_here, sem):
+    start = lax.axis_index("freq") * half
+    copy = pltpu.make_async_copy(u_factors.at[0, :, pl.ds(start, half)], u_here, sem)
+    copy.start()
+    copy.wait()
+
+
+def load_factors(half, u_factors):
+    shape = (2, half) + u_factors.shape[3:]
+    return pl.pallas_call(
+        functools.partial(load_kernel, half),
+        in_specs=[pl.BlockSpec(memory_space=pl.ANY)],
+        out_specs=pl.BlockSpec(memory_space=pltpu.VMEM),
+        out_shape=jax.ShapeDtypeStruct(shape, jnp.bfloat16),
+        scratch_shapes=[pltpu.SemaphoreType.DMA],
+        compiler_params=pltpu.CompilerParams(vmem_limit_bytes=46 * 2**20),
+        cost_estimate=pl.CostEstimate(flops=0, bytes_accessed=2 * int(np.prod(shape)), transcendentals=0),
+        name="load_factors",
+    )(u_factors)
+
+
+def receiver_kernel(count_col, half, chunk, owners, ranks, onsets, table, *refs):
+    arrived = refs[: 2 * count_col]
+    u_own = refs[2 * count_col]
+    u_other = refs[2 * count_col + 1 : 2 * count_col + 5]
+    outs = refs[-2 * count_col - 7 : -7]
+    earlier = refs[2 * count_col + 5 : -2 * count_col - 7]
+    factors, coefs, field, windowed, tile_of, held, sems = refs[-7:]
     column = lax.axis_index("col")
     mine = lax.axis_index("freq")
+    vis = field.shape[1]
+    rows = factors.shape[1]
     place = lax.axis_index("grp") * 2 + lax.axis_index("rep")
-    vis = field.shape[1]
-    rows = factors.shape[2]
-    quarter = rows // 4
-    copies = [
-        pltpu.make_async_copy(u_own.at[0, :, mine * half + chunk], factors.at[0], sems.at[0])
-    ]
-    for n, ref in enumerate((quarter_0, quarter_1, quarter_2, quarter_3)):
+    quarter = u_other[0].shape[1]
+    copies = []
+    for n, ref in enumerate(u_other):
         start = pl.multiple_of((place ^ n) * quarter, quarter)
         copies.append(
-            pltpu.make_async_copy(ref, factors.at[1, :, pl.ds(start, quarter), :], sems.at[n + 1])
+            pltpu.make_async_copy(ref, factors.at[:, pl.ds(start, quarter), :], sems.at[n])
         )
     for copy in copies:
         copy.start()
     list_tiles(owners, tile_of, held, count_col, 2 * half)
     tile = tile_of[column * 2 * half + mine * half + chunk]
-    strip = crossed.shape[1]
+    strip = arrived[0].shape[1]
     for d in range(count_col):
         start = pl.multiple_of((column ^ d) * strip, strip)
-        arrived = (kept if d == 0 else others[d - 1])[0]
-        for e, values in enumerate((arrived, crossed[d])):
+        for e in range(2):
+            values = arrived[2 * d + e][chunk]
             coefs[e, 0, pl.ds(start, strip), :] = values
             coefs[e, 1, pl.ds(start, strip), :] = jnp.concatenate([-values[:, vis:], values[:, :vis]], axis=1)
     times = lax.broadcasted_iota(jnp.int32, (NT, TS), 0)
@@ -276,9 +314,10 @@
     count = tables.shape[0] // 3
     mixing = tables[:count] + tables[count : 2 * count] + tables[2 * count :]
     for e in range(2):
-        for copy in copies[:1] if e == 0 else copies[1:]:
+        for copy in copies if e == 1 else []:
             copy.wait()
-        product = dot(coefs[e].reshape(2 * rows, 2 * vis), factors[e].reshape(2 * rows, TS), 0, 0)
+        matrix = (u_own[:, chunk] if e == 0 else factors[...]).reshape(2 * rows, TS)
+        product = dot(coefs[e].reshape(2 * rows, 2 * vis), matrix, 0, 0)
         low = product.astype(jnp.bfloat16).astype(jnp.float32)
         field[2 * e] = low[:vis]
         field[2 * e + 1] = low[vis:]
@@ -288,9 +327,9 @@
             total = total + mixing[4 * p + q : 4 * p + q + 1] * field[q]
         windowed[p // 2, (p % 2) * vis : (p % 2 + 1) * vis, :] = total.astype(jnp.bfloat16)
     row_id = lax.broadcasted_iota(jnp.int32, (R, 2 * vis), 0)
-    per_column = strip // R
     for e in range(2):
-        back = dot(factors[e].reshape(2 * rows, TS), windowed[e], 1, 1)
+        matrix = (u_own[:, chunk] if e == 0 else factors[...]).reshape(2 * rows, TS)
+        back = dot(matrix, windowed[e], 1, 1)
         by_real, by_imag = back[:rows], back[rows:]
         adjoint = jnp.concatenate(
             [by_real[:, :vis] + by_imag[:, vis:], by_real[:, vis:] - by_imag[:, :vis]], axis=1
@@ -301,115 +340,123 @@
         coefs[e, 0] = jnp.concatenate(pieces, axis=0).astype(jnp.bfloat16)
         for d in range(count_col):
             start = pl.multiple_of((column ^ d) * strip, strip)
-            outs[d][e] = coefs[e, 0, pl.ds(start, strip), :]
-
-
-def receiver_products(count_col, half, chunk, owners, tile_ranks, onsets, table, arrived, crossed, u_factors, quarters):
-    strip, columns = crossed.shape[1:]
-    rows = u_factors.shape[3]
+            outs[2 * d + e][chunk] = coefs[e, 0, pl.ds(start, strip), :]
+            for s in range(chunk):
+                outs[2 * d + e][s] = earlier[2 * d + e][s]
+
+
+def receiver_products(count_col, half, chunk, owners, tile_ranks, onsets, table, arrived, u_factors, u_other, earlier):
+    strip, columns = arrived[0].shape[1:]
+    rows = u_factors.shape[2]
     vis = columns // 2
     smem = pl.BlockSpec(memory_space=pltpu.SMEM)
     vmem = pl.BlockSpec(memory_space=pltpu.VMEM)
-    anywhere = pl.BlockSpec(memory_space=pl.ANY)
-    out = jax.ShapeDtypeStruct((2, strip, columns), jnp.bfloat16)
+    out = jax.ShapeDtypeStruct((chunk + 1, strip, columns), jnp.bfloat16)
     return pl.pallas_call(
         functools.partial(receiver_kernel, count_col, half, chunk),
-        in_specs=[smem, smem, vmem, vmem] + [vmem] * (count_col + 1) + [anywhere] * 5,
-        out_specs=[vmem] * count_col,
-        out_shape=[out] * count_col,
+        in_specs=[smem, smem, vmem, vmem]
+        + [vmem] * (2 * count_col)
+        + [vmem] * 5
+        + [vmem] * len(earlier),
+        out_specs=[vmem] * (2 * count_col),
+        out_shape=[out] * (2 * count_col),
         scratch_shapes=[
-            pltpu.VMEM((2, 2, rows, TS), jnp.bfloat16),
+            pltpu.VMEM((2, rows, TS), jnp.bfloat16),
             pltpu.VMEM((2, 2, rows, columns), jnp.bfloat16),
             pltpu.VMEM((4, vis, TS), jnp.float32),
             pltpu.VMEM((2, columns, TS), jnp.bfloat16),
             pltpu.SMEM((count_col * 2 * half,), jnp.int32),
             pltpu.SMEM((count_col,), jnp.int32),
-            pltpu.SemaphoreType.DMA((5,)),
+            pltpu.SemaphoreType.DMA((4,)),
         ],
-        compiler_params=pltpu.CompilerParams(vmem_limit_bytes=40 * 2**20),
+        compiler_params=pltpu.CompilerParams(vmem_limit_bytes=24 * 2**20),
         cost_estimate=pl.CostEstimate(
             flops=32 * rows * vis * TS, bytes_accessed=8 * rows * TS, transcendentals=0
         ),
         name="receiver_products",
-    )(owners, tile_ranks, onsets, table, *arrived, crossed, u_factors, *quarters)
+    )(owners, tile_ranks, onsets, table, *arrived, u_factors, *u_other, *earlier)
 
 
 def update_kernel(count_col, half, owners, *refs):
-    per = count_col + 1
-    arrivals = [refs[s * per : (s + 1) * per] for s in range(half)]
-    focus, factors, out, gathered, adjoint, tile_of, held = refs[half * per :]
-    step = pl.program_id(0)
+    arrivals = refs[: 2 * count_col]
+    focus, factors, out, out_here, gathered, adjoint, tile_of, held, sems = refs[2 * count_col :]
     column = lax.axis_index("col")
     mine = lax.axis_index("freq")
-    two, vis, width = focus.shape[1:]
-    rows = factors.shape[2]
-
-    @pl.when(step == 0)
-    def _():
-        capacity = 2 * half
-        list_tiles(owners, tile_of, held, count_col, capacity)
-        for s in range(half):
-            crossed = arrivals[s][count_col]
-            for d in range(count_col):
-                for e in range(2):
-                    tile = tile_of[(column ^ d) * capacity + (mine ^ e) * half + s]
-                    values = (arrivals[s][d][0] if e == 0 else crossed[d]).astype(jnp.float32)
-                    for j in range(gathered.shape[0]):
-                        gathered[j, pl.ds(pl.multiple_of(tile * R, 8), R), :] = values[j * R : (j + 1) * R]
-        for j in range(gathered.shape[0]):
-            values = gathered[j]
-            adjoint[j, :rows] = values.astype(jnp.bfloat16)
-            adjoint[j, rows:] = jnp.concatenate([values[:, vis:], -values[:, :vis]], axis=1).astype(jnp.bfloat16)
-
-    block = step * width // TS
-    wave = dot(adjoint[block], factors[0].reshape(2 * rows, width), 0, 0)
-    out[0] = focus[0] - wave.reshape(two, vis, width)
-
-
-def update_products(count_col, half, owners, arrivals, focusing, v_factors):
-    vis, sources = focusing.shape[2:]
-    rows = v_factors.shape[2]
+    two, vis, sources = out_here.shape
+    rows = factors.shape[1]
     blocks = sources // TS
     width = 512
+    capacity = 2 * half
+    list_tiles(owners, tile_of, held, count_col, capacity)
+    for s in range(half):
+        for d in range(count_col):
+            for e in range(2):
+                tile = tile_of[(column ^ d) * capacity + (mine ^ e) * half + s]
+                values = arrivals[2 * d + e][s].astype(jnp.float32)
+                for j in range(blocks):
+                    gathered[j, pl.ds(pl.multiple_of(tile * R, 8), R), :] = values[j * R : (j + 1) * R]
+    row_id = lax.broadcasted_iota(jnp.int32, (2 * vis, 2 * vis), 0)
+    column_id = lax.broadcasted_iota(jnp.int32, (2 * vis, 2 * vis), 1)
+    identity = jnp.where(row_id == column_id, 1.0, 0.0).astype(jnp.bfloat16)
+    for j in range(blocks):
+        values = gathered[j]
+        adjoint[j, :rows] = values.astype(jnp.bfloat16)
+        adjoint[j, rows:] = jnp.concatenate([values[:, vis:], -values[:, :vis]], axis=1).astype(jnp.bfloat16)
+
+    writes = []
+    for n in range(sources // width):
+        j = n * width // TS
+        at = pl.ds(n * width, width)
+        right = factors[:, :, at].reshape(2 * rows, width)
+        wave = dot(adjoint[j], right, 0, 0)
+        out_here[:, :, at] = focus[:, :, at] - wave.reshape(two, vis, width)
+        writes.append(pltpu.make_async_copy(out_here.at[:, :, at], out.at[0, :, :, at], sems.at[n]))
+        writes[n].start()
+    for write in writes:
+        write.wait()
+
+
+def update_products(count_col, half, owners, arrivals, focusing, v_factors):
+    vis, sources = focusing.shape[1:]
+    rows = v_factors.shape[1]
+    blocks = sources // TS
     smem = pl.BlockSpec(memory_space=pltpu.SMEM)
-    specs = [smem]
-    for group in arrivals:
-        for array in group:
-            specs.append(pl.BlockSpec(array.shape, lambda j: (0, 0, 0)))
+    vmem = pl.BlockSpec(memory_space=pltpu.VMEM)
+    anywhere = pl.BlockSpec(memory_space=pl.ANY)
     return pl.pallas_call(
         functools.partial(update_kernel, count_col, half),
-        grid=(sources // width,),
-        in_specs=specs
-        + [
-            pl.BlockSpec((1, 2, vis, width), lambda j: (0, 0, 0, j)),
-            pl.BlockSpec((1, 2, rows, width), lambda j: (0, 0, 0, j)),
-        ],
-        out_specs=pl.BlockSpec((1, 2, vis, width), lambda j: (0, 0, 0, j)),
-        out_shape=jax.ShapeDtypeStruct(focusing.shape, jnp.float32),
+        in_specs=[smem] + [vmem] * (len(arrivals) + 2),
+        out_specs=anywhere,
+        out_shape=jax.ShapeDtypeStruct((1,) + focusing.shape, jnp.float32),
         scratch_shapes=[
+            pltpu.VMEM(focusing.shape, jnp.float32),
             pltpu.VMEM((blocks, rows, 2 * vis), jnp.float32),
             pltpu.VMEM((blocks, 2 * rows, 2 * vis), jnp.bfloat16),
             pltpu.SMEM((count_col * 2 * half,), jnp.int32),
             pltpu.SMEM((count_col,), jnp.int32),
+            pltpu.SemaphoreType.DMA((sources // 512,)),
         ],
-        compiler_params=pltpu.CompilerParams(
-            dimension_semantics=("arbitrary",), vmem_limit_bytes=40 * 2**20
-        ),
+        compiler_params=pltpu.CompilerParams(vmem_limit_bytes=24 * 2**20),
         cost_estimate=pl.CostEstimate(
             flops=8 * rows * vis * sources, bytes_accessed=16 * vis * sources + 4 * rows * sources, transcendentals=0
         ),
         name="update_products",
-    )(owners, *[array for group in arrivals for array in group], focusing, v_factors)
+    )(owners, *arrivals, focusing, v_factors)
 
 
 def swap(array, axis):
     return lax.ppermute(array, axis, [(0, 1), (1, 0)])
 
 
-def exchange_columns(arrays, count_col):
+def exchange(arrays, count_col):
     moved = list(arrays)
-    for d in range(count_col - 1, 0, -1):
-        moved[d] = lax.ppermute(arrays[d], "col", [(i, i ^ d) for i in range(count_col)])
+    for d in range(count_col - 1, -1, -1):
+        for e in (1, 0):
+            offset = 2 * d + e
+            if offset:
+                moved[offset] = lax.ppermute(
+                    arrays[offset], ("col", "freq"), [(i, i ^ offset) for i in range(2 * count_col)]
+                )
     return moved
 
 
@@ -422,25 +469,45 @@
     place = lax.axis_index("grp") * 2 + lax.axis_index("rep")
     table = jnp.asarray(mixing_table(2))
     tile_onsets = onsets.reshape(NR // TS, 1, TS)
-    quarters = []
+    first = []
     for s in range(half):
         piece = lax.dynamic_slice(
             u_factors, (0, 0, (1 - mine) * half + s, place * (rows // 4), 0), (1, 2, 1, rows // 4, TS)
         ).reshape(2, rows // 4, TS)
-        first = swap(piece, "freq")
-        second = swap(first, "grp")
-        quarters.append([first, swap(first, "rep"), second, swap(second, "rep")])
-    outgoing = forward_products(count_col, half, focusing, v_factors, tile_ranks, owners)
-    arrivals = []
+        first.append(swap(piece, "freq"))
+    *outgoing, focus_here, v_here = forward_products(count_col, half, focusing, v_factors, tile_ranks, owners)
+    def move(offset, payload):
+        return lax.ppermute(payload, ("col", "freq"), [(i, i ^ offset) for i in range(2 * count_col)])
+    arrived = list(outgoing)
+    far, _ = lax.optimization_barrier((u_factors, outgoing[0]))
+    u_here = load_factors(half, far)
+    second = []
+    if 2 == 2:
+        first[0], _ = lax.optimization_barrier((first[0], outgoing[0]))
+        second.append(swap(first[0], "grp"))
+    for offset in (6, 4, 2):
+        arrived[offset] = move(offset, arrived[offset])
+    held = lax.optimization_barrier(tuple(arrived + first + [u_here] + second))
+    if 2 == 2:
+        second = [held[-1]]
+        held = held[:-1]
+    arrived, first, u_here = list(held[: 2 * count_col]), list(held[2 * count_col : -1]), held[-1]
+    if 2 == 3:
+        second.append(swap(first[0], "grp"))
+    second.append(swap(first[1], "grp"))
+    for offset in (7, 5, 3, 1):
+        arrived[offset] = move(offset, arrived[offset])
+    held = lax.optimization_barrier(tuple(arrived + first + second[:1]))
+    arrived = list(held[:-3])
+    first, second = list(held[-3:-1]), [held[-1], second[1]]
+    back = []
     for s in range(half):
-        arrived = exchange_columns(outgoing[s * count_col : (s + 1) * count_col], count_col)
-        crossed = swap(jnp.stack([array[1] for array in arrived]), "freq")
+        gathered = [first[s], swap(first[s], "rep"), second[s], swap(second[s], "rep")]
         back = receiver_products(
-            count_col, half, s, owners, tile_ranks, tile_onsets, table, arrived, crossed, u_factors, quarters[s]
+            count_col, half, s, owners, tile_ranks, tile_onsets, table, arrived, u_here, gathered, back
         )
-        returned = exchange_columns(back, count_col)
-        arrivals.append(returned + [swap(jnp.stack([array[1] for array in returned]), "freq")])
-    return update_products(count_col, half, owners, arrivals, focusing, v_factors)
+    returned = exchange(back, count_col)
+    return update_products(count_col, half, owners, returned, focus_here, v_here)
 
 
 def per_device(focusing, v_factors, u_factors, tile_ranks, owners, onsets):

time: 97.1 us -> 74.5 us (0.77); the launches traced: 96.9 us -> 73.3 us
  waiting for transfers between devices: 40.3 us -> 21.1 us
  local copies, waits for them, and re-layouts: 7.62 us -> 2.55 us
  Pallas kernels: 18.3 us -> 20.4 us
  starting transfers between devices: 30.3 us -> 29 us
    ppermute x12 -> x8, waiting for transfers between devices: 24.9 us -> 2.21 us  [swap(): return lax.ppermute(array, axis, [(0, 1), (1, 0)])]
    ppermute x12 -> x8, starting transfers between devices: 12.1 us -> 6.7 us  [swap(): return lax.ppermute(array, axis, [(0, 1), (1, 0)])]
    unnamed x18 -> x16, local copies, waits for them, and re-layouts: 6.35 us -> 1.39 us
    ppermute x12 -> x14, starting transfers between devices: 18.2 us -> 22.3 us  [the longest x7 11.2 us: exchange(): lax.ppermute(arrays[offset], ('col', 'freq'), [(i, i ^ offset) for i in r...]
    ppermute x12 -> x14, waiting for transfers between devices: 15.4 us -> 18.9 us  [the longest x7 9.89 us: move(): lax.ppermute(payload, ('col', 'freq'), [(i, i ^ offset) for i in range(2...]
    pallas_call x2 -> x3, Pallas kernels: 10.5 us -> 13 us  [the longest x1 7.52 us: forward_products(): pl.pallas_call(functools.partial(forward_kernel, count_col, half), in_spe...]
  transfers between devices with their start and end apart: 24 -> 22, of which waited for: 12 -> 10; matrix products, arithmetic and copies ran while one was open for 0% -> 0% of each run, Pallas kernels for 12% -> 18%
where the time goes in v2:
time: 74.5 us; the launch traced here: 73.3 us
  starting transfers between devices  29 us (39%)
  waiting for transfers between devices  21.1 us (28%)
  Pallas kernels  20.4 us (27%)
  local copies, waits for them, and re-layouts  2.55 us (3%)
    ppermute x7, starting transfers between devices, exchange(): lax.ppermute(arrays[offset], ('col', 'freq'), [(i, i ^ offset) for i in r...  11.2 us
    ppermute x7, starting transfers between devices, move(): lax.ppermute(payload, ('col', 'freq'), [(i, i ^ offset) for i in range(2...  11.1 us
    ppermute x7, waiting for transfers between devices, move(): lax.ppermute(payload, ('col', 'freq'), [(i, i ^ offset) for i in range(2...  9.89 us
    ppermute x7, waiting for transfers between devices, exchange(): lax.ppermute(arrays[offset], ('col', 'freq'), [(i, i ^ offset) for i in r...  9.04 us
    pallas_call x1, Pallas kernels, forward_products(): pl.pallas_call(functools.partial(forward_kernel, count_col, half), in_spe...  7.52 us
    pallas_call x2, Pallas kernels, receiver_products(): pl.pallas_call(functools.partial(receiver_kernel, count_col, half, chunk)...  7.39 us
    ppermute x8, starting transfers between devices, swap(): return lax.ppermute(array, axis, [(0, 1), (1, 0)])  6.7 us
    pallas_call x1, Pallas kernels, update_products(): pl.pallas_call(functools.partial(update_kernel, count_col, half), in_spec...  3.42 us
  transfers between devices with their start and end apart: 22, of which 10 were waited for; matrix products, arithmetic and copies ran while one was open for 0% of the time, Pallas kernels for 18%

profile of v2, /device:TPU:0, one launch (start us, length us, event | category | flops | bytes accessed | tf_op | source)
XLA Modules:
  0.0 73.3 jit_solution(9725646512638079245)
XLA Ops:
  0.0 1.2 %dynamic-slice_bitcast_fusion = (bf16[2,96,1024]{2,1,0:T(8,128)(2,1)S(1)}, bf16[2,96,1024]{2,1,0:T(8,128)(2,1)S(1)}) fusion(bf16[1,2,4,384,1024]{4,3,2,1,0:T(8,128)(2,1)} %u_factors, s32[]{:T(128)S(6)} %select_n.12, s32[]{:T(128)S(6)} %select_n.11, s32[]{:T(128)S(6)} %select_n.10), kind=kLoop, calls=%fused_computation | loop fusion | bytes 1572876 | tf_op jit(solution)/shard_map/reshape | solution.py:476
  1.2 3.0 %collective-permute-start.3 = (bf16[2,96,1024]{2,1,0:T(8,128)(2,1)S(1)}, bf16[2,96,1024]{2,1,0:T(8,128)(2,1)S(1)}, u32[]{:S(2)}, u32[]{:S(2)}) collective-permute-start(bf16[2,96,1024]{2,1,0:T(8,128)(2,1)S(1)} %get-tuple-element.108), channel_id=1, source_target_pairs={{0,2},{2,0},{1,3},{3,1},{4,6},{6,4},{5,7},{7,5},{8,10},{10,8},{9,1... | collective-permute-start | bytes 1179656 | tf_op jit(solution)/shard_map/ppermute | solution.py:448
  4.2 0.1 collective-permute-start.4
  4.3 0.0 copy-start.2
  4.3 0.7 copy-done.2
  5.0 0.7 copy-done.4
  5.6 7.5 %forward_products.1 = (bf16[2,96,256]{2,1,0:T(8,128)(2,1)S(1)}, bf16[2,96,256]{2,1,0:T(8,128)(2,1)S(1)}, bf16[2,96,256]{2,1,0:T(8,128)(2,1)S(1)}, bf16[2,96,256]...) custom-call(s32[16]{0:T(128)S(1)} %copy-done.4, ...), custom_call_target="tpu_custom_call" | custom-call | flops 1610612736 | bytes 10485760 | tf_op jit(solution)/shard_map/forward_products/pallas_call | solution.py:235
  13.1 0.0 copy-start
  13.1 0.0 copy-start.1
  13.2 0.0 copy-start.3
  13.2 0.0 copy-start.5
  13.2 0.9 %collective-permute-done.3.refs_9_ = bf16[2,96,1024]{2,1,0:T(8,128)(2,1)S(1)} collective-permute-done((bf16[2,96,1024]{2,1,0:T(8,128)(2,1)S(1)}, bf16[2,96,1024]{2,1,0:T(8,128)(2,1)S(1)}, u32[]{:S(2)}, u32[]{:S(2)}) %collective-permute-start.3) | collective-permute-done | bytes 393248 | tf_op jit(solution)/shard_map/ppermute | solution.py:448
  14.1 2.1 %collective-permute-start.5 = (bf16[2,96,1024]{2,1,0:T(8,128)(2,1)S(1)}, bf16[2,96,1024]{2,1,0:T(8,128)(2,1)S(1)}, u32[]{:S(2)}, u32[]{:S(2)}) collective-permute-start(bf16[2,96,1024]{2,1,0:T(8,128)(2,1)S(1)} %collective-permute-done.3.refs_9_), channel_id=1, source_target_pairs={{0,16},{16,0},{1,17},{17,1},{2,18},{18,2},{3,19},{19,3},{4,20},{20... | collective-permute-start | bytes 1179656 | tf_op jit(solution)/shard_map/ppermute | solution.py:448
  16.2 1.6 %collective-permute-start = (bf16[2,96,256]{2,1,0:T(8,128)(2,1)S(1)}, bf16[2,96,256]{2,1,0:T(8,128)(2,1)S(1)}, u32[]{:S(2)}, u32[]{:S(2)}) collective-permute-start(bf16[2,96,256]{2,1,0:T(8,128)(2,1)S(1)} %get-tuple-element.58), channel_id=1, source_target_pairs={{0,4},{2,6},{4,0},{6,2},{8,12},{10,14},{12,8},{14,10},{1,5},{3,7},... | collective-permute-start | bytes 294920 | tf_op jit(solution)/shard_map/ppermute | solution.py:480
  17.8 2.6 %collective-permute-start.1 = (bf16[2,96,256]{2,1,0:T(8,128)(2,1)S(1)}, bf16[2,96,256]{2,1,0:T(8,128)(2,1)S(1)}, u32[]{:S(2)}, u32[]{:S(2)}) collective-permute-start(bf16[2,96,256]{2,1,0:T(8,128)(2,1)S(1)} %get-tuple-element.60), channel_id=1, source_target_pairs={{0,8},{2,10},{4,12},{6,14},{8,0},{10,2},{12,4},{14,6},{1,9},{3,11}... | collective-permute-start | bytes 294920 | tf_op jit(solution)/shard_map/ppermute | solution.py:480
  20.4 0.2 collective-permute-start.2
  20.6 2.0 %load_factors.1.refs_8_ = bf16[2,2,384,1024]{3,2,1,0:T(8,128)(2,1)S(1)} custom-call(bf16[1,2,4,384,1024]{4,3,2,1,0:T(8,128)(2,1)} %u_factors), custom_call_target="tpu_custom_call" | custom-call | bytes 3145728 | tf_op jit(solution)/shard_map/load_factors/pallas_call | solution.py:269
  22.6 0.0 collective-permute-done.refs_2_
  22.7 2.7 %collective-permute-done.1.refs_4_ = bf16[2,96,256]{2,1,0:T(8,128)(2,1)S(1)} collective-permute-done((bf16[2,96,256]{2,1,0:T(8,128)(2,1)S(1)}, bf16[2,96,256]{2,1,0:T(8,128)(2,1)S(1)}, u32[]{:S(2)}, u32[]{:S(2)}) %collective-permute-start.1) | collective-permute-done | bytes 98336 | tf_op jit(solution)/shard_map/ppermute | solution.py:480
  25.4 1.5 %collective-permute-done.2.refs_6_ = bf16[2,96,256]{2,1,0:T(8,128)(2,1)S(1)} collective-permute-done((bf16[2,96,256]{2,1,0:T(8,128)(2,1)S(1)}, bf16[2,96,256]{2,1,0:T(8,128)(2,1)S(1)}, u32[]{:S(2)}, u32[]{:S(2)}) %collective-permute-start.2) | collective-permute-done | bytes 98336 | tf_op jit(solution)/shard_map/ppermute | solution.py:480
  26.9 0.0 collective-permute-done.4.refs_9_
  26.9 0.0 collective-permute-done.5.refs_11_
  26.9 0.5 collective-permute-start.11
  27.4 1.5 %collective-permute-start.6 = (bf16[2,96,256]{2,1,0:T(8,128)(2,1)S(1)}, bf16[2,96,256]{2,1,0:T(8,128)(2,1)S(1)}, u32[]{:S(2)}, u32[]{:S(2)}) collective-permute-start(bf16[2,96,256]{2,1,0:T(8,128)(2,1)S(1)} %get-tuple-element.67), channel_id=1, source_target_pairs={{0,2},{2,0},{4,6},{6,4},{8,10},{10,8},{12,14},{14,12},{1,3},{3,1},... | collective-permute-start | bytes 294920 | tf_op jit(solution)/shard_map/ppermute | solution.py:480
  28.9 1.1 %collective-permute-start.7 = (bf16[2,96,256]{2,1,0:T(8,128)(2,1)S(1)}, bf16[2,96,256]{2,1,0:T(8,128)(2,1)S(1)}, u32[]{:S(2)}, u32[]{:S(2)}) collective-permute-start(bf16[2,96,256]{2,1,0:T(8,128)(2,1)S(1)} %get-tuple-element.69), channel_id=1, source_target_pairs={{0,6},{2,4},{4,2},{6,0},{8,14},{10,12},{12,10},{14,8},{1,7},{3,5},... | collective-permute-start | bytes 294920 | tf_op jit(solution)/shard_map/ppermute | solution.py:480
  30.0 2.4 %collective-permute-start.8 = (bf16[2,96,256]{2,1,0:T(8,128)(2,1)S(1)}, bf16[2,96,256]{2,1,0:T(8,128)(2,1)S(1)}, u32[]{:S(2)}, u32[]{:S(2)}) collective-permute-start(bf16[2,96,256]{2,1,0:T(8,128)(2,1)S(1)} %get-tuple-element.71), channel_id=1, source_target_pairs={{0,10},{2,8},{4,14},{6,12},{8,2},{10,0},{12,6},{14,4},{1,11},{3,9}... | collective-permute-start | bytes 294920 | tf_op jit(solution)/shard_map/ppermute | solution.py:480
  32.4 1.8 %collective-permute-start.9 = (bf16[2,96,256]{2,1,0:T(8,128)(2,1)S(1)}, bf16[2,96,256]{2,1,0:T(8,128)(2,1)S(1)}, u32[]{:S(2)}, u32[]{:S(2)}) collective-permute-start(bf16[2,96,256]{2,1,0:T(8,128)(2,1)S(1)} %get-tuple-element.73), channel_id=1, source_target_pairs={{0,14},{2,12},{4,10},{6,8},{8,6},{10,4},{12,2},{14,0},{1,15},{3,13... | collective-permute-start | bytes 294920 | tf_op jit(solution)/shard_map/ppermute | solution.py:480
  34.2 0.0 collective-permute-done.6.refs_1_
  34.2 1.3 %collective-permute-done.7.refs_3_ = bf16[2,96,256]{2,1,0:T(8,128)(2,1)S(1)} collective-permute-done((bf16[2,96,256]{2,1,0:T(8,128)(2,1)S(1)}, bf16[2,96,256]{2,1,0:T(8,128)(2,1)S(1)}, u32[]{:S(2)}, u32[]{:S(2)}) %collective-permute-start.7) | collective-permute-done | bytes 98336 | tf_op jit(solution)/shard_map/ppermute | solution.py:480
  35.5 2.6 %collective-permute-done.8.refs_5_ = bf16[2,96,256]{2,1,0:T(8,128)(2,1)S(1)} collective-permute-done((bf16[2,96,256]{2,1,0:T(8,128)(2,1)S(1)}, bf16[2,96,256]{2,1,0:T(8,128)(2,1)S(1)}, u32[]{:S(2)}, u32[]{:S(2)}) %collective-permute-start.8) | collective-permute-done | bytes 98336 | tf_op jit(solution)/shard_map/ppermute | solution.py:480
  38.0 1.8 %collective-permute-done.9.refs_7_ = bf16[2,96,256]{2,1,0:T(8,128)(2,1)S(1)} collective-permute-done((bf16[2,96,256]{2,1,0:T(8,128)(2,1)S(1)}, bf16[2,96,256]{2,1,0:T(8,128)(2,1)S(1)}, u32[]{:S(2)}, u32[]{:S(2)}) %collective-permute-start.9) | collective-permute-done | bytes 98336 | tf_op jit(solution)/shard_map/ppermute | solution.py:480
  39.8 0.0 collective-permute-start.13
  39.8 0.5 collective-permute-start.14
  40.3 0.0 collective-permute-start.10
  40.3 0.0 collective-permute-done.11.refs_11_
  40.3 0.5 collective-permute-start.12
  40.8 0.7 collective-permute-done.13.refs_10_
  41.5 0.6 collective-permute-done.14.refs_12_
  42.1 0.0 copy-done
  42.1 0.0 copy-done.1
  42.1 0.0 copy-done.3
  42.1 0.0 copy-done.5
  42.1 0.0 slice-start.1
  42.1 3.7 %receiver_products.2 = (bf16[1,96,256]{2,1,0:T(8,128)(2,1)S(1)}, bf16[1,96,256]{2,1,0:T(8,128)(2,1)S(1)}, bf16[1,96,256]{2,1,0:T(8,128)(2,1)S(1)}, bf16[1,96,256...) custom-call(s32[16]{0:T(128)S(1)} %copy-done.5, ...), custom_call_target="tpu_custom_call" | custom-call | flops 1610612736 | bytes 3145728 | tf_op jit(solution)/shard_map/receiver_products/pallas_call | solution.py:355
  45.8 0.0 collective-permute-done.10.refs_10_
  45.8 0.0 collective-permute-done.12.refs_12_
  45.8 3.7 %receiver_products.3 = (bf16[2,96,256]{2,1,0:T(8,128)(2,1)S(1)}, bf16[2,96,256]{2,1,0:T(8,128)(2,1)S(1)}, bf16[2,96,256]{2,1,0:T(8,128)(2,1)S(1)}, bf16[2,96,256...) custom-call(s32[16]{0:T(128)S(1)} %copy-done.5, ...), custom_call_target="tpu_custom_call" | custom-call | flops 1610612736 | bytes 3145728 | tf_op jit(solution)/shard_map/receiver_products/pallas_call | solution.py:355
  49.6 0.6 collective-permute-start.15
  50.2 1.3 %collective-permute-start.16 = (bf16[2,96,256]{2,1,0:T(8,128)(2,1)S(1)}, bf16[2,96,256]{2,1,0:T(8,128)(2,1)S(1)}, u32[]{:S(2)}, u32[]{:S(2)}) collective-permute-start(bf16[2,96,256]{2,1,0:T(8,128)(2,1)S(1)} %get-tuple-element.99), channel_id=1, source_target_pairs={{0,4},{2,6},{4,0},{6,2},{8,12},{10,14},{12,8},{14,10},{1,5},{3,7},... | collective-permute-start | bytes 294920 | tf_op jit(solution)/shard_map/ppermute | solution.py:457
  51.5 1.6 %collective-permute-start.17 = (bf16[2,96,256]{2,1,0:T(8,128)(2,1)S(1)}, bf16[2,96,256]{2,1,0:T(8,128)(2,1)S(1)}, u32[]{:S(2)}, u32[]{:S(2)}) collective-permute-start(bf16[2,96,256]{2,1,0:T(8,128)(2,1)S(1)} %get-tuple-element.100), channel_id=1, source_target_pairs={{0,6},{2,4},{4,2},{6,0},{8,14},{10,12},{12,10},{14,8},{1,7},{3,5},... | collective-permute-start | bytes 294920 | tf_op jit(solution)/shard_map/ppermute | solution.py:457
  53.1 1.9 %collective-permute-start.18 = (bf16[2,96,256]{2,1,0:T(8,128)(2,1)S(1)}, bf16[2,96,256]{2,1,0:T(8,128)(2,1)S(1)}, u32[]{:S(2)}, u32[]{:S(2)}) collective-permute-start(bf16[2,96,256]{2,1,0:T(8,128)(2,1)S(1)} %get-tuple-element.101), channel_id=1, source_target_pairs={{0,8},{2,10},{4,12},{6,14},{8,0},{10,2},{12,4},{14,6},{1,9},{3,11}... | collective-permute-start | bytes 294920 | tf_op jit(solution)/shard_map/ppermute | solution.py:457
  55.0 1.0 %collective-permute-start.19 = (bf16[2,96,256]{2,1,0:T(8,128)(2,1)S(1)}, bf16[2,96,256]{2,1,0:T(8,128)(2,1)S(1)}, u32[]{:S(2)}, u32[]{:S(2)}) collective-permute-start(bf16[2,96,256]{2,1,0:T(8,128)(2,1)S(1)} %get-tuple-element.102), channel_id=1, source_target_pairs={{0,10},{2,8},{4,14},{6,12},{8,2},{10,0},{12,6},{14,4},{1,11},{3,9}... | collective-permute-start | bytes 294920 | tf_op jit(solution)/shard_map/ppermute | solution.py:457
  56.0 0.0 collective-permute-done.15.refs_1_
  56.0 2.0 %collective-permute-start.20 = (bf16[2,96,256]{2,1,0:T(8,128)(2,1)S(1)}, bf16[2,96,256]{2,1,0:T(8,128)(2,1)S(1)}, u32[]{:S(2)}, u32[]{:S(2)}) collective-permute-start(bf16[2,96,256]{2,1,0:T(8,128)(2,1)S(1)} %get-tuple-element.103), channel_id=1, source_target_pairs={{0,12},{2,14},{4,8},{6,10},{8,4},{10,6},{12,0},{14,2},{1,13},{3,15... | collective-permute-start | bytes 294920 | tf_op jit(solution)/shard_map/ppermute | solution.py:457
  58.1 0.0 collective-permute-done.16.refs_2_
  58.1 2.7 %collective-permute-start.21 = (bf16[2,96,256]{2,1,0:T(8,128)(2,1)S(1)}, bf16[2,96,256]{2,1,0:T(8,128)(2,1)S(1)}, u32[]{:S(2)}, u32[]{:S(2)}) collective-permute-start(bf16[2,96,256]{2,1,0:T(8,128)(2,1)S(1)} %get-tuple-element.104), channel_id=1, source_target_pairs={{0,14},{2,12},{4,10},{6,8},{8,6},{10,4},{12,2},{14,0},{1,15},{3,13... | collective-permute-start | bytes 294920 | tf_op jit(solution)/shard_map/ppermute | solution.py:457
  60.8 0.0 collective-permute-done.17.refs_3_
  60.8 7.1 %collective-permute-done.18.refs_4_ = bf16[2,96,256]{2,1,0:T(8,128)(2,1)S(1)} collective-permute-done((bf16[2,96,256]{2,1,0:T(8,128)(2,1)S(1)}, bf16[2,96,256]{2,1,0:T(8,128)(2,1)S(1)}, u32[]{:S(2)}, u32[]{:S(2)}) %collective-permute-start.18) | collective-permute-done | bytes 98336 | tf_op jit(solution)/shard_map/ppermute | solution.py:457
  67.9 1.9 %collective-permute-done.19.refs_5_ = bf16[2,96,256]{2,1,0:T(8,128)(2,1)S(1)} collective-permute-done((bf16[2,96,256]{2,1,0:T(8,128)(2,1)S(1)}, bf16[2,96,256]{2,1,0:T(8,128)(2,1)S(1)}, u32[]{:S(2)}, u32[]{:S(2)}) %collective-permute-start.19) | collective-permute-done | bytes 98336 | tf_op jit(solution)/shard_map/ppermute | solution.py:457
  69.8 0.0 collective-permute-done.20.refs_6_
  69.8 0.0 collective-permute-done.21.refs_7_
  69.8 0.0 slice-done
  69.8 0.0 slice-done.1
  69.8 3.4 %update_products.1 = f32[1,2,128,4096]{3,2,1,0:T(8,128)} custom-call(s32[16]{0:T(128)S(1)} %copy-done.5, bf16[2,96,256]{2,1,0:T(8,128)(2,1)S(1)} %get-tuple-element.97.refs_0_, bf16[2,96,256]{2,1,0:T(8,128)(2,1)S(1)} %collective-permute-done.15.refs_1_, bf16[2,96,256]{2,1,0:T(8,128)(2,1)S(1)} %collective-permute-done.16.refs_2_, ...), custom_call_target="tpu_custom_call" | custom-call | flops 1610612736 | bytes 14680064 | tf_op jit(solution)/shard_map/update_products/pallas_call | solution.py:426
  (3 shorter events, 0.0 us)
Async XLA Ops:
  1.2 12.9 %collective-permute-start.3 = (bf16[2,96,1024]{2,1,0:T(8,128)(2,1)S(1)}, bf16[2,96,1024]{2,1,0:T(8,128)(2,1)S(1)}, u32[]{:S(2)}, u32[]{:S(2)}) collective-permute-start(bf16[2,96,1024]{2,1,0:T(8,128)(2,1)S(1)} %get-tuple-element.108), channel_id=1, source_target_pairs={{0,2},{2,0},{1,3},{3,1},{4,6},{6,4},{5,7},{7,5},{8,10},{10,8},{9,1... | collective-permute-start | bytes 1179656 | tf_op jit(solution)/shard_map/ppermute | solution.py:448
  4.2 22.7 %collective-permute-start.4 = (bf16[2,96,1024]{2,1,0:T(8,128)(2,1)S(1)}, bf16[2,96,1024]{2,1,0:T(8,128)(2,1)S(1)}, u32[]{:S(2)}, u32[]{:S(2)}) collective-permute-start(bf16[2,96,1024]{2,1,0:T(8,128)(2,1)S(1)} %get-tuple-element.107), channel_id=1, source_target_pairs={{0,2},{2,0},{1,3},{3,1},{4,6},{6,4},{5,7},{7,5},{8,10},{10,8},{9,1... | collective-permute-start | bytes 1179656 | tf_op jit(solution)/shard_map/ppermute | solution.py:448
  4.3 0.7 copy-start.2
  5.0 0.7 copy-start.4
  13.1 29.0 %copy-start = (bf16[2,48,512]{2,1,0:T(8,128)(2,1)S(1)}, bf16[2,48,512]{2,1,0:T(8,128)(2,1)}, u32[]{:S(2)}) copy-start(bf16[2,48,512]{2,1,0:T(8,128)(2,1)} %constant.26.clone.table) | copy-start | bytes 294916
  13.1 29.0 %copy-start.1 = (s32[16384]{0:T(1024)S(1)}, s32[16384]{0:T(1024)}, u32[]{:S(2)}) copy-start(s32[16384]{0:T(1024)} %param.12) | copy-start | bytes 196612
  13.2 29.0 %copy-start.3 = (s32[16,16]{1,0:T(8,128)S(1)}, s32[16,16]{1,0:T(8,128)}, u32[]{:S(2)}) copy-start(s32[16,16]{1,0:T(8,128)} %ranks.3) | copy-start | bytes 3076
  13.2 28.9 %copy-start.5 = (s32[16]{0:T(128)S(1)}, s32[16]{0:T(128)}, u32[]{:S(2)}) copy-start(s32[16]{0:T(128)} %owners.5) | copy-start | bytes 196
  14.1 12.8 %collective-permute-start.5 = (bf16[2,96,1024]{2,1,0:T(8,128)(2,1)S(1)}, bf16[2,96,1024]{2,1,0:T(8,128)(2,1)S(1)}, u32[]{:S(2)}, u32[]{:S(2)}) collective-permute-start(bf16[2,96,1024]{2,1,0:T(8,128)(2,1)S(1)} %collective-permute-done.3.refs_9_), channel_id=1, source_target_pairs={{0,16},{16,0},{1,17},{17,1},{2,18},{18,2},{3,19},{19,3},{4,20},{20... | collective-permute-start | bytes 1179656 | tf_op jit(solution)/shard_map/ppermute | solution.py:448
  16.2 6.4 %collective-permute-start = (bf16[2,96,256]{2,1,0:T(8,128)(2,1)S(1)}, bf16[2,96,256]{2,1,0:T(8,128)(2,1)S(1)}, u32[]{:S(2)}, u32[]{:S(2)}) collective-permute-start(bf16[2,96,256]{2,1,0:T(8,128)(2,1)S(1)} %get-tuple-element.58), channel_id=1, source_target_pairs={{0,4},{2,6},{4,0},{6,2},{8,12},{10,14},{12,8},{14,10},{1,5},{3,7},... | collective-permute-start | bytes 294920 | tf_op jit(solution)/shard_map/ppermute | solution.py:480
  17.8 7.6 %collective-permute-start.1 = (bf16[2,96,256]{2,1,0:T(8,128)(2,1)S(1)}, bf16[2,96,256]{2,1,0:T(8,128)(2,1)S(1)}, u32[]{:S(2)}, u32[]{:S(2)}) collective-permute-start(bf16[2,96,256]{2,1,0:T(8,128)(2,1)S(1)} %get-tuple-element.60), channel_id=1, source_target_pairs={{0,8},{2,10},{4,12},{6,14},{8,0},{10,2},{12,4},{14,6},{1,9},{3,11}... | collective-permute-start | bytes 294920 | tf_op jit(solution)/shard_map/ppermute | solution.py:480
  20.4 6.5 %collective-permute-start.2 = (bf16[2,96,256]{2,1,0:T(8,128)(2,1)S(1)}, bf16[2,96,256]{2,1,0:T(8,128)(2,1)S(1)}, u32[]{:S(2)}, u32[]{:S(2)}) collective-permute-start(bf16[2,96,256]{2,1,0:T(8,128)(2,1)S(1)} %get-tuple-element.62), channel_id=1, source_target_pairs={{0,12},{2,14},{4,8},{6,10},{8,4},{10,6},{12,0},{14,2},{1,13},{3,15... | collective-permute-start | bytes 294920 | tf_op jit(solution)/shard_map/ppermute | solution.py:480
  20.6 49.2 %slice-start = ((s8[6291456]{0:T(1024)(128)(4,1)}), s8[4194304]{0:T(1024)(128)(4,1)S(1)}, s32[]{:S(2)}) async-start(s8[6291456]{0:T(1024)(128)(4,1)} %bitcast.5), calls=%async_computation | async-start | bytes 8388608
  26.9 13.4 %collective-permute-start.11 = (bf16[2,96,1024]{2,1,0:T(8,128)(2,1)S(1)}, bf16[2,96,1024]{2,1,0:T(8,128)(2,1)S(1)}, u32[]{:S(2)}, u32[]{:S(2)}) collective-permute-start(bf16[2,96,1024]{2,1,0:T(8,128)(2,1)S(1)} %collective-permute-done.4.refs_9_), channel_id=1, source_target_pairs={{0,16},{16,0},{1,17},{17,1},{2,18},{18,2},{3,19},{19,3},{4,20},{20... | collective-permute-start | bytes 1179656 | tf_op jit(solution)/shard_map/ppermute | solution.py:448
  27.4 6.8 %collective-permute-start.6 = (bf16[2,96,256]{2,1,0:T(8,128)(2,1)S(1)}, bf16[2,96,256]{2,1,0:T(8,128)(2,1)S(1)}, u32[]{:S(2)}, u32[]{:S(2)}) collective-permute-start(bf16[2,96,256]{2,1,0:T(8,128)(2,1)S(1)} %get-tuple-element.67), channel_id=1, source_target_pairs={{0,2},{2,0},{4,6},{6,4},{8,10},{10,8},{12,14},{14,12},{1,3},{3,1},... | collective-permute-start | bytes 294920 | tf_op jit(solution)/shard_map/ppermute | solution.py:480
  28.9 6.6 %collective-permute-start.7 = (bf16[2,96,256]{2,1,0:T(8,128)(2,1)S(1)}, bf16[2,96,256]{2,1,0:T(8,128)(2,1)S(1)}, u32[]{:S(2)}, u32[]{:S(2)}) collective-permute-start(bf16[2,96,256]{2,1,0:T(8,128)(2,1)S(1)} %get-tuple-element.69), channel_id=1, source_target_pairs={{0,6},{2,4},{4,2},{6,0},{8,14},{10,12},{12,10},{14,8},{1,7},{3,5},... | collective-permute-start | bytes 294920 | tf_op jit(solution)/shard_map/ppermute | solution.py:480
  30.0 8.0 %collective-permute-start.8 = (bf16[2,96,256]{2,1,0:T(8,128)(2,1)S(1)}, bf16[2,96,256]{2,1,0:T(8,128)(2,1)S(1)}, u32[]{:S(2)}, u32[]{:S(2)}) collective-permute-start(bf16[2,96,256]{2,1,0:T(8,128)(2,1)S(1)} %get-tuple-element.71), channel_id=1, source_target_pairs={{0,10},{2,8},{4,14},{6,12},{8,2},{10,0},{12,6},{14,4},{1,11},{3,9}... | collective-permute-start | bytes 294920 | tf_op jit(solution)/shard_map/ppermute | solution.py:480
  32.4 7.4 %collective-permute-start.9 = (bf16[2,96,256]{2,1,0:T(8,128)(2,1)S(1)}, bf16[2,96,256]{2,1,0:T(8,128)(2,1)S(1)}, u32[]{:S(2)}, u32[]{:S(2)}) collective-permute-start(bf16[2,96,256]{2,1,0:T(8,128)(2,1)S(1)} %get-tuple-element.73), channel_id=1, source_target_pairs={{0,14},{2,12},{4,10},{6,8},{8,6},{10,4},{12,2},{14,0},{1,15},{3,13... | collective-permute-start | bytes 294920 | tf_op jit(solution)/shard_map/ppermute | solution.py:480
  39.8 1.7 %collective-permute-start.13 = (bf16[2,96,1024]{2,1,0:T(8,128)(2,1)S(1)}, bf16[2,96,1024]{2,1,0:T(8,128)(2,1)S(1)}, u32[]{:S(2)}, u32[]{:S(2)}) collective-permute-start(bf16[2,96,1024]{2,1,0:T(8,128)(2,1)S(1)} %collective-permute-done.3.refs_9_), channel_id=1, source_target_pairs={{0,1},{1,0},{2,3},{3,2},{4,5},{5,4},{6,7},{7,6},{8,9},{9,8},{10,11... | collective-permute-start | bytes 1179656 | tf_op jit(solution)/shard_map/ppermute | solution.py:448
  39.8 2.3 %collective-permute-start.14 = (bf16[2,96,1024]{2,1,0:T(8,128)(2,1)S(1)}, bf16[2,96,1024]{2,1,0:T(8,128)(2,1)S(1)}, u32[]{:S(2)}, u32[]{:S(2)}) collective-permute-start(bf16[2,96,1024]{2,1,0:T(8,128)(2,1)S(1)} %collective-permute-done.5.refs_11_), channel_id=1, source_target_pairs={{0,1},{1,0},{2,3},{3,2},{4,5},{5,4},{6,7},{7,6},{8,9},{9,8},{10,11... | collective-permute-start | bytes 1179656 | tf_op jit(solution)/shard_map/ppermute | solution.py:448
  40.3 5.5 %collective-permute-start.10 = (bf16[2,96,1024]{2,1,0:T(8,128)(2,1)S(1)}, bf16[2,96,1024]{2,1,0:T(8,128)(2,1)S(1)}, u32[]{:S(2)}, u32[]{:S(2)}) collective-permute-start(bf16[2,96,1024]{2,1,0:T(8,128)(2,1)S(1)} %collective-permute-done.4.refs_9_), channel_id=1, source_target_pairs={{0,1},{1,0},{2,3},{3,2},{4,5},{5,4},{6,7},{7,6},{8,9},{9,8},{10,11... | collective-permute-start | bytes 1179656 | tf_op jit(solution)/shard_map/ppermute | solution.py:448
  40.3 5.5 %collective-permute-start.12 = (bf16[2,96,1024]{2,1,0:T(8,128)(2,1)S(1)}, bf16[2,96,1024]{2,1,0:T(8,128)(2,1)S(1)}, u32[]{:S(2)}, u32[]{:S(2)}) collective-permute-start(bf16[2,96,1024]{2,1,0:T(8,128)(2,1)S(1)} %collective-permute-done.11.refs_11_), channel_id=1, source_target_pairs={{0,1},{1,0},{2,3},{3,2},{4,5},{5,4},{6,7},{7,6},{8,9},{9,8},{10,11... | collective-permute-start | bytes 1179656 | tf_op jit(solution)/shard_map/ppermute | solution.py:448
  42.1 27.7 %slice-start.1 = ((s8[6291456]{0:T(1024)(128)(4,1)}), s8[2097152]{0:T(1024)(128)(4,1)S(1)}, s32[]{:S(2)}) async-start(s8[6291456]{0:T(1024)(128)(4,1)} %bitcast.5), calls=%async_computation.1 | async-start | bytes 4194304
  49.6 6.5 %collective-permute-start.15 = (bf16[2,96,256]{2,1,0:T(8,128)(2,1)S(1)}, bf16[2,96,256]{2,1,0:T(8,128)(2,1)S(1)}, u32[]{:S(2)}, u32[]{:S(2)}) collective-permute-start(bf16[2,96,256]{2,1,0:T(8,128)(2,1)S(1)} %get-tuple-element.98), channel_id=1, source_target_pairs={{0,2},{2,0},{4,6},{6,4},{8,10},{10,8},{12,14},{14,12},{1,3},{3,1},... | collective-permute-start | bytes 294920 | tf_op jit(solution)/shard_map/ppermute | solution.py:457
  50.2 7.9 %collective-permute-start.16 = (bf16[2,96,256]{2,1,0:T(8,128)(2,1)S(1)}, bf16[2,96,256]{2,1,0:T(8,128)(2,1)S(1)}, u32[]{:S(2)}, u32[]{:S(2)}) collective-permute-start(bf16[2,96,256]{2,1,0:T(8,128)(2,1)S(1)} %get-tuple-element.99), channel_id=1, source_target_pairs={{0,4},{2,6},{4,0},{6,2},{8,12},{10,14},{12,8},{14,10},{1,5},{3,7},... | collective-permute-start | bytes 294920 | tf_op jit(solution)/shard_map/ppermute | solution.py:457
  51.5 9.3 %collective-permute-start.17 = (bf16[2,96,256]{2,1,0:T(8,128)(2,1)S(1)}, bf16[2,96,256]{2,1,0:T(8,128)(2,1)S(1)}, u32[]{:S(2)}, u32[]{:S(2)}) collective-permute-start(bf16[2,96,256]{2,1,0:T(8,128)(2,1)S(1)} %get-tuple-element.100), channel_id=1, source_target_pairs={{0,6},{2,4},{4,2},{6,0},{8,14},{10,12},{12,10},{14,8},{1,7},{3,5},... | collective-permute-start | bytes 294920 | tf_op jit(solution)/shard_map/ppermute | solution.py:457
  53.1 14.8 %collective-permute-start.18 = (bf16[2,96,256]{2,1,0:T(8,128)(2,1)S(1)}, bf16[2,96,256]{2,1,0:T(8,128)(2,1)S(1)}, u32[]{:S(2)}, u32[]{:S(2)}) collective-permute-start(bf16[2,96,256]{2,1,0:T(8,128)(2,1)S(1)} %get-tuple-element.101), channel_id=1, source_target_pairs={{0,8},{2,10},{4,12},{6,14},{8,0},{10,2},{12,4},{14,6},{1,9},{3,11}... | collective-permute-start | bytes 294920 | tf_op jit(solution)/shard_map/ppermute | solution.py:457
  55.0 14.8 %collective-permute-start.19 = (bf16[2,96,256]{2,1,0:T(8,128)(2,1)S(1)}, bf16[2,96,256]{2,1,0:T(8,128)(2,1)S(1)}, u32[]{:S(2)}, u32[]{:S(2)}) collective-permute-start(bf16[2,96,256]{2,1,0:T(8,128)(2,1)S(1)} %get-tuple-element.102), channel_id=1, source_target_pairs={{0,10},{2,8},{4,14},{6,12},{8,2},{10,0},{12,6},{14,4},{1,11},{3,9}... | collective-permute-start | bytes 294920 | tf_op jit(solution)/shard_map/ppermute | solution.py:457
  56.0 13.8 %collective-permute-start.20 = (bf16[2,96,256]{2,1,0:T(8,128)(2,1)S(1)}, bf16[2,96,256]{2,1,0:T(8,128)(2,1)S(1)}, u32[]{:S(2)}, u32[]{:S(2)}) collective-permute-start(bf16[2,96,256]{2,1,0:T(8,128)(2,1)S(1)} %get-tuple-element.103), channel_id=1, source_target_pairs={{0,12},{2,14},{4,8},{6,10},{8,4},{10,6},{12,0},{14,2},{1,13},{3,15... | collective-permute-start | bytes 294920 | tf_op jit(solution)/shard_map/ppermute | solution.py:457
  58.1 11.7 %collective-permute-start.21 = (bf16[2,96,256]{2,1,0:T(8,128)(2,1)S(1)}, bf16[2,96,256]{2,1,0:T(8,128)(2,1)S(1)}, u32[]{:S(2)}, u32[]{:S(2)}) collective-permute-start(bf16[2,96,256]{2,1,0:T(8,128)(2,1)S(1)} %get-tuple-element.104), channel_id=1, source_target_pairs={{0,14},{2,12},{4,10},{6,8},{8,6},{10,4},{12,2},{14,0},{1,15},{3,13... | collective-permute-start | bytes 294920 | tf_op jit(solution)/shard_map/ppermute | solution.py:457

commit v3 on v2

--- a/solution.py
+++ b/solution.py
@@ -175,9 +175,9 @@
         held[owner] = slot + 1
 
 
-def forward_kernel(count_col, half, owners_far, ranks_far, focus, factors, *refs):
+def forward_kernel(count_col, half, owners_far, focus, factors, *refs):
     outs = refs[: 2 * count_col]
-    focus_here, factors_here, sums, owners, ranks, tile_of, held, sems = refs[2 * count_col :]
+    focus_here, factors_here, sums, owners, tile_of, held, sems = refs[2 * count_col :]
     column = lax.axis_index("col")
     mine = lax.axis_index("freq")
     two, vis, sources = focus_here.shape
@@ -193,14 +193,9 @@
         )
         for copy in copies[j]:
             copy.start()
-    small = [
-        pltpu.make_async_copy(owners_far, owners, sems.at[2, 0]),
-        pltpu.make_async_copy(ranks_far, ranks, sems.at[2, 1]),
-    ]
-    for copy in small:
-        copy.start()
-    for copy in small:
-        copy.wait()
+    owners_copy = pltpu.make_async_copy(owners_far, owners, sems.at[2, 0])
+    owners_copy.start()
+    owners_copy.wait()
     capacity = 2 * half
     list_tiles(owners, tile_of, held, count_col, capacity)
     for j in range(blocks):
@@ -212,20 +207,16 @@
         by_imag = dot(factors_here[1, :, at], low, 1, 1)
         sums[j, :, :vis] = by_real[:, :vis] - by_imag[:, vis:]
         sums[j, :, vis:] = by_real[:, vis:] + by_imag[:, :vis]
-    row_id = lax.broadcasted_iota(jnp.int32, (R, 2 * vis), 0)
     for d in range(count_col):
         for e in range(2):
             for s in range(half):
                 tile = tile_of[(column ^ d) * capacity + (mine ^ e) * half + s]
-                pieces = []
-                for j in range(blocks):
-                    rank = ranks[tile, column * blocks + j]
-                    piece = sums[j, pl.ds(pl.multiple_of(tile * R, 8), R), :]
-                    pieces.append(jnp.where(row_id < rank, piece, 0.0))
+                at = pl.ds(pl.multiple_of(tile * R, 8), R)
+                pieces = [sums[j, at, :] for j in range(blocks)]
                 outs[2 * d + e][s] = jnp.concatenate(pieces, axis=0).astype(jnp.bfloat16)
 
 
-def forward_products(count_col, half, focusing, v_factors, tile_ranks, owners):
+def forward_products(count_col, half, focusing, v_factors, owners):
     vis, sources = focusing.shape[2:]
     rows = v_factors.shape[2]
     blocks = sources // TS
@@ -234,7 +225,7 @@
     anywhere = pl.BlockSpec(memory_space=pl.ANY)
     return pl.pallas_call(
         functools.partial(forward_kernel, count_col, half),
-        in_specs=[anywhere] * 4,
+        in_specs=[anywhere] * 3,
         out_specs=[vmem] * (2 * count_col + 2),
         out_shape=[out] * (2 * count_col)
         + [
@@ -244,7 +235,6 @@
         scratch_shapes=[
             pltpu.VMEM((blocks, rows, 2 * vis), jnp.float32),
             pltpu.SMEM(owners.shape, jnp.int32),
-            pltpu.SMEM(tile_ranks.shape, jnp.int32),
             pltpu.SMEM((count_col * 2 * half,), jnp.int32),
             pltpu.SMEM((count_col,), jnp.int32),
             pltpu.SemaphoreType.DMA((3, blocks)),
@@ -254,127 +244,167 @@
             flops=8 * rows * vis * sources, bytes_accessed=8 * vis * sources + 4 * rows * sources, transcendentals=0
         ),
         name="forward_products",
-    )(owners, tile_ranks, focusing, v_factors)
-
-
-def load_kernel(half, u_factors, u_here, sem):
-    start = lax.axis_index("freq") * half
-    copy = pltpu.make_async_copy(u_factors.at[0, :, pl.ds(start, half)], u_here, sem)
-    copy.start()
-    copy.wait()
-
-
-def load_factors(half, u_factors):
-    shape = (2, half) + u_factors.shape[3:]
-    return pl.pallas_call(
-        functools.partial(load_kernel, half),
-        in_specs=[pl.BlockSpec(memory_space=pl.ANY)],
-        out_specs=pl.BlockSpec(memory_space=pltpu.VMEM),
-        out_shape=jax.ShapeDtypeStruct(shape, jnp.bfloat16),
-        scratch_shapes=[pltpu.SemaphoreType.DMA],
-        compiler_params=pltpu.CompilerParams(vmem_limit_bytes=46 * 2**20),
-        cost_estimate=pl.CostEstimate(flops=0, bytes_accessed=2 * int(np.prod(shape)), transcendentals=0),
-        name="load_factors",
-    )(u_factors)
-
-
-def receiver_kernel(count_col, half, chunk, owners, ranks, onsets, table, *refs):
-    arrived = refs[: 2 * count_col]
-    u_own = refs[2 * count_col]
-    u_other = refs[2 * count_col + 1 : 2 * count_col + 5]
-    outs = refs[-2 * count_col - 7 : -7]
-    earlier = refs[2 * count_col + 5 : -2 * count_col - 7]
-    factors, coefs, field, windowed, tile_of, held, sems = refs[-7:]
+    )(owners, focusing, v_factors)
+
+
+def prepare_kernel(count_col, half, owners, ranks, onsets, table, u_factors, u_here, mixing, mask, tile_of, held, sem):
     column = lax.axis_index("col")
     mine = lax.axis_index("freq")
-    vis = field.shape[1]
-    rows = factors.shape[1]
+    copy = pltpu.make_async_copy(u_factors.at[0, :, pl.ds(mine * half, half)], u_here, sem)
+    copy.start()
+    list_tiles(owners, tile_of, held, count_col, 2 * half)
+    times = lax.broadcasted_iota(jnp.int32, (NT, TS), 0)
+    row_id = lax.broadcasted_iota(jnp.int32, (R, mask.shape[2]), 0)
+    for s in range(half):
+        tile = tile_of[column * 2 * half + mine * half + s]
+        inside = jnp.where(times < onsets[tile], 1.0, 0.0).astype(jnp.bfloat16)
+        tables = dot(table[mine], inside, 1, 0)
+        count = tables.shape[0] // 3
+        mixing[s] = tables[:count] + tables[count : 2 * count] + tables[2 * count :]
+        pieces = [jnp.where(row_id < ranks[tile, j], 1.0, 0.0) for j in range(mask.shape[1] // R)]
+        mask[s] = jnp.concatenate(pieces, axis=0).astype(jnp.bfloat16)
+    copy.wait()
+
+
+def prepare(count_col, half, columns, owners, tile_ranks, onsets, table, u_factors):
+    shape = (2, half) + u_factors.shape[3:]
+    vmem = pl.BlockSpec(memory_space=pltpu.VMEM)
+    return pl.pallas_call(
+        functools.partial(prepare_kernel, count_col, half),
+        in_specs=[pl.BlockSpec(memory_space=pltpu.SMEM)] * 2 + [vmem, vmem, pl.BlockSpec(memory_space=pl.ANY)],
+        out_specs=[vmem, vmem, vmem],
+        out_shape=[
+            jax.ShapeDtypeStruct(shape, jnp.bfloat16),
+            jax.ShapeDtypeStruct((half, table.shape[1] // 3, TS), jnp.float32),
+            jax.ShapeDtypeStruct((half, shape[2], columns), jnp.bfloat16),
+        ],
+        scratch_shapes=[
+            pltpu.SMEM((count_col * 2 * half,), jnp.int32),
+            pltpu.SMEM((count_col,), jnp.int32),
+            pltpu.SemaphoreType.DMA,
+        ],
+        compiler_params=pltpu.CompilerParams(vmem_limit_bytes=40 * 2**20),
+        cost_estimate=pl.CostEstimate(flops=0, bytes_accessed=4 * int(np.prod(shape)), transcendentals=0),
+        name="prepare",
+    )(owners, tile_ranks, onsets, table, u_factors)
+
+
+def stack_coefficients(column, arrived, vis, slot, mask, matrix):
+    strip = arrived[0].shape[1]
+    for d, ref in enumerate(arrived):
+        start = pl.multiple_of((column ^ d) * strip, strip)
+        values = ref[slot] * mask[slot, pl.ds(start, strip), :]
+        matrix[0, pl.ds(start, strip), :] = values
+        matrix[1, pl.ds(start, strip), :] = jnp.concatenate([-values[:, vis:], values[:, :vis]], axis=1)
+
+
+def own_field_kernel(count_col, half, mask, u_own, *refs):
+    arrived = refs[:count_col]
+    field, coefs = refs[count_col:]
+    column = lax.axis_index("col")
+    rows, columns = coefs.shape[2:]
+    for s in range(half):
+        stack_coefficients(column, arrived, columns // 2, s, mask, coefs.at[s])
+        factors = u_own[:, s].reshape(2 * rows, TS)
+        field[s] = dot(coefs[s].reshape(2 * rows, columns), factors, 0, 0).astype(jnp.bfloat16)
+
+
+def own_field(count_col, half, mask, u_own, arrived):
+    columns = arrived[0].shape[2]
+    rows = u_own.shape[2]
+    vmem = pl.BlockSpec(memory_space=pltpu.VMEM)
+    return pl.pallas_call(
+        functools.partial(own_field_kernel, count_col, half),
+        in_specs=[vmem] * (2 + count_col),
+        out_specs=vmem,
+        out_shape=jax.ShapeDtypeStruct((half, columns, TS), jnp.bfloat16),
+        scratch_shapes=[pltpu.VMEM((half, 2, rows, columns), jnp.bfloat16)],
+        compiler_params=pltpu.CompilerParams(vmem_limit_bytes=20 * 2**20),
+        cost_estimate=pl.CostEstimate(
+            flops=4 * half * rows * columns * TS, bytes_accessed=2 * half * rows * TS, transcendentals=0
+        ),
+        name="own_field",
+    )(mask, u_own, *arrived)
+
+
+def receiver_kernel(count_col, half, mask, mixing, own, u_own, *refs):
+    arrived = refs[:count_col]
+    u_other = refs[count_col : -2 * count_col - 5]
+    outs = refs[-2 * count_col - 5 : -5]
+    factors, coefs, field, windowed, sems = refs[-5:]
+    column = lax.axis_index("col")
     place = lax.axis_index("grp") * 2 + lax.axis_index("rep")
-    quarter = u_other[0].shape[1]
+    rows, columns = coefs.shape[2:]
+    vis = columns // 2
     copies = []
     for n, ref in enumerate(u_other):
-        start = pl.multiple_of((place ^ n) * quarter, quarter)
-        copies.append(
-            pltpu.make_async_copy(ref, factors.at[:, pl.ds(start, quarter), :], sems.at[n])
-        )
+        cuts = len(u_other) // 4
+        start = (place ^ (n // cuts)) * (rows // 4) + sum(ref.shape[2] for ref in u_other[: n % cuts])
+        at = pl.ds(pl.multiple_of(start, 16), ref.shape[2])
+        copies.append(pltpu.make_async_copy(ref, factors.at[:, :, at, :], sems.at[n]))
+        copies[n].start()
+    for s in range(half):
+        stack_coefficients(column, arrived, vis, s, mask, coefs.at[s])
     for copy in copies:
-        copy.start()
-    list_tiles(owners, tile_of, held, count_col, 2 * half)
-    tile = tile_of[column * 2 * half + mine * half + chunk]
+        copy.wait()
     strip = arrived[0].shape[1]
-    for d in range(count_col):
-        start = pl.multiple_of((column ^ d) * strip, strip)
+    for s in range(half):
+        matrix = factors[:, s].reshape(2 * rows, TS)
+        field[s] = dot(coefs[s].reshape(2 * rows, columns), matrix, 0, 0).astype(jnp.bfloat16)
+    for s in range(half):
+        high = 64
+        for lane in range(0, TS, 128):
+            at = pl.ds(lane, 128)
+            mix = mixing[s, :, at]
+            for row in range(0, vis, high):
+                inputs = []
+                for source in (own, field):
+                    for part in range(2):
+                        inputs.append(source[s, pl.ds(part * vis + row, high), at].astype(jnp.float32))
+                for p in range(4):
+                    total = mix[4 * p : 4 * p + 1] * inputs[0]
+                    for q in range(1, 4):
+                        total = total + mix[4 * p + q : 4 * p + q + 1] * inputs[q]
+                    windowed[s, p // 2, pl.ds((p % 2) * vis + row, high), at] = total.astype(jnp.bfloat16)
         for e in range(2):
-            values = arrived[2 * d + e][chunk]
-            coefs[e, 0, pl.ds(start, strip), :] = values
-            coefs[e, 1, pl.ds(start, strip), :] = jnp.concatenate([-values[:, vis:], values[:, :vis]], axis=1)
-    times = lax.broadcasted_iota(jnp.int32, (NT, TS), 0)
-    inside = jnp.where(times < onsets[tile], 1.0, 0.0).astype(jnp.bfloat16)
-    tables = dot(table[mine], inside, 1, 0)
-    count = tables.shape[0] // 3
-    mixing = tables[:count] + tables[count : 2 * count] + tables[2 * count :]
-    for e in range(2):
-        for copy in copies if e == 1 else []:
-            copy.wait()
-        matrix = (u_own[:, chunk] if e == 0 else factors[...]).reshape(2 * rows, TS)
-        product = dot(coefs[e].reshape(2 * rows, 2 * vis), matrix, 0, 0)
-        low = product.astype(jnp.bfloat16).astype(jnp.float32)
-        field[2 * e] = low[:vis]
-        field[2 * e + 1] = low[vis:]
-    for p in range(4):
-        total = mixing[4 * p : 4 * p + 1] * field[0]
-        for q in range(1, 4):
-            total = total + mixing[4 * p + q : 4 * p + q + 1] * field[q]
-        windowed[p // 2, (p % 2) * vis : (p % 2 + 1) * vis, :] = total.astype(jnp.bfloat16)
-    row_id = lax.broadcasted_iota(jnp.int32, (R, 2 * vis), 0)
-    for e in range(2):
-        matrix = (u_own[:, chunk] if e == 0 else factors[...]).reshape(2 * rows, TS)
-        back = dot(matrix, windowed[e], 1, 1)
-        by_real, by_imag = back[:rows], back[rows:]
-        adjoint = jnp.concatenate(
-            [by_real[:, :vis] + by_imag[:, vis:], by_real[:, vis:] - by_imag[:, :vis]], axis=1
-        )
-        pieces = []
-        for j in range(rows // R):
-            pieces.append(jnp.where(row_id < ranks[tile, j], adjoint[j * R : (j + 1) * R], 0.0))
-        coefs[e, 0] = jnp.concatenate(pieces, axis=0).astype(jnp.bfloat16)
-        for d in range(count_col):
-            start = pl.multiple_of((column ^ d) * strip, strip)
-            outs[2 * d + e][chunk] = coefs[e, 0, pl.ds(start, strip), :]
-            for s in range(chunk):
-                outs[2 * d + e][s] = earlier[2 * d + e][s]
-
-
-def receiver_products(count_col, half, chunk, owners, tile_ranks, onsets, table, arrived, u_factors, u_other, earlier):
+            if e == 0:
+                matrix = u_own[:, s].reshape(2 * rows, TS)
+            back = dot(matrix, windowed[s, e], 1, 1)
+            by_real, by_imag = back[:rows], back[rows:]
+            adjoint = jnp.concatenate(
+                [by_real[:, :vis] + by_imag[:, vis:], by_real[:, vis:] - by_imag[:, :vis]], axis=1
+            )
+            coefs[s, 0] = adjoint.astype(jnp.bfloat16) * mask[s]
+            for d in range(count_col):
+                start = pl.multiple_of((column ^ d) * strip, strip)
+                outs[2 * d + e][s] = coefs[s, 0, pl.ds(start, strip), :]
+            if e == 0:
+                matrix = factors[:, s].reshape(2 * rows, TS)
+
+
+def receiver_products(count_col, half, mask, mixing, own, arrived, u_own, u_other):
     strip, columns = arrived[0].shape[1:]
-    rows = u_factors.shape[2]
-    vis = columns // 2
-    smem = pl.BlockSpec(memory_space=pltpu.SMEM)
+    rows = u_own.shape[2]
     vmem = pl.BlockSpec(memory_space=pltpu.VMEM)
-    out = jax.ShapeDtypeStruct((chunk + 1, strip, columns), jnp.bfloat16)
+    out = jax.ShapeDtypeStruct((half, strip, columns), jnp.bfloat16)
     return pl.pallas_call(
-        functools.partial(receiver_kernel, count_col, half, chunk),
-        in_specs=[smem, smem, vmem, vmem]
-        + [vmem] * (2 * count_col)
-        + [vmem] * 5
-        + [vmem] * len(earlier),
+        functools.partial(receiver_kernel, count_col, half),
+        in_specs=[vmem] * (4 + count_col + len(u_other)),
         out_specs=[vmem] * (2 * count_col),
         out_shape=[out] * (2 * count_col),
         scratch_shapes=[
-            pltpu.VMEM((2, rows, TS), jnp.bfloat16),
-            pltpu.VMEM((2, 2, rows, columns), jnp.bfloat16),
-            pltpu.VMEM((4, vis, TS), jnp.float32),
-            pltpu.VMEM((2, columns, TS), jnp.bfloat16),
-            pltpu.SMEM((count_col * 2 * half,), jnp.int32),
-            pltpu.SMEM((count_col,), jnp.int32),
-            pltpu.SemaphoreType.DMA((4,)),
+            pltpu.VMEM((2, half, rows, TS), jnp.bfloat16),
+            pltpu.VMEM((half, 2, rows, columns), jnp.bfloat16),
+            pltpu.VMEM((half, columns, TS), jnp.bfloat16),
+            pltpu.VMEM((half, 2, columns, TS), jnp.bfloat16),
+            pltpu.SemaphoreType.DMA((len(u_other),)),
         ],
         compiler_params=pltpu.CompilerParams(vmem_limit_bytes=24 * 2**20),
         cost_estimate=pl.CostEstimate(
-            flops=32 * rows * vis * TS, bytes_accessed=8 * rows * TS, transcendentals=0
+            flops=12 * half * rows * columns * TS, bytes_accessed=8 * half * rows * TS, transcendentals=0
         ),
         name="receiver_products",
-    )(owners, tile_ranks, onsets, table, *arrived, u_factors, *u_other, *earlier)
+    )(mask, mixing, own, u_own, *arrived, *u_other)
 
 
 def update_kernel(count_col, half, owners, *refs):
@@ -469,43 +499,39 @@
     place = lax.axis_index("grp") * 2 + lax.axis_index("rep")
     table = jnp.asarray(mixing_table(2))
     tile_onsets = onsets.reshape(NR // TS, 1, TS)
+    quarter = rows // 4
+    cuts = (quarter // 2, quarter - quarter // 2)
     first = []
-    for s in range(half):
-        piece = lax.dynamic_slice(
-            u_factors, (0, 0, (1 - mine) * half + s, place * (rows // 4), 0), (1, 2, 1, rows // 4, TS)
-        ).reshape(2, rows // 4, TS)
-        first.append(swap(piece, "freq"))
-    *outgoing, focus_here, v_here = forward_products(count_col, half, focusing, v_factors, tile_ranks, owners)
+    share = lax.dynamic_slice(
+        u_factors, (0, 0, (1 - mine) * half, place * quarter, 0), (1, 2, half, quarter, TS)
+    ).reshape(2, half, quarter, TS)
+    first = [swap(share[:, :, : cuts[0]], "freq"), swap(share[:, :, cuts[0] :], "freq")]
+    *outgoing, focus_here, v_here = forward_products(count_col, half, focusing, v_factors, owners)
     def move(offset, payload):
         return lax.ppermute(payload, ("col", "freq"), [(i, i ^ offset) for i in range(2 * count_col)])
     arrived = list(outgoing)
     far, _ = lax.optimization_barrier((u_factors, outgoing[0]))
-    u_here = load_factors(half, far)
-    second = []
-    if 2 == 2:
-        first[0], _ = lax.optimization_barrier((first[0], outgoing[0]))
-        second.append(swap(first[0], "grp"))
+    u_here, mixing, mask = prepare(
+        count_col, half, outgoing[0].shape[2], owners, tile_ranks, tile_onsets, table, far
+    )
+    first[0], _ = lax.optimization_barrier((first[0], outgoing[0]))
+    second = [swap(first[0], "grp")]
     for offset in (6, 4, 2):
         arrived[offset] = move(offset, arrived[offset])
-    held = lax.optimization_barrier(tuple(arrived + first + [u_here] + second))
-    if 2 == 2:
-        second = [held[-1]]
-        held = held[:-1]
-    arrived, first, u_here = list(held[: 2 * count_col]), list(held[2 * count_col : -1]), held[-1]
-    if 2 == 3:
-        second.append(swap(first[0], "grp"))
-    second.append(swap(first[1], "grp"))
+    held = lax.optimization_barrier(tuple(arrived + first + [u_here, mixing] + second))
+    arrived, (*first, u_here, mixing, head) = list(held[: 2 * count_col]), held[2 * count_col :]
+    second = [head, swap(first[1], "grp")]
     for offset in (7, 5, 3, 1):
         arrived[offset] = move(offset, arrived[offset])
-    held = lax.optimization_barrier(tuple(arrived + first + second[:1]))
-    arrived = list(held[:-3])
-    first, second = list(held[-3:-1]), [held[-1], second[1]]
-    back = []
-    for s in range(half):
-        gathered = [first[s], swap(first[s], "rep"), second[s], swap(second[s], "rep")]
-        back = receiver_products(
-            count_col, half, s, owners, tile_ranks, tile_onsets, table, arrived, u_here, gathered, back
-        )
+    held = lax.optimization_barrier(tuple(arrived + first + second + [u_here]))
+    arrived, (*pieces, u_here) = list(held[: 2 * count_col]), held[2 * count_col :]
+    first, second = pieces[: len(cuts)], pieces[len(cuts) :]
+    own = own_field(count_col, half, mask, u_here, arrived[::2])
+    gathered = []
+    for group in (first, second):
+        gathered.extend(group)
+        gathered.extend([swap(piece, "rep") for piece in group])
+    back = receiver_products(count_col, half, mask, mixing, own, arrived[1::2], u_here, gathered)
     returned = exchange(back, count_col)
     return update_products(count_col, half, owners, returned, focus_here, v_here)
 

time: 74.5 us -> 71.6 us (0.961)
  Pallas kernels: 20.4 us -> 17.3 us
  waiting for transfers between devices: 21.1 us -> 22 us
    pallas_call x3, Pallas kernels: 9.44 us -> 6.39 us  [the longest x1 3.78 us: receiver_products(): pl.pallas_call(functools.partial(receiver_kernel, count_col, half), in_sp...]
  transfers between devices with their start and end apart: 22 -> 22, of which waited for: 10 -> 11; matrix products, arithmetic and copies ran while one was open for 0% -> 0% of each run, Pallas kernels for 18% -> 14%
where the time goes in v3:
time: 71.6 us; the launch traced here: 70.6 us
  starting transfers between devices  29 us (41%)
  waiting for transfers between devices  22 us (31%)
  Pallas kernels  17.3 us (24%)
  local copies, waits for them, and re-layouts  2.06 us (3%)
    ppermute x7, starting transfers between devices, exchange(): lax.ppermute(arrays[offset], ('col', 'freq'), [(i, i ^ offset) for i in r...  11.2 us
    ppermute x7, starting transfers between devices, move(): lax.ppermute(payload, ('col', 'freq'), [(i, i ^ offset) for i in range(2...  11.1 us
    ppermute x7, waiting for transfers between devices, move(): lax.ppermute(payload, ('col', 'freq'), [(i, i ^ offset) for i in range(2...  9.92 us
    ppermute x7, waiting for transfers between devices, exchange(): lax.ppermute(arrays[offset], ('col', 'freq'), [(i, i ^ offset) for i in r...  9.26 us
    pallas_call x1, Pallas kernels, forward_products(): pl.pallas_call(functools.partial(forward_kernel, count_col, half), in_spe...  7.49 us
    ppermute x8, starting transfers between devices, swap(): return lax.ppermute(array, axis, [(0, 1), (1, 0)])  6.71 us
    pallas_call x1, Pallas kernels, receiver_products(): pl.pallas_call(functools.partial(receiver_kernel, count_col, half), in_sp...  3.78 us
    pallas_call x1, Pallas kernels, update_products(): pl.pallas_call(functools.partial(update_kernel, count_col, half), in_spec...  3.46 us
  transfers between devices with their start and end apart: 22, of which 11 were waited for; matrix products, arithmetic and copies ran while one was open for 0% of the time, Pallas kernels for 14%

profile of v3, /device:TPU:0, one launch (start us, length us, event | category | flops | bytes accessed | tf_op | source)
XLA Modules:
  0.0 70.6 jit_solution(830683640305189446)
XLA Ops:
  0.0 1.2 %dynamic-slice_bitcast_fusion = bf16[2,2,96,1024]{3,2,1,0:T(8,128)(2,1)S(1)} fusion(bf16[1,2,4,384,1024]{4,3,2,1,0:T(8,128)(2,1)} %u_factors, s32[]{:T(128)S(6)} %select_n.6, s32[]{:T(128)S(6)} %select_n.7), kind=kLoop, calls=%fused_computation | loop fusion | bytes 1572872 | tf_op jit(solution)/shard_map/reshape | solution.py:507
  1.2 0.0 slice-start
  1.2 0.0 copy-start
  1.2 0.0 copy-start.1
  1.2 0.0 copy-start.2
  1.2 0.1 fusion
  1.3 3.0 %collective-permute-start.3 = (bf16[2,2,48,1024]{3,2,1,0:T(8,128)(2,1)S(1)}, bf16[2,2,48,1024]{3,2,1,0:T(8,128)(2,1)S(1)}, u32[]{:S(2)}, u32[]{:S(2)}) collective-permute-start(bf16[2,2,48,1024]{3,2,1,0:T(8,128)(2,1)S(1)} %get-tuple-element.104), channel_id=1, source_target_pairs={{0,2},{2,0},{1,3},{3,1},{4,6},{6,4},{5,7},{7,5},{8,10},{10,8},{9,1... | collective-permute-start | bytes 1179656 | tf_op jit(solution)/shard_map/ppermute | solution.py:478
  4.3 0.1 collective-permute-start.4
  4.4 0.8 %copy-done.3 = s32[16]{0:T(128)S(1)} copy-done((s32[16]{0:T(128)S(1)}, s32[16]{0:T(128)}, u32[]{:S(2)}) %copy-start.3) | copy-done | bytes 88
  5.2 7.5 %forward_products.1 = (bf16[2,96,256]{2,1,0:T(8,128)(2,1)S(1)}, bf16[2,96,256]{2,1,0:T(8,128)(2,1)S(1)}, bf16[2,96,256]{2,1,0:T(8,128)(2,1)S(1)}, bf16[2,96,256]...) custom-call(s32[16]{0:T(128)S(1)} %copy-done.3, ...), custom_call_target="tpu_custom_call" | custom-call | flops 1610612736 | bytes 10485760 | tf_op jit(solution)/shard_map/forward_products/pallas_call | solution.py:226
  12.7 1.6 %collective-permute-done.3.refs_4_ = bf16[2,2,48,1024]{3,2,1,0:T(8,128)(2,1)S(1)} collective-permute-done((bf16[2,2,48,1024]{3,2,1,0:T(8,128)(2,1)S(1)}, bf16[2,2,48,1024]{3,2,1,0:T(8,128)(2,1)S(1)}, u32[]{:S(2)}, u32[]{:S(2)}) %collective-permute-start.3) | collective-permute-done | bytes 393248 | tf_op jit(solution)/shard_map/ppermute | solution.py:478
  14.2 2.1 %collective-permute-start.5 = (bf16[2,2,48,1024]{3,2,1,0:T(8,128)(2,1)S(1)}, bf16[2,2,48,1024]{3,2,1,0:T(8,128)(2,1)S(1)}, u32[]{:S(2)}, u32[]{:S(2)}) collective-permute-start(bf16[2,2,48,1024]{3,2,1,0:T(8,128)(2,1)S(1)} %collective-permute-done.3.refs_4_), channel_id=1, source_target_pairs={{0,16},{16,0},{1,17},{17,1},{2,18},{18,2},{3,19},{19,3},{4,20},{20... | collective-permute-start | bytes 1179656 | tf_op jit(solution)/shard_map/ppermute | solution.py:478
  16.3 1.6 %collective-permute-start = (bf16[2,96,256]{2,1,0:T(8,128)(2,1)S(1)}, bf16[2,96,256]{2,1,0:T(8,128)(2,1)S(1)}, u32[]{:S(2)}, u32[]{:S(2)}) collective-permute-start(bf16[2,96,256]{2,1,0:T(8,128)(2,1)S(1)} %get-tuple-element.58), channel_id=1, source_target_pairs={{0,4},{2,6},{4,0},{6,2},{8,12},{10,14},{12,8},{14,10},{1,5},{3,7},... | collective-permute-start | bytes 294920 | tf_op jit(solution)/shard_map/ppermute | solution.py:511
  17.9 2.6 %collective-permute-start.1 = (bf16[2,96,256]{2,1,0:T(8,128)(2,1)S(1)}, bf16[2,96,256]{2,1,0:T(8,128)(2,1)S(1)}, u32[]{:S(2)}, u32[]{:S(2)}) collective-permute-start(bf16[2,96,256]{2,1,0:T(8,128)(2,1)S(1)} %get-tuple-element.60), channel_id=1, source_target_pairs={{0,8},{2,10},{4,12},{6,14},{8,0},{10,2},{12,4},{14,6},{1,9},{3,11}... | collective-permute-start | bytes 294920 | tf_op jit(solution)/shard_map/ppermute | solution.py:511
  20.5 0.2 collective-permute-start.2
  20.7 0.0 slice-done
  20.7 0.0 copy-done
  20.7 0.0 copy-done.1
  20.7 0.0 copy-done.2
  20.7 0.0 slice-done.1
  20.8 1.5 %prepare.1 = (bf16[2,2,384,1024]{3,2,1,0:T(8,128)(2,1)S(1)}, f32[2,16,1024]{2,1,0:T(8,128)S(1)}, bf16[2,384,256]{2,1,0:T(8,128)(2,1)S(1)}) custom-call(s32[16]{0:T(128)S(1)} %copy-done.3, s32[16,16]{1,0:T(8,128)S(1)} %copy-done.2, s32[16,1,1024]{2,1,0:T(1,128)S(1)} %bitcast.7, bf16[2,48,512]{2,1,0:T(8,128)(2,1)S(1)} %copy-done, ...), custom_call_target="tpu_custom_call" | custom-call | bytes 6291456 | tf_op jit(solution)/shard_map/prepare/pallas_call | solution.py:272
  22.3 0.0 collective-permute-done.refs_1_
  22.3 3.0 %collective-permute-done.1.refs_2_ = bf16[2,96,256]{2,1,0:T(8,128)(2,1)S(1)} collective-permute-done((bf16[2,96,256]{2,1,0:T(8,128)(2,1)S(1)}, bf16[2,96,256]{2,1,0:T(8,128)(2,1)S(1)}, u32[]{:S(2)}, u32[]{:S(2)}) %collective-permute-start.1) | collective-permute-done | bytes 98336 | tf_op jit(solution)/shard_map/ppermute | solution.py:511
  25.3 1.8 %collective-permute-done.2.refs_3_ = bf16[2,96,256]{2,1,0:T(8,128)(2,1)S(1)} collective-permute-done((bf16[2,96,256]{2,1,0:T(8,128)(2,1)S(1)}, bf16[2,96,256]{2,1,0:T(8,128)(2,1)S(1)}, u32[]{:S(2)}, u32[]{:S(2)}) %collective-permute-start.2) | collective-permute-done | bytes 98336 | tf_op jit(solution)/shard_map/ppermute | solution.py:511
  27.0 0.0 collective-permute-done.4.refs_5_
  27.0 0.0 collective-permute-done.5.refs_8_
  27.0 0.5 collective-permute-start.10
  27.5 1.5 %collective-permute-start.6 = (bf16[2,96,256]{2,1,0:T(8,128)(2,1)S(1)}, bf16[2,96,256]{2,1,0:T(8,128)(2,1)S(1)}, u32[]{:S(2)}, u32[]{:S(2)}) collective-permute-start(bf16[2,96,256]{2,1,0:T(8,128)(2,1)S(1)} %get-tuple-element.69), channel_id=1, source_target_pairs={{0,2},{2,0},{4,6},{6,4},{8,10},{10,8},{12,14},{14,12},{1,3},{3,1},... | collective-permute-start | bytes 294920 | tf_op jit(solution)/shard_map/ppermute | solution.py:511
  29.0 0.9 %collective-permute-start.7 = (bf16[2,96,256]{2,1,0:T(8,128)(2,1)S(1)}, bf16[2,96,256]{2,1,0:T(8,128)(2,1)S(1)}, u32[]{:S(2)}, u32[]{:S(2)}) collective-permute-start(bf16[2,96,256]{2,1,0:T(8,128)(2,1)S(1)} %get-tuple-element.71), channel_id=1, source_target_pairs={{0,6},{2,4},{4,2},{6,0},{8,14},{10,12},{12,10},{14,8},{1,7},{3,5},... | collective-permute-start | bytes 294920 | tf_op jit(solution)/shard_map/ppermute | solution.py:511
  29.9 2.1 %collective-permute-start.8 = (bf16[2,96,256]{2,1,0:T(8,128)(2,1)S(1)}, bf16[2,96,256]{2,1,0:T(8,128)(2,1)S(1)}, u32[]{:S(2)}, u32[]{:S(2)}) collective-permute-start(bf16[2,96,256]{2,1,0:T(8,128)(2,1)S(1)} %get-tuple-element.73), channel_id=1, source_target_pairs={{0,10},{2,8},{4,14},{6,12},{8,2},{10,0},{12,6},{14,4},{1,11},{3,9}... | collective-permute-start | bytes 294920 | tf_op jit(solution)/shard_map/ppermute | solution.py:511
  32.0 2.2 %collective-permute-start.9 = (bf16[2,96,256]{2,1,0:T(8,128)(2,1)S(1)}, bf16[2,96,256]{2,1,0:T(8,128)(2,1)S(1)}, u32[]{:S(2)}, u32[]{:S(2)}) collective-permute-start(bf16[2,96,256]{2,1,0:T(8,128)(2,1)S(1)} %get-tuple-element.75), channel_id=1, source_target_pairs={{0,14},{2,12},{4,10},{6,8},{8,6},{10,4},{12,2},{14,0},{1,15},{3,13... | collective-permute-start | bytes 294920 | tf_op jit(solution)/shard_map/ppermute | solution.py:511
  34.3 0.0 collective-permute-done.6.refs_0_
  34.3 1.8 %collective-permute-done.7.refs_1_ = bf16[2,96,256]{2,1,0:T(8,128)(2,1)S(1)} collective-permute-done((bf16[2,96,256]{2,1,0:T(8,128)(2,1)S(1)}, bf16[2,96,256]{2,1,0:T(8,128)(2,1)S(1)}, u32[]{:S(2)}, u32[]{:S(2)}) %collective-permute-start.7) | collective-permute-done | bytes 98336 | tf_op jit(solution)/shard_map/ppermute | solution.py:511
  36.1 1.3 %collective-permute-done.8.refs_2_ = bf16[2,96,256]{2,1,0:T(8,128)(2,1)S(1)} collective-permute-done((bf16[2,96,256]{2,1,0:T(8,128)(2,1)S(1)}, bf16[2,96,256]{2,1,0:T(8,128)(2,1)S(1)}, u32[]{:S(2)}, u32[]{:S(2)}) %collective-permute-start.8) | collective-permute-done | bytes 98336 | tf_op jit(solution)/shard_map/ppermute | solution.py:511
  37.4 2.1 %collective-permute-done.9.refs_3_ = bf16[2,96,256]{2,1,0:T(8,128)(2,1)S(1)} collective-permute-done((bf16[2,96,256]{2,1,0:T(8,128)(2,1)S(1)}, bf16[2,96,256]{2,1,0:T(8,128)(2,1)S(1)}, u32[]{:S(2)}, u32[]{:S(2)}) %collective-permute-start.9) | collective-permute-done | bytes 98336 | tf_op jit(solution)/shard_map/ppermute | solution.py:511
  39.5 0.0 collective-permute-done.10.refs_9_
  39.5 0.0 collective-permute-start.11
  39.5 0.5 collective-permute-start.12
  40.0 0.0 collective-permute-start.13
  40.0 0.5 collective-permute-start.14
  40.5 1.1 %own_field.1.own = bf16[2,256,1024]{2,1,0:T(8,128)(2,1)S(1)} custom-call(bf16[2,384,256]{2,1,0:T(8,128)(2,1)S(1)} %get-tuple-element.56.mask, bf16[2,2,384,1024]{3,2,1,0:T(8,128)(2,1)S(1)} %get-tuple-element.80.u_own, bf16[2,96,256]{2,1,0:T(8,128)(2,1)S(1)} %get-tuple-element.81.refs_0_, bf16[2,96,256]{2,1,0:T(8,128)(2,1)S(1)} %collective-permute-done.refs_1_, ...), custom_call_target="tpu_custom_call" | custom-call | flops 805306368 | bytes 1572864 | tf_op jit(solution)/shard_map/own_field/pallas_call | solution.py:316
  41.6 0.0 slice-start.3
  41.6 0.0 collective-permute-done.11.refs_6_
  41.6 0.1 collective-permute-done.12.refs_7_
  41.8 0.6 collective-permute-done.13.refs_10_
  42.3 0.6 collective-permute-done.14.refs_11_
  42.9 3.8 %receiver_products.1 = (bf16[2,96,256]{2,1,0:T(8,128)(2,1)S(1)}, bf16[2,96,256]{2,1,0:T(8,128)(2,1)S(1)}, bf16[2,96,256]{2,1,0:T(8,128)(2,1)S(1)}, bf16[2,96,256...) custom-call(bf16[2,384,256]{2,1,0:T(8,128)(2,1)S(1)} %get-tuple-elem, ...), custom_call_target="tpu_custom_call" | custom-call | flops 2415919104 | bytes 6291456 | tf_op jit(solution)/shard_map/receiver_products/pallas_call | solution.py:390
  46.7 0.5 collective-permute-start.15
  47.2 1.6 %collective-permute-start.16 = (bf16[2,96,256]{2,1,0:T(8,128)(2,1)S(1)}, bf16[2,96,256]{2,1,0:T(8,128)(2,1)S(1)}, u32[]{:S(2)}, u32[]{:S(2)}) collective-permute-start(bf16[2,96,256]{2,1,0:T(8,128)(2,1)S(1)} %get-tuple-element.95), channel_id=1, source_target_pairs={{0,4},{2,6},{4,0},{6,2},{8,12},{10,14},{12,8},{14,10},{1,5},{3,7},... | collective-permute-start | bytes 294920 | tf_op jit(solution)/shard_map/ppermute | solution.py:487
  48.8 1.4 %collective-permute-start.17 = (bf16[2,96,256]{2,1,0:T(8,128)(2,1)S(1)}, bf16[2,96,256]{2,1,0:T(8,128)(2,1)S(1)}, u32[]{:S(2)}, u32[]{:S(2)}) collective-permute-start(bf16[2,96,256]{2,1,0:T(8,128)(2,1)S(1)} %get-tuple-element.96), channel_id=1, source_target_pairs={{0,6},{2,4},{4,2},{6,0},{8,14},{10,12},{12,10},{14,8},{1,7},{3,5},... | collective-permute-start | bytes 294920 | tf_op jit(solution)/shard_map/ppermute | solution.py:487
  50.2 0.8 %collective-permute-start.18 = (bf16[2,96,256]{2,1,0:T(8,128)(2,1)S(1)}, bf16[2,96,256]{2,1,0:T(8,128)(2,1)S(1)}, u32[]{:S(2)}, u32[]{:S(2)}) collective-permute-start(bf16[2,96,256]{2,1,0:T(8,128)(2,1)S(1)} %get-tuple-element.97), channel_id=1, source_target_pairs={{0,8},{2,10},{4,12},{6,14},{8,0},{10,2},{12,4},{14,6},{1,9},{3,11}... | collective-permute-start | bytes 294920 | tf_op jit(solution)/shard_map/ppermute | solution.py:487
  51.0 2.0 %collective-permute-start.19 = (bf16[2,96,256]{2,1,0:T(8,128)(2,1)S(1)}, bf16[2,96,256]{2,1,0:T(8,128)(2,1)S(1)}, u32[]{:S(2)}, u32[]{:S(2)}) collective-permute-start(bf16[2,96,256]{2,1,0:T(8,128)(2,1)S(1)} %get-tuple-element.98), channel_id=1, source_target_pairs={{0,10},{2,8},{4,14},{6,12},{8,2},{10,0},{12,6},{14,4},{1,11},{3,9}... | collective-permute-start | bytes 294920 | tf_op jit(solution)/shard_map/ppermute | solution.py:487
  53.0 0.0 collective-permute-done.15.refs_1_
  53.0 2.4 %collective-permute-start.20 = (bf16[2,96,256]{2,1,0:T(8,128)(2,1)S(1)}, bf16[2,96,256]{2,1,0:T(8,128)(2,1)S(1)}, u32[]{:S(2)}, u32[]{:S(2)}) collective-permute-start(bf16[2,96,256]{2,1,0:T(8,128)(2,1)S(1)} %get-tuple-element.99), channel_id=1, source_target_pairs={{0,12},{2,14},{4,8},{6,10},{8,4},{10,6},{12,0},{14,2},{1,13},{3,15... | collective-permute-start | bytes 294920 | tf_op jit(solution)/shard_map/ppermute | solution.py:487
  55.4 0.0 collective-permute-done.16.refs_2_
  55.4 2.5 %collective-permute-start.21 = (bf16[2,96,256]{2,1,0:T(8,128)(2,1)S(1)}, bf16[2,96,256]{2,1,0:T(8,128)(2,1)S(1)}, u32[]{:S(2)}, u32[]{:S(2)}) collective-permute-start(bf16[2,96,256]{2,1,0:T(8,128)(2,1)S(1)} %get-tuple-element.100), channel_id=1, source_target_pairs={{0,14},{2,12},{4,10},{6,8},{8,6},{10,4},{12,2},{14,0},{1,15},{3,13... | collective-permute-start | bytes 294920 | tf_op jit(solution)/shard_map/ppermute | solution.py:487
  57.9 0.0 collective-permute-done.17.refs_3_
  57.9 7.2 %collective-permute-done.18.refs_4_ = bf16[2,96,256]{2,1,0:T(8,128)(2,1)S(1)} collective-permute-done((bf16[2,96,256]{2,1,0:T(8,128)(2,1)S(1)}, bf16[2,96,256]{2,1,0:T(8,128)(2,1)S(1)}, u32[]{:S(2)}, u32[]{:S(2)}) %collective-permute-start.18) | collective-permute-done | bytes 98336 | tf_op jit(solution)/shard_map/ppermute | solution.py:487
  65.1 2.0 %collective-permute-done.19.refs_5_ = bf16[2,96,256]{2,1,0:T(8,128)(2,1)S(1)} collective-permute-done((bf16[2,96,256]{2,1,0:T(8,128)(2,1)S(1)}, bf16[2,96,256]{2,1,0:T(8,128)(2,1)S(1)}, u32[]{:S(2)}, u32[]{:S(2)}) %collective-permute-start.19) | collective-permute-done | bytes 98336 | tf_op jit(solution)/shard_map/ppermute | solution.py:487
  67.1 0.0 collective-permute-done.20.refs_6_
  67.1 0.0 collective-permute-done.21.refs_7_
  67.1 0.0 slice-done.2
  67.1 0.0 slice-done.3
  67.2 3.5 %update_products.1 = f32[1,2,128,4096]{3,2,1,0:T(8,128)} custom-call(s32[16]{0:T(128)S(1)} %copy-done.3, bf16[2,96,256]{2,1,0:T(8,128)(2,1)S(1)} %get-tuple-element.93.refs_0_, bf16[2,96,256]{2,1,0:T(8,128)(2,1)S(1)} %collective-permute-done.15.refs_1_, bf16[2,96,256]{2,1,0:T(8,128)(2,1)S(1)} %collective-permute-done.16.refs_2_, ...), custom_call_target="tpu_custom_call" | custom-call | flops 1610612736 | bytes 14680064 | tf_op jit(solution)/shard_map/update_products/pallas_call | solution.py:456
  (5 shorter events, 0.0 us)
Async XLA Ops:
  1.2 19.5 %slice-start = ((s8[6291456]{0:T(1024)(128)(4,1)}), s8[4194304]{0:T(1024)(128)(4,1)S(1)}, s32[]{:S(2)}) async-start(s8[6291456]{0:T(1024)(128)(4,1)} %bitcast.3), calls=%async_computation | async-start | bytes 8388608
  1.2 19.5 %copy-start = (bf16[2,48,512]{2,1,0:T(8,128)(2,1)S(1)}, bf16[2,48,512]{2,1,0:T(8,128)(2,1)}, u32[]{:S(2)}) copy-start(bf16[2,48,512]{2,1,0:T(8,128)(2,1)} %constant.24.clone.table) | copy-start | bytes 294916
  1.2 19.5 %copy-start.1 = (s32[16384]{0:T(1024)S(1)}, s32[16384]{0:T(1024)}, u32[]{:S(2)}) copy-start(s32[16384]{0:T(1024)} %param.12) | copy-start | bytes 196612
  1.2 19.5 %copy-start.2 = (s32[16,16]{1,0:T(8,128)S(1)}, s32[16,16]{1,0:T(8,128)}, u32[]{:S(2)}) copy-start(s32[16,16]{1,0:T(8,128)} %ranks.1) | copy-start | bytes 3076
  1.3 12.9 %collective-permute-start.3 = (bf16[2,2,48,1024]{3,2,1,0:T(8,128)(2,1)S(1)}, bf16[2,2,48,1024]{3,2,1,0:T(8,128)(2,1)S(1)}, u32[]{:S(2)}, u32[]{:S(2)}) collective-permute-start(bf16[2,2,48,1024]{3,2,1,0:T(8,128)(2,1)S(1)} %get-tuple-element.104), channel_id=1, source_target_pairs={{0,2},{2,0},{1,3},{3,1},{4,6},{6,4},{5,7},{7,5},{8,10},{10,8},{9,1... | collective-permute-start | bytes 1179656 | tf_op jit(solution)/shard_map/ppermute | solution.py:478
  4.3 16.4 %slice-start.1 = ((s8[6291456]{0:T(1024)(128)(4,1)}), s8[2097152]{0:T(1024)(128)(4,1)S(1)}, s32[]{:S(2)}) async-start(s8[6291456]{0:T(1024)(128)(4,1)} %bitcast.3), calls=%async_computation.1 | async-start | bytes 4194304
  4.3 22.7 %collective-permute-start.4 = (bf16[2,2,48,1024]{3,2,1,0:T(8,128)(2,1)S(1)}, bf16[2,2,48,1024]{3,2,1,0:T(8,128)(2,1)S(1)}, u32[]{:S(2)}, u32[]{:S(2)}) collective-permute-start(bf16[2,2,48,1024]{3,2,1,0:T(8,128)(2,1)S(1)} %get-tuple-element.103), channel_id=1, source_target_pairs={{0,2},{2,0},{1,3},{3,1},{4,6},{6,4},{5,7},{7,5},{8,10},{10,8},{9,1... | collective-permute-start | bytes 1179656 | tf_op jit(solution)/shard_map/ppermute | solution.py:478
  4.4 0.8 %copy-start.3 = (s32[16]{0:T(128)S(1)}, s32[16]{0:T(128)}, u32[]{:S(2)}) copy-start(s32[16]{0:T(128)} %owners.3) | copy-start | bytes 196
  14.2 12.8 %collective-permute-start.5 = (bf16[2,2,48,1024]{3,2,1,0:T(8,128)(2,1)S(1)}, bf16[2,2,48,1024]{3,2,1,0:T(8,128)(2,1)S(1)}, u32[]{:S(2)}, u32[]{:S(2)}) collective-permute-start(bf16[2,2,48,1024]{3,2,1,0:T(8,128)(2,1)S(1)} %collective-permute-done.3.refs_4_), channel_id=1, source_target_pairs={{0,16},{16,0},{1,17},{17,1},{2,18},{18,2},{3,19},{19,3},{4,20},{20... | collective-permute-start | bytes 1179656 | tf_op jit(solution)/shard_map/ppermute | solution.py:478
  16.3 5.9 %collective-permute-start = (bf16[2,96,256]{2,1,0:T(8,128)(2,1)S(1)}, bf16[2,96,256]{2,1,0:T(8,128)(2,1)S(1)}, u32[]{:S(2)}, u32[]{:S(2)}) collective-permute-start(bf16[2,96,256]{2,1,0:T(8,128)(2,1)S(1)} %get-tuple-element.58), channel_id=1, source_target_pairs={{0,4},{2,6},{4,0},{6,2},{8,12},{10,14},{12,8},{14,10},{1,5},{3,7},... | collective-permute-start | bytes 294920 | tf_op jit(solution)/shard_map/ppermute | solution.py:511
  17.9 7.3 %collective-permute-start.1 = (bf16[2,96,256]{2,1,0:T(8,128)(2,1)S(1)}, bf16[2,96,256]{2,1,0:T(8,128)(2,1)S(1)}, u32[]{:S(2)}, u32[]{:S(2)}) collective-permute-start(bf16[2,96,256]{2,1,0:T(8,128)(2,1)S(1)} %get-tuple-element.60), channel_id=1, source_target_pairs={{0,8},{2,10},{4,12},{6,14},{8,0},{10,2},{12,4},{14,6},{1,9},{3,11}... | collective-permute-start | bytes 294920 | tf_op jit(solution)/shard_map/ppermute | solution.py:511
  20.5 6.5 %collective-permute-start.2 = (bf16[2,96,256]{2,1,0:T(8,128)(2,1)S(1)}, bf16[2,96,256]{2,1,0:T(8,128)(2,1)S(1)}, u32[]{:S(2)}, u32[]{:S(2)}) collective-permute-start(bf16[2,96,256]{2,1,0:T(8,128)(2,1)S(1)} %get-tuple-element.62), channel_id=1, source_target_pairs={{0,12},{2,14},{4,8},{6,10},{8,4},{10,6},{12,0},{14,2},{1,13},{3,15... | collective-permute-start | bytes 294920 | tf_op jit(solution)/shard_map/ppermute | solution.py:511
  27.0 12.4 %collective-permute-start.10 = (bf16[2,2,48,1024]{3,2,1,0:T(8,128)(2,1)S(1)}, bf16[2,2,48,1024]{3,2,1,0:T(8,128)(2,1)S(1)}, u32[]{:S(2)}, u32[]{:S(2)}) collective-permute-start(bf16[2,2,48,1024]{3,2,1,0:T(8,128)(2,1)S(1)} %collective-permute-done.4.refs_5_), channel_id=1, source_target_pairs={{0,16},{16,0},{1,17},{17,1},{2,18},{18,2},{3,19},{19,3},{4,20},{20... | collective-permute-start | bytes 1179656 | tf_op jit(solution)/shard_map/ppermute | solution.py:478
  27.5 6.8 %collective-permute-start.6 = (bf16[2,96,256]{2,1,0:T(8,128)(2,1)S(1)}, bf16[2,96,256]{2,1,0:T(8,128)(2,1)S(1)}, u32[]{:S(2)}, u32[]{:S(2)}) collective-permute-start(bf16[2,96,256]{2,1,0:T(8,128)(2,1)S(1)} %get-tuple-element.69), channel_id=1, source_target_pairs={{0,2},{2,0},{4,6},{6,4},{8,10},{10,8},{12,14},{14,12},{1,3},{3,1},... | collective-permute-start | bytes 294920 | tf_op jit(solution)/shard_map/ppermute | solution.py:511
  29.0 7.0 %collective-permute-start.7 = (bf16[2,96,256]{2,1,0:T(8,128)(2,1)S(1)}, bf16[2,96,256]{2,1,0:T(8,128)(2,1)S(1)}, u32[]{:S(2)}, u32[]{:S(2)}) collective-permute-start(bf16[2,96,256]{2,1,0:T(8,128)(2,1)S(1)} %get-tuple-element.71), channel_id=1, source_target_pairs={{0,6},{2,4},{4,2},{6,0},{8,14},{10,12},{12,10},{14,8},{1,7},{3,5},... | collective-permute-start | bytes 294920 | tf_op jit(solution)/shard_map/ppermute | solution.py:511
  29.9 7.5 %collective-permute-start.8 = (bf16[2,96,256]{2,1,0:T(8,128)(2,1)S(1)}, bf16[2,96,256]{2,1,0:T(8,128)(2,1)S(1)}, u32[]{:S(2)}, u32[]{:S(2)}) collective-permute-start(bf16[2,96,256]{2,1,0:T(8,128)(2,1)S(1)} %get-tuple-element.73), channel_id=1, source_target_pairs={{0,10},{2,8},{4,14},{6,12},{8,2},{10,0},{12,6},{14,4},{1,11},{3,9}... | collective-permute-start | bytes 294920 | tf_op jit(solution)/shard_map/ppermute | solution.py:511
  32.0 7.4 %collective-permute-start.9 = (bf16[2,96,256]{2,1,0:T(8,128)(2,1)S(1)}, bf16[2,96,256]{2,1,0:T(8,128)(2,1)S(1)}, u32[]{:S(2)}, u32[]{:S(2)}) collective-permute-start(bf16[2,96,256]{2,1,0:T(8,128)(2,1)S(1)} %get-tuple-element.75), channel_id=1, source_target_pairs={{0,14},{2,12},{4,10},{6,8},{8,6},{10,4},{12,2},{14,0},{1,15},{3,13... | collective-permute-start | bytes 294920 | tf_op jit(solution)/shard_map/ppermute | solution.py:511
  39.5 2.1 %collective-permute-start.11 = (bf16[2,2,48,1024]{3,2,1,0:T(8,128)(2,1)S(1)}, bf16[2,2,48,1024]{3,2,1,0:T(8,128)(2,1)S(1)}, u32[]{:S(2)}, u32[]{:S(2)}) collective-permute-start(bf16[2,2,48,1024]{3,2,1,0:T(8,128)(2,1)S(1)} %collective-permute-done.3.refs_4_), channel_id=1, source_target_pairs={{0,1},{1,0},{2,3},{3,2},{4,5},{5,4},{6,7},{7,6},{8,9},{9,8},{10,11... | collective-permute-start | bytes 1179656 | tf_op jit(solution)/shard_map/ppermute | solution.py:478
  39.5 2.3 %collective-permute-start.12 = (bf16[2,2,48,1024]{3,2,1,0:T(8,128)(2,1)S(1)}, bf16[2,2,48,1024]{3,2,1,0:T(8,128)(2,1)S(1)}, u32[]{:S(2)}, u32[]{:S(2)}) collective-permute-start(bf16[2,2,48,1024]{3,2,1,0:T(8,128)(2,1)S(1)} %collective-permute-done.4.refs_5_), channel_id=1, source_target_pairs={{0,1},{1,0},{2,3},{3,2},{4,5},{5,4},{6,7},{7,6},{8,9},{9,8},{10,11... | collective-permute-start | bytes 1179656 | tf_op jit(solution)/shard_map/ppermute | solution.py:478
  40.0 2.3 %collective-permute-start.13 = (bf16[2,2,48,1024]{3,2,1,0:T(8,128)(2,1)S(1)}, bf16[2,2,48,1024]{3,2,1,0:T(8,128)(2,1)S(1)}, u32[]{:S(2)}, u32[]{:S(2)}) collective-permute-start(bf16[2,2,48,1024]{3,2,1,0:T(8,128)(2,1)S(1)} %collective-permute-done.5.refs_8_), channel_id=1, source_target_pairs={{0,1},{1,0},{2,3},{3,2},{4,5},{5,4},{6,7},{7,6},{8,9},{9,8},{10,11... | collective-permute-start | bytes 1179656 | tf_op jit(solution)/shard_map/ppermute | solution.py:478
  40.0 2.9 %collective-permute-start.14 = (bf16[2,2,48,1024]{3,2,1,0:T(8,128)(2,1)S(1)}, bf16[2,2,48,1024]{3,2,1,0:T(8,128)(2,1)S(1)}, u32[]{:S(2)}, u32[]{:S(2)}) collective-permute-start(bf16[2,2,48,1024]{3,2,1,0:T(8,128)(2,1)S(1)} %collective-permute-done.10.refs_9_), channel_id=1, source_target_pairs={{0,1},{1,0},{2,3},{3,2},{4,5},{5,4},{6,7},{7,6},{8,9},{9,8},{10,11... | collective-permute-start | bytes 1179656 | tf_op jit(solution)/shard_map/ppermute | solution.py:478
  40.5 26.7 %slice-start.2 = ((s8[6291456]{0:T(1024)(128)(4,1)}), s8[4194304]{0:T(1024)(128)(4,1)S(1)}, s32[]{:S(2)}) async-start(s8[6291456]{0:T(1024)(128)(4,1)} %bitcast.5), calls=%async_computation.2 | async-start | bytes 8388608
  41.6 25.6 %slice-start.3 = ((s8[6291456]{0:T(1024)(128)(4,1)}), s8[2097152]{0:T(1024)(128)(4,1)S(1)}, s32[]{:S(2)}) async-start(s8[6291456]{0:T(1024)(128)(4,1)} %bitcast.5), calls=%async_computation.3 | async-start | bytes 4194304
  46.7 6.4 %collective-permute-start.15 = (bf16[2,96,256]{2,1,0:T(8,128)(2,1)S(1)}, bf16[2,96,256]{2,1,0:T(8,128)(2,1)S(1)}, u32[]{:S(2)}, u32[]{:S(2)}) collective-permute-start(bf16[2,96,256]{2,1,0:T(8,128)(2,1)S(1)} %get-tuple-element.94), channel_id=1, source_target_pairs={{0,2},{2,0},{4,6},{6,4},{8,10},{10,8},{12,14},{14,12},{1,3},{3,1},... | collective-permute-start | bytes 294920 | tf_op jit(solution)/shard_map/ppermute | solution.py:487
  47.2 8.2 %collective-permute-start.16 = (bf16[2,96,256]{2,1,0:T(8,128)(2,1)S(1)}, bf16[2,96,256]{2,1,0:T(8,128)(2,1)S(1)}, u32[]{:S(2)}, u32[]{:S(2)}) collective-permute-start(bf16[2,96,256]{2,1,0:T(8,128)(2,1)S(1)} %get-tuple-element.95), channel_id=1, source_target_pairs={{0,4},{2,6},{4,0},{6,2},{8,12},{10,14},{12,8},{14,10},{1,5},{3,7},... | collective-permute-start | bytes 294920 | tf_op jit(solution)/shard_map/ppermute | solution.py:487
  48.8 9.1 %collective-permute-start.17 = (bf16[2,96,256]{2,1,0:T(8,128)(2,1)S(1)}, bf16[2,96,256]{2,1,0:T(8,128)(2,1)S(1)}, u32[]{:S(2)}, u32[]{:S(2)}) collective-permute-start(bf16[2,96,256]{2,1,0:T(8,128)(2,1)S(1)} %get-tuple-element.96), channel_id=1, source_target_pairs={{0,6},{2,4},{4,2},{6,0},{8,14},{10,12},{12,10},{14,8},{1,7},{3,5},... | collective-permute-start | bytes 294920 | tf_op jit(solution)/shard_map/ppermute | solution.py:487
  50.2 14.9 %collective-permute-start.18 = (bf16[2,96,256]{2,1,0:T(8,128)(2,1)S(1)}, bf16[2,96,256]{2,1,0:T(8,128)(2,1)S(1)}, u32[]{:S(2)}, u32[]{:S(2)}) collective-permute-start(bf16[2,96,256]{2,1,0:T(8,128)(2,1)S(1)} %get-tuple-element.97), channel_id=1, source_target_pairs={{0,8},{2,10},{4,12},{6,14},{8,0},{10,2},{12,4},{14,6},{1,9},{3,11}... | collective-permute-start | bytes 294920 | tf_op jit(solution)/shard_map/ppermute | solution.py:487
  51.0 16.1 %collective-permute-start.19 = (bf16[2,96,256]{2,1,0:T(8,128)(2,1)S(1)}, bf16[2,96,256]{2,1,0:T(8,128)(2,1)S(1)}, u32[]{:S(2)}, u32[]{:S(2)}) collective-permute-start(bf16[2,96,256]{2,1,0:T(8,128)(2,1)S(1)} %get-tuple-element.98), channel_id=1, source_target_pairs={{0,10},{2,8},{4,14},{6,12},{8,2},{10,0},{12,6},{14,4},{1,11},{3,9}... | collective-permute-start | bytes 294920 | tf_op jit(solution)/shard_map/ppermute | solution.py:487
  53.0 14.1 %collective-permute-start.20 = (bf16[2,96,256]{2,1,0:T(8,128)(2,1)S(1)}, bf16[2,96,256]{2,1,0:T(8,128)(2,1)S(1)}, u32[]{:S(2)}, u32[]{:S(2)}) collective-permute-start(bf16[2,96,256]{2,1,0:T(8,128)(2,1)S(1)} %get-tuple-element.99), channel_id=1, source_target_pairs={{0,12},{2,14},{4,8},{6,10},{8,4},{10,6},{12,0},{14,2},{1,13},{3,15... | collective-permute-start | bytes 294920 | tf_op jit(solution)/shard_map/ppermute | solution.py:487
  55.4 11.7 %collective-permute-start.21 = (bf16[2,96,256]{2,1,0:T(8,128)(2,1)S(1)}, bf16[2,96,256]{2,1,0:T(8,128)(2,1)S(1)}, u32[]{:S(2)}, u32[]{:S(2)}) collective-permute-start(bf16[2,96,256]{2,1,0:T(8,128)(2,1)S(1)} %get-tuple-element.100), channel_id=1, source_target_pairs={{0,14},{2,12},{4,10},{6,8},{8,6},{10,4},{12,2},{14,0},{1,15},{3,13... | collective-permute-start | bytes 294920 | tf_op jit(solution)/shard_map/ppermute | solution.py:487

commit v4 on v3

--- a/solution.py
+++ b/solution.py
@@ -418,17 +418,13 @@
     width = 512
     capacity = 2 * half
     list_tiles(owners, tile_of, held, count_col, capacity)
-    for s in range(half):
-        for d in range(count_col):
-            for e in range(2):
-                tile = tile_of[(column ^ d) * capacity + (mine ^ e) * half + s]
-                values = arrivals[2 * d + e][s].astype(jnp.float32)
-                for j in range(blocks):
+    def gather(j):
+        for s in range(half):
+            for d in range(count_col):
+                for e in range(2):
+                    tile = tile_of[(column ^ d) * capacity + (mine ^ e) * half + s]
+                    values = arrivals[2 * d + e][s].astype(jnp.float32)
                     gathered[j, pl.ds(pl.multiple_of(tile * R, 8), R), :] = values[j * R : (j + 1) * R]
-    row_id = lax.broadcasted_iota(jnp.int32, (2 * vis, 2 * vis), 0)
-    column_id = lax.broadcasted_iota(jnp.int32, (2 * vis, 2 * vis), 1)
-    identity = jnp.where(row_id == column_id, 1.0, 0.0).astype(jnp.bfloat16)
-    for j in range(blocks):
         values = gathered[j]
         adjoint[j, :rows] = values.astype(jnp.bfloat16)
         adjoint[j, rows:] = jnp.concatenate([values[:, vis:], -values[:, :vis]], axis=1).astype(jnp.bfloat16)
@@ -437,6 +433,8 @@
     for n in range(sources // width):
         j = n * width // TS
         at = pl.ds(n * width, width)
+        if n * width % TS == 0:
+            gather(j)
         right = factors[:, :, at].reshape(2 * rows, width)
         wave = dot(adjoint[j], right, 0, 0)
         out_here[:, :, at] = focus[:, :, at] - wave.reshape(two, vis, width)
@@ -523,14 +521,14 @@
     second = [head, swap(first[1], "grp")]
     for offset in (7, 5, 3, 1):
         arrived[offset] = move(offset, arrived[offset])
-    held = lax.optimization_barrier(tuple(arrived + first + second + [u_here]))
-    arrived, (*pieces, u_here) = list(held[: 2 * count_col]), held[2 * count_col :]
-    first, second = pieces[: len(cuts)], pieces[len(cuts) :]
+    tied = lax.optimization_barrier(tuple(first + [arrived[n] for n in (7, 5)]))
+    first = list(tied[:2])
+    mates = [swap(piece, "rep") for piece in first]
     own = own_field(count_col, half, mask, u_here, arrived[::2])
-    gathered = []
-    for group in (first, second):
-        gathered.extend(group)
-        gathered.extend([swap(piece, "rep") for piece in group])
+    held = lax.optimization_barrier(tuple(arrived + first + second + [u_here, own]))
+    arrived, (*pieces, u_here, own) = list(held[: 2 * count_col]), held[2 * count_col :]
+    first, second = pieces[:2], pieces[2:4]
+    gathered = first + mates + second + [swap(piece, "rep") for piece in second]
     back = receiver_products(count_col, half, mask, mixing, own, arrived[1::2], u_here, gathered)
     returned = exchange(back, count_col)
     return update_products(count_col, half, owners, returned, focus_here, v_here)

time: 71.6 us -> 70.8 us (0.989)
  waiting for transfers between devices: 22 us -> 21.1 us
    ppermute x7, waiting for transfers between devices: 9.92 us -> 8.61 us  [move(): lax.ppermute(payload, ('col', 'freq'), [(i, i ^ offset) for i in range(2...]
  transfers between devices with their start and end apart: 22 -> 22, of which waited for: 11 -> 10; matrix products, arithmetic and copies ran while one was open for 0% -> 0% of each run, Pallas kernels for 14% -> 15%
where the time goes in v4:
time: 70.8 us; the launch traced here: 69.6 us
  starting transfers between devices  29 us (41%)
  waiting for transfers between devices  21.1 us (30%)
  Pallas kernels  17.3 us (24%)
  local copies, waits for them, and re-layouts  2.06 us (3%)
    ppermute x7, starting transfers between devices, exchange(): lax.ppermute(arrays[offset], ('col', 'freq'), [(i, i ^ offset) for i in r...  11.2 us
    ppermute x7, starting transfers between devices, move(): lax.ppermute(payload, ('col', 'freq'), [(i, i ^ offset) for i in range(2...  11.1 us
    ppermute x7, waiting for transfers between devices, exchange(): lax.ppermute(arrays[offset], ('col', 'freq'), [(i, i ^ offset) for i in r...  9.12 us
    ppermute x7, waiting for transfers between devices, move(): lax.ppermute(payload, ('col', 'freq'), [(i, i ^ offset) for i in range(2...  8.61 us
    pallas_call x1, Pallas kernels, forward_products(): pl.pallas_call(functools.partial(forward_kernel, count_col, half), in_spe...  7.49 us
    ppermute x8, starting transfers between devices, swap(): return lax.ppermute(array, axis, [(0, 1), (1, 0)])  6.71 us
    pallas_call x1, Pallas kernels, receiver_products(): pl.pallas_call(functools.partial(receiver_kernel, count_col, half), in_sp...  3.78 us
    pallas_call x1, Pallas kernels, update_products(): pl.pallas_call(functools.partial(update_kernel, count_col, half), in_spec...  3.44 us
  transfers between devices with their start and end apart: 22, of which 10 were waited for; matrix products, arithmetic and copies ran while one was open for 0% of the time, Pallas kernels for 15%

profile of v4, /device:TPU:0, one launch (start us, length us, event | category | flops | bytes accessed | tf_op | source)
XLA Modules:
  0.0 69.6 jit_solution(11919438822088850646)
XLA Ops:
  0.0 1.2 %dynamic-slice_bitcast_fusion = bf16[2,2,96,1024]{3,2,1,0:T(8,128)(2,1)S(1)} fusion(bf16[1,2,4,384,1024]{4,3,2,1,0:T(8,128)(2,1)} %u_factors, s32[]{:T(128)S(6)} %select_n.6, s32[]{:T(128)S(6)} %select_n.7), kind=kLoop, calls=%fused_computation | loop fusion | bytes 1572872 | tf_op jit(solution)/shard_map/reshape | solution.py:505
  1.2 0.0 slice-start
  1.2 0.0 copy-start
  1.2 0.0 copy-start.1
  1.2 0.0 copy-start.2
  1.2 0.1 fusion
  1.3 3.0 %collective-permute-start.3 = (bf16[2,2,48,1024]{3,2,1,0:T(8,128)(2,1)S(1)}, bf16[2,2,48,1024]{3,2,1,0:T(8,128)(2,1)S(1)}, u32[]{:S(2)}, u32[]{:S(2)}) collective-permute-start(bf16[2,2,48,1024]{3,2,1,0:T(8,128)(2,1)S(1)} %get-tuple-element.102), channel_id=1, source_target_pairs={{0,2},{2,0},{1,3},{3,1},{4,6},{6,4},{5,7},{7,5},{8,10},{10,8},{9,1... | collective-permute-start | bytes 1179656 | tf_op jit(solution)/shard_map/ppermute | solution.py:476
  4.3 0.1 collective-permute-start.4
  4.4 0.8 %copy-done.3 = s32[16]{0:T(128)S(1)} copy-done((s32[16]{0:T(128)S(1)}, s32[16]{0:T(128)}, u32[]{:S(2)}) %copy-start.3) | copy-done | bytes 88
  5.2 7.5 %forward_products.1 = (bf16[2,96,256]{2,1,0:T(8,128)(2,1)S(1)}, bf16[2,96,256]{2,1,0:T(8,128)(2,1)S(1)}, bf16[2,96,256]{2,1,0:T(8,128)(2,1)S(1)}, bf16[2,96,256]...) custom-call(s32[16]{0:T(128)S(1)} %copy-done.3, ...), custom_call_target="tpu_custom_call" | custom-call | flops 1610612736 | bytes 10485760 | tf_op jit(solution)/shard_map/forward_products/pallas_call | solution.py:226
  12.7 1.6 %collective-permute-done.3.refs_4_ = bf16[2,2,48,1024]{3,2,1,0:T(8,128)(2,1)S(1)} collective-permute-done((bf16[2,2,48,1024]{3,2,1,0:T(8,128)(2,1)S(1)}, bf16[2,2,48,1024]{3,2,1,0:T(8,128)(2,1)S(1)}, u32[]{:S(2)}, u32[]{:S(2)}) %collective-permute-start.3) | collective-permute-done | bytes 393248 | tf_op jit(solution)/shard_map/ppermute | solution.py:476
  14.2 2.1 %collective-permute-start.5 = (bf16[2,2,48,1024]{3,2,1,0:T(8,128)(2,1)S(1)}, bf16[2,2,48,1024]{3,2,1,0:T(8,128)(2,1)S(1)}, u32[]{:S(2)}, u32[]{:S(2)}) collective-permute-start(bf16[2,2,48,1024]{3,2,1,0:T(8,128)(2,1)S(1)} %collective-permute-done.3.refs_4_), channel_id=1, source_target_pairs={{0,16},{16,0},{1,17},{17,1},{2,18},{18,2},{3,19},{19,3},{4,20},{20... | collective-permute-start | bytes 1179656 | tf_op jit(solution)/shard_map/ppermute | solution.py:476
  16.3 1.6 %collective-permute-start = (bf16[2,96,256]{2,1,0:T(8,128)(2,1)S(1)}, bf16[2,96,256]{2,1,0:T(8,128)(2,1)S(1)}, u32[]{:S(2)}, u32[]{:S(2)}) collective-permute-start(bf16[2,96,256]{2,1,0:T(8,128)(2,1)S(1)} %get-tuple-element.57), channel_id=1, source_target_pairs={{0,4},{2,6},{4,0},{6,2},{8,12},{10,14},{12,8},{14,10},{1,5},{3,7},... | collective-permute-start | bytes 294920 | tf_op jit(solution)/shard_map/ppermute | solution.py:509
  17.9 2.6 %collective-permute-start.1 = (bf16[2,96,256]{2,1,0:T(8,128)(2,1)S(1)}, bf16[2,96,256]{2,1,0:T(8,128)(2,1)S(1)}, u32[]{:S(2)}, u32[]{:S(2)}) collective-permute-start(bf16[2,96,256]{2,1,0:T(8,128)(2,1)S(1)} %get-tuple-element.59), channel_id=1, source_target_pairs={{0,8},{2,10},{4,12},{6,14},{8,0},{10,2},{12,4},{14,6},{1,9},{3,11}... | collective-permute-start | bytes 294920 | tf_op jit(solution)/shard_map/ppermute | solution.py:509
  20.5 0.2 collective-permute-start.2
  20.7 0.0 slice-done
  20.7 0.0 copy-done
  20.7 0.0 copy-done.1
  20.7 0.0 copy-done.2
  20.7 0.0 slice-done.1
  20.8 1.5 %prepare.1 = (bf16[2,2,384,1024]{3,2,1,0:T(8,128)(2,1)S(1)}, f32[2,16,1024]{2,1,0:T(8,128)S(1)}, bf16[2,384,256]{2,1,0:T(8,128)(2,1)S(1)}) custom-call(s32[16]{0:T(128)S(1)} %copy-done.3, s32[16,16]{1,0:T(8,128)S(1)} %copy-done.2, s32[16,1,1024]{2,1,0:T(1,128)S(1)} %bitcast.7, bf16[2,48,512]{2,1,0:T(8,128)(2,1)S(1)} %copy-done, ...), custom_call_target="tpu_custom_call" | custom-call | bytes 6291456 | tf_op jit(solution)/shard_map/prepare/pallas_call | solution.py:272
  22.3 0.0 collective-permute-done.refs_1_
  22.3 3.0 %collective-permute-done.1.refs_2_ = bf16[2,96,256]{2,1,0:T(8,128)(2,1)S(1)} collective-permute-done((bf16[2,96,256]{2,1,0:T(8,128)(2,1)S(1)}, bf16[2,96,256]{2,1,0:T(8,128)(2,1)S(1)}, u32[]{:S(2)}, u32[]{:S(2)}) %collective-permute-start.1) | collective-permute-done | bytes 98336 | tf_op jit(solution)/shard_map/ppermute | solution.py:509
  25.3 1.8 %collective-permute-done.2.refs_3_ = bf16[2,96,256]{2,1,0:T(8,128)(2,1)S(1)} collective-permute-done((bf16[2,96,256]{2,1,0:T(8,128)(2,1)S(1)}, bf16[2,96,256]{2,1,0:T(8,128)(2,1)S(1)}, u32[]{:S(2)}, u32[]{:S(2)}) %collective-permute-start.2) | collective-permute-done | bytes 98336 | tf_op jit(solution)/shard_map/ppermute | solution.py:509
  27.0 0.0 collective-permute-done.4.refs_5_
  27.0 0.0 collective-permute-done.5.refs_8_
  27.0 0.5 collective-permute-start.10
  27.5 3.3 %collective-permute-start.8 = (bf16[2,96,256]{2,1,0:T(8,128)(2,1)S(1)}, bf16[2,96,256]{2,1,0:T(8,128)(2,1)S(1)}, u32[]{:S(2)}, u32[]{:S(2)}) collective-permute-start(bf16[2,96,256]{2,1,0:T(8,128)(2,1)S(1)} %get-tuple-element.72), channel_id=1, source_target_pairs={{0,10},{2,8},{4,14},{6,12},{8,2},{10,0},{12,6},{14,4},{1,11},{3,9}... | collective-permute-start | bytes 294920 | tf_op jit(solution)/shard_map/ppermute | solution.py:509
  30.9 0.8 %collective-permute-start.9 = (bf16[2,96,256]{2,1,0:T(8,128)(2,1)S(1)}, bf16[2,96,256]{2,1,0:T(8,128)(2,1)S(1)}, u32[]{:S(2)}, u32[]{:S(2)}) collective-permute-start(bf16[2,96,256]{2,1,0:T(8,128)(2,1)S(1)} %get-tuple-element.74), channel_id=1, source_target_pairs={{0,14},{2,12},{4,10},{6,8},{8,6},{10,4},{12,2},{14,0},{1,15},{3,13... | collective-permute-start | bytes 294920 | tf_op jit(solution)/shard_map/ppermute | solution.py:509
  31.7 2.5 %collective-permute-start.6 = (bf16[2,96,256]{2,1,0:T(8,128)(2,1)S(1)}, bf16[2,96,256]{2,1,0:T(8,128)(2,1)S(1)}, u32[]{:S(2)}, u32[]{:S(2)}) collective-permute-start(bf16[2,96,256]{2,1,0:T(8,128)(2,1)S(1)} %get-tuple-element.68), channel_id=1, source_target_pairs={{0,2},{2,0},{4,6},{6,4},{8,10},{10,8},{12,14},{14,12},{1,3},{3,1},... | collective-permute-start | bytes 294920 | tf_op jit(solution)/shard_map/ppermute | solution.py:509
  34.2 0.0 collective-permute-start.7
  34.2 1.1 %own_field.1.own = bf16[2,256,1024]{2,1,0:T(8,128)(2,1)S(1)} custom-call(bf16[2,384,256]{2,1,0:T(8,128)(2,1)S(1)} %get-tuple-element.55.mask, bf16[2,2,384,1024]{3,2,1,0:T(8,128)(2,1)S(1)} %get-tuple-element.82.u_own, bf16[2,96,256]{2,1,0:T(8,128)(2,1)S(1)} %get-tuple-element.67.refs_0_, bf16[2,96,256]{2,1,0:T(8,128)(2,1)S(1)} %collective-permute-done.refs_1_, ...), custom_call_target="tpu_custom_call" | custom-call | flops 805306368 | bytes 1572864 | tf_op jit(solution)/shard_map/own_field/pallas_call | solution.py:316
  35.4 0.0 slice-start.3
  35.4 0.0 collective-permute-done.8.refs_2_
  35.4 2.8 %collective-permute-done.9.refs_3_ = bf16[2,96,256]{2,1,0:T(8,128)(2,1)S(1)} collective-permute-done((bf16[2,96,256]{2,1,0:T(8,128)(2,1)S(1)}, bf16[2,96,256]{2,1,0:T(8,128)(2,1)S(1)}, u32[]{:S(2)}, u32[]{:S(2)}) %collective-permute-start.9) | collective-permute-done | bytes 98336 | tf_op jit(solution)/shard_map/ppermute | solution.py:509
  38.2 0.0 collective-permute-start.11
  38.2 0.5 collective-permute-start.12
  38.7 0.0 collective-permute-done.6.refs_0_
  38.7 1.1 %collective-permute-done.7.refs_1_ = bf16[2,96,256]{2,1,0:T(8,128)(2,1)S(1)} collective-permute-done((bf16[2,96,256]{2,1,0:T(8,128)(2,1)S(1)}, bf16[2,96,256]{2,1,0:T(8,128)(2,1)S(1)}, u32[]{:S(2)}, u32[]{:S(2)}) %collective-permute-start.7) | collective-permute-done | bytes 98336 | tf_op jit(solution)/shard_map/ppermute | solution.py:509
  39.8 0.0 collective-permute-done.10.refs_9_
  39.8 0.0 collective-permute-start.13
  39.8 0.5 collective-permute-start.14
  40.3 0.0 collective-permute-done.11.refs_6_
  40.3 0.2 collective-permute-done.12.refs_7_
  40.5 1.0 %collective-permute-done.13.refs_10_ = bf16[2,2,48,1024]{3,2,1,0:T(8,128)(2,1)S(1)} collective-permute-done((bf16[2,2,48,1024]{3,2,1,0:T(8,128)(2,1)S(1)}, bf16[2,2,48,1024]{3,2,1,0:T(8,128)(2,1)S(1)}, u32[]{:S(2)}, u32[]{:S(2)}) %collective-permute-start.13) | collective-permute-done | bytes 393248 | tf_op jit(solution)/shard_map/ppermute | solution.py:476
  41.5 0.6 collective-permute-done.14.refs_11_
  42.1 3.8 %receiver_products.1 = (bf16[2,96,256]{2,1,0:T(8,128)(2,1)S(1)}, bf16[2,96,256]{2,1,0:T(8,128)(2,1)S(1)}, bf16[2,96,256]{2,1,0:T(8,128)(2,1)S(1)}, bf16[2,96,256...) custom-call(bf16[2,384,256]{2,1,0:T(8,128)(2,1)S(1)} %get-tuple-elem, ...), custom_call_target="tpu_custom_call" | custom-call | flops 2415919104 | bytes 6291456 | tf_op jit(solution)/shard_map/receiver_products/pallas_call | solution.py:390
  45.8 0.4 collective-permute-start.15
  46.2 0.2 collective-permute-start.16
  46.5 2.9 %collective-permute-start.17 = (bf16[2,96,256]{2,1,0:T(8,128)(2,1)S(1)}, bf16[2,96,256]{2,1,0:T(8,128)(2,1)S(1)}, u32[]{:S(2)}, u32[]{:S(2)}) collective-permute-start(bf16[2,96,256]{2,1,0:T(8,128)(2,1)S(1)} %get-tuple-element.94), channel_id=1, source_target_pairs={{0,6},{2,4},{4,2},{6,0},{8,14},{10,12},{12,10},{14,8},{1,7},{3,5},... | collective-permute-start | bytes 294920 | tf_op jit(solution)/shard_map/ppermute | solution.py:485
  49.4 0.4 collective-permute-start.18
  49.8 2.3 %collective-permute-start.19 = (bf16[2,96,256]{2,1,0:T(8,128)(2,1)S(1)}, bf16[2,96,256]{2,1,0:T(8,128)(2,1)S(1)}, u32[]{:S(2)}, u32[]{:S(2)}) collective-permute-start(bf16[2,96,256]{2,1,0:T(8,128)(2,1)S(1)} %get-tuple-element.96), channel_id=1, source_target_pairs={{0,10},{2,8},{4,14},{6,12},{8,2},{10,0},{12,6},{14,4},{1,11},{3,9}... | collective-permute-start | bytes 294920 | tf_op jit(solution)/shard_map/ppermute | solution.py:485
  52.1 0.0 collective-permute-done.15.refs_1_
  52.1 1.9 %collective-permute-start.20 = (bf16[2,96,256]{2,1,0:T(8,128)(2,1)S(1)}, bf16[2,96,256]{2,1,0:T(8,128)(2,1)S(1)}, u32[]{:S(2)}, u32[]{:S(2)}) collective-permute-start(bf16[2,96,256]{2,1,0:T(8,128)(2,1)S(1)} %get-tuple-element.97), channel_id=1, source_target_pairs={{0,12},{2,14},{4,8},{6,10},{8,4},{10,6},{12,0},{14,2},{1,13},{3,15... | collective-permute-start | bytes 294920 | tf_op jit(solution)/shard_map/ppermute | solution.py:485
  54.0 0.0 collective-permute-done.16.refs_2_
  54.0 3.0 %collective-permute-start.21 = (bf16[2,96,256]{2,1,0:T(8,128)(2,1)S(1)}, bf16[2,96,256]{2,1,0:T(8,128)(2,1)S(1)}, u32[]{:S(2)}, u32[]{:S(2)}) collective-permute-start(bf16[2,96,256]{2,1,0:T(8,128)(2,1)S(1)} %get-tuple-element.98), channel_id=1, source_target_pairs={{0,14},{2,12},{4,10},{6,8},{8,6},{10,4},{12,2},{14,0},{1,15},{3,13... | collective-permute-start | bytes 294920 | tf_op jit(solution)/shard_map/ppermute | solution.py:485
  57.0 0.0 collective-permute-done.17.refs_3_
  57.1 6.5 %collective-permute-done.18.refs_4_ = bf16[2,96,256]{2,1,0:T(8,128)(2,1)S(1)} collective-permute-done((bf16[2,96,256]{2,1,0:T(8,128)(2,1)S(1)}, bf16[2,96,256]{2,1,0:T(8,128)(2,1)S(1)}, u32[]{:S(2)}, u32[]{:S(2)}) %collective-permute-start.18) | collective-permute-done | bytes 98336 | tf_op jit(solution)/shard_map/ppermute | solution.py:485
  63.6 2.6 %collective-permute-done.19.refs_5_ = bf16[2,96,256]{2,1,0:T(8,128)(2,1)S(1)} collective-permute-done((bf16[2,96,256]{2,1,0:T(8,128)(2,1)S(1)}, bf16[2,96,256]{2,1,0:T(8,128)(2,1)S(1)}, u32[]{:S(2)}, u32[]{:S(2)}) %collective-permute-start.19) | collective-permute-done | bytes 98336 | tf_op jit(solution)/shard_map/ppermute | solution.py:485
  66.2 0.0 collective-permute-done.20.refs_6_
  66.2 0.0 collective-permute-done.21.refs_7_
  66.2 0.0 slice-done.2
  66.2 0.0 slice-done.3
  66.2 3.4 %update_products.1 = f32[1,2,128,4096]{3,2,1,0:T(8,128)} custom-call(s32[16]{0:T(128)S(1)} %copy-done.3, bf16[2,96,256]{2,1,0:T(8,128)(2,1)S(1)} %get-tuple-element.91.refs_0_, bf16[2,96,256]{2,1,0:T(8,128)(2,1)S(1)} %collective-permute-done.15.refs_1_, bf16[2,96,256]{2,1,0:T(8,128)(2,1)S(1)} %collective-permute-done.16.refs_2_, ...), custom_call_target="tpu_custom_call" | custom-call | flops 1610612736 | bytes 14680064 | tf_op jit(solution)/shard_map/update_products/pallas_call | solution.py:454
  (5 shorter events, 0.0 us)
Async XLA Ops:
  1.2 19.5 %slice-start = ((s8[6291456]{0:T(1024)(128)(4,1)}), s8[4194304]{0:T(1024)(128)(4,1)S(1)}, s32[]{:S(2)}) async-start(s8[6291456]{0:T(1024)(128)(4,1)} %bitcast.3), calls=%async_computation | async-start | bytes 8388608
  1.2 19.5 %copy-start = (bf16[2,48,512]{2,1,0:T(8,128)(2,1)S(1)}, bf16[2,48,512]{2,1,0:T(8,128)(2,1)}, u32[]{:S(2)}) copy-start(bf16[2,48,512]{2,1,0:T(8,128)(2,1)} %constant.24.clone.table) | copy-start | bytes 294916
  1.2 19.5 %copy-start.1 = (s32[16384]{0:T(1024)S(1)}, s32[16384]{0:T(1024)}, u32[]{:S(2)}) copy-start(s32[16384]{0:T(1024)} %param.12) | copy-start | bytes 196612
  1.2 19.5 %copy-start.2 = (s32[16,16]{1,0:T(8,128)S(1)}, s32[16,16]{1,0:T(8,128)}, u32[]{:S(2)}) copy-start(s32[16,16]{1,0:T(8,128)} %ranks.1) | copy-start | bytes 3076
  1.3 12.9 %collective-permute-start.3 = (bf16[2,2,48,1024]{3,2,1,0:T(8,128)(2,1)S(1)}, bf16[2,2,48,1024]{3,2,1,0:T(8,128)(2,1)S(1)}, u32[]{:S(2)}, u32[]{:S(2)}) collective-permute-start(bf16[2,2,48,1024]{3,2,1,0:T(8,128)(2,1)S(1)} %get-tuple-element.102), channel_id=1, source_target_pairs={{0,2},{2,0},{1,3},{3,1},{4,6},{6,4},{5,7},{7,5},{8,10},{10,8},{9,1... | collective-permute-start | bytes 1179656 | tf_op jit(solution)/shard_map/ppermute | solution.py:476
  4.3 16.4 %slice-start.1 = ((s8[6291456]{0:T(1024)(128)(4,1)}), s8[2097152]{0:T(1024)(128)(4,1)S(1)}, s32[]{:S(2)}) async-start(s8[6291456]{0:T(1024)(128)(4,1)} %bitcast.3), calls=%async_computation.1 | async-start | bytes 4194304
  4.3 22.7 %collective-permute-start.4 = (bf16[2,2,48,1024]{3,2,1,0:T(8,128)(2,1)S(1)}, bf16[2,2,48,1024]{3,2,1,0:T(8,128)(2,1)S(1)}, u32[]{:S(2)}, u32[]{:S(2)}) collective-permute-start(bf16[2,2,48,1024]{3,2,1,0:T(8,128)(2,1)S(1)} %get-tuple-element.101), channel_id=1, source_target_pairs={{0,2},{2,0},{1,3},{3,1},{4,6},{6,4},{5,7},{7,5},{8,10},{10,8},{9,1... | collective-permute-start | bytes 1179656 | tf_op jit(solution)/shard_map/ppermute | solution.py:476
  4.4 0.8 %copy-start.3 = (s32[16]{0:T(128)S(1)}, s32[16]{0:T(128)}, u32[]{:S(2)}) copy-start(s32[16]{0:T(128)} %owners.3) | copy-start | bytes 196
  14.2 12.8 %collective-permute-start.5 = (bf16[2,2,48,1024]{3,2,1,0:T(8,128)(2,1)S(1)}, bf16[2,2,48,1024]{3,2,1,0:T(8,128)(2,1)S(1)}, u32[]{:S(2)}, u32[]{:S(2)}) collective-permute-start(bf16[2,2,48,1024]{3,2,1,0:T(8,128)(2,1)S(1)} %collective-permute-done.3.refs_4_), channel_id=1, source_target_pairs={{0,16},{16,0},{1,17},{17,1},{2,18},{18,2},{3,19},{19,3},{4,20},{20... | collective-permute-start | bytes 1179656 | tf_op jit(solution)/shard_map/ppermute | solution.py:476
  16.3 5.9 %collective-permute-start = (bf16[2,96,256]{2,1,0:T(8,128)(2,1)S(1)}, bf16[2,96,256]{2,1,0:T(8,128)(2,1)S(1)}, u32[]{:S(2)}, u32[]{:S(2)}) collective-permute-start(bf16[2,96,256]{2,1,0:T(8,128)(2,1)S(1)} %get-tuple-element.57), channel_id=1, source_target_pairs={{0,4},{2,6},{4,0},{6,2},{8,12},{10,14},{12,8},{14,10},{1,5},{3,7},... | collective-permute-start | bytes 294920 | tf_op jit(solution)/shard_map/ppermute | solution.py:509
  17.9 7.3 %collective-permute-start.1 = (bf16[2,96,256]{2,1,0:T(8,128)(2,1)S(1)}, bf16[2,96,256]{2,1,0:T(8,128)(2,1)S(1)}, u32[]{:S(2)}, u32[]{:S(2)}) collective-permute-start(bf16[2,96,256]{2,1,0:T(8,128)(2,1)S(1)} %get-tuple-element.59), channel_id=1, source_target_pairs={{0,8},{2,10},{4,12},{6,14},{8,0},{10,2},{12,4},{14,6},{1,9},{3,11}... | collective-permute-start | bytes 294920 | tf_op jit(solution)/shard_map/ppermute | solution.py:509
  20.5 6.5 %collective-permute-start.2 = (bf16[2,96,256]{2,1,0:T(8,128)(2,1)S(1)}, bf16[2,96,256]{2,1,0:T(8,128)(2,1)S(1)}, u32[]{:S(2)}, u32[]{:S(2)}) collective-permute-start(bf16[2,96,256]{2,1,0:T(8,128)(2,1)S(1)} %get-tuple-element.61), channel_id=1, source_target_pairs={{0,12},{2,14},{4,8},{6,10},{8,4},{10,6},{12,0},{14,2},{1,13},{3,15... | collective-permute-start | bytes 294920 | tf_op jit(solution)/shard_map/ppermute | solution.py:509
  27.0 12.7 %collective-permute-start.10 = (bf16[2,2,48,1024]{3,2,1,0:T(8,128)(2,1)S(1)}, bf16[2,2,48,1024]{3,2,1,0:T(8,128)(2,1)S(1)}, u32[]{:S(2)}, u32[]{:S(2)}) collective-permute-start(bf16[2,2,48,1024]{3,2,1,0:T(8,128)(2,1)S(1)} %collective-permute-done.4.refs_5_), channel_id=1, source_target_pairs={{0,16},{16,0},{1,17},{17,1},{2,18},{18,2},{3,19},{19,3},{4,20},{20... | collective-permute-start | bytes 1179656 | tf_op jit(solution)/shard_map/ppermute | solution.py:476
  27.5 7.8 %collective-permute-start.8 = (bf16[2,96,256]{2,1,0:T(8,128)(2,1)S(1)}, bf16[2,96,256]{2,1,0:T(8,128)(2,1)S(1)}, u32[]{:S(2)}, u32[]{:S(2)}) collective-permute-start(bf16[2,96,256]{2,1,0:T(8,128)(2,1)S(1)} %get-tuple-element.72), channel_id=1, source_target_pairs={{0,10},{2,8},{4,14},{6,12},{8,2},{10,0},{12,6},{14,4},{1,11},{3,9}... | collective-permute-start | bytes 294920 | tf_op jit(solution)/shard_map/ppermute | solution.py:509
  30.9 7.3 %collective-permute-start.9 = (bf16[2,96,256]{2,1,0:T(8,128)(2,1)S(1)}, bf16[2,96,256]{2,1,0:T(8,128)(2,1)S(1)}, u32[]{:S(2)}, u32[]{:S(2)}) collective-permute-start(bf16[2,96,256]{2,1,0:T(8,128)(2,1)S(1)} %get-tuple-element.74), channel_id=1, source_target_pairs={{0,14},{2,12},{4,10},{6,8},{8,6},{10,4},{12,2},{14,0},{1,15},{3,13... | collective-permute-start | bytes 294920 | tf_op jit(solution)/shard_map/ppermute | solution.py:509
  31.7 7.0 %collective-permute-start.6 = (bf16[2,96,256]{2,1,0:T(8,128)(2,1)S(1)}, bf16[2,96,256]{2,1,0:T(8,128)(2,1)S(1)}, u32[]{:S(2)}, u32[]{:S(2)}) collective-permute-start(bf16[2,96,256]{2,1,0:T(8,128)(2,1)S(1)} %get-tuple-element.68), channel_id=1, source_target_pairs={{0,2},{2,0},{4,6},{6,4},{8,10},{10,8},{12,14},{14,12},{1,3},{3,1},... | collective-permute-start | bytes 294920 | tf_op jit(solution)/shard_map/ppermute | solution.py:509
  34.2 5.5 %collective-permute-start.7 = (bf16[2,96,256]{2,1,0:T(8,128)(2,1)S(1)}, bf16[2,96,256]{2,1,0:T(8,128)(2,1)S(1)}, u32[]{:S(2)}, u32[]{:S(2)}) collective-permute-start(bf16[2,96,256]{2,1,0:T(8,128)(2,1)S(1)} %get-tuple-element.70), channel_id=1, source_target_pairs={{0,6},{2,4},{4,2},{6,0},{8,14},{10,12},{12,10},{14,8},{1,7},{3,5},... | collective-permute-start | bytes 294920 | tf_op jit(solution)/shard_map/ppermute | solution.py:509
  34.2 31.9 %slice-start.2 = ((s8[6291456]{0:T(1024)(128)(4,1)}), s8[4194304]{0:T(1024)(128)(4,1)S(1)}, s32[]{:S(2)}) async-start(s8[6291456]{0:T(1024)(128)(4,1)} %bitcast.5), calls=%async_computation.2 | async-start | bytes 8388608
  35.4 30.8 %slice-start.3 = ((s8[6291456]{0:T(1024)(128)(4,1)}), s8[2097152]{0:T(1024)(128)(4,1)S(1)}, s32[]{:S(2)}) async-start(s8[6291456]{0:T(1024)(128)(4,1)} %bitcast.5), calls=%async_computation.3 | async-start | bytes 4194304
  38.2 2.1 %collective-permute-start.11 = (bf16[2,2,48,1024]{3,2,1,0:T(8,128)(2,1)S(1)}, bf16[2,2,48,1024]{3,2,1,0:T(8,128)(2,1)S(1)}, u32[]{:S(2)}, u32[]{:S(2)}) collective-permute-start(bf16[2,2,48,1024]{3,2,1,0:T(8,128)(2,1)S(1)} %collective-permute-done.3.refs_4_), channel_id=1, source_target_pairs={{0,1},{1,0},{2,3},{3,2},{4,5},{5,4},{6,7},{7,6},{8,9},{9,8},{10,11... | collective-permute-start | bytes 1179656 | tf_op jit(solution)/shard_map/ppermute | solution.py:476
  38.2 2.3 %collective-permute-start.12 = (bf16[2,2,48,1024]{3,2,1,0:T(8,128)(2,1)S(1)}, bf16[2,2,48,1024]{3,2,1,0:T(8,128)(2,1)S(1)}, u32[]{:S(2)}, u32[]{:S(2)}) collective-permute-start(bf16[2,2,48,1024]{3,2,1,0:T(8,128)(2,1)S(1)} %collective-permute-done.4.refs_5_), channel_id=1, source_target_pairs={{0,1},{1,0},{2,3},{3,2},{4,5},{5,4},{6,7},{7,6},{8,9},{9,8},{10,11... | collective-permute-start | bytes 1179656 | tf_op jit(solution)/shard_map/ppermute | solution.py:476
  39.8 1.7 %collective-permute-start.13 = (bf16[2,2,48,1024]{3,2,1,0:T(8,128)(2,1)S(1)}, bf16[2,2,48,1024]{3,2,1,0:T(8,128)(2,1)S(1)}, u32[]{:S(2)}, u32[]{:S(2)}) collective-permute-start(bf16[2,2,48,1024]{3,2,1,0:T(8,128)(2,1)S(1)} %collective-permute-done.5.refs_8_), channel_id=1, source_target_pairs={{0,1},{1,0},{2,3},{3,2},{4,5},{5,4},{6,7},{7,6},{8,9},{9,8},{10,11... | collective-permute-start | bytes 1179656 | tf_op jit(solution)/shard_map/ppermute | solution.py:476
  39.8 2.3 %collective-permute-start.14 = (bf16[2,2,48,1024]{3,2,1,0:T(8,128)(2,1)S(1)}, bf16[2,2,48,1024]{3,2,1,0:T(8,128)(2,1)S(1)}, u32[]{:S(2)}, u32[]{:S(2)}) collective-permute-start(bf16[2,2,48,1024]{3,2,1,0:T(8,128)(2,1)S(1)} %collective-permute-done.10.refs_9_), channel_id=1, source_target_pairs={{0,1},{1,0},{2,3},{3,2},{4,5},{5,4},{6,7},{7,6},{8,9},{9,8},{10,11... | collective-permute-start | bytes 1179656 | tf_op jit(solution)/shard_map/ppermute | solution.py:476
  45.8 6.3 %collective-permute-start.15 = (bf16[2,96,256]{2,1,0:T(8,128)(2,1)S(1)}, bf16[2,96,256]{2,1,0:T(8,128)(2,1)S(1)}, u32[]{:S(2)}, u32[]{:S(2)}) collective-permute-start(bf16[2,96,256]{2,1,0:T(8,128)(2,1)S(1)} %get-tuple-element.92), channel_id=1, source_target_pairs={{0,2},{2,0},{4,6},{6,4},{8,10},{10,8},{12,14},{14,12},{1,3},{3,1},... | collective-permute-start | bytes 294920 | tf_op jit(solution)/shard_map/ppermute | solution.py:485
  46.2 7.8 %collective-permute-start.16 = (bf16[2,96,256]{2,1,0:T(8,128)(2,1)S(1)}, bf16[2,96,256]{2,1,0:T(8,128)(2,1)S(1)}, u32[]{:S(2)}, u32[]{:S(2)}) collective-permute-start(bf16[2,96,256]{2,1,0:T(8,128)(2,1)S(1)} %get-tuple-element.93), channel_id=1, source_target_pairs={{0,4},{2,6},{4,0},{6,2},{8,12},{10,14},{12,8},{14,10},{1,5},{3,7},... | collective-permute-start | bytes 294920 | tf_op jit(solution)/shard_map/ppermute | solution.py:485
  46.5 10.6 %collective-permute-start.17 = (bf16[2,96,256]{2,1,0:T(8,128)(2,1)S(1)}, bf16[2,96,256]{2,1,0:T(8,128)(2,1)S(1)}, u32[]{:S(2)}, u32[]{:S(2)}) collective-permute-start(bf16[2,96,256]{2,1,0:T(8,128)(2,1)S(1)} %get-tuple-element.94), channel_id=1, source_target_pairs={{0,6},{2,4},{4,2},{6,0},{8,14},{10,12},{12,10},{14,8},{1,7},{3,5},... | collective-permute-start | bytes 294920 | tf_op jit(solution)/shard_map/ppermute | solution.py:485
  49.4 14.2 %collective-permute-start.18 = (bf16[2,96,256]{2,1,0:T(8,128)(2,1)S(1)}, bf16[2,96,256]{2,1,0:T(8,128)(2,1)S(1)}, u32[]{:S(2)}, u32[]{:S(2)}) collective-permute-start(bf16[2,96,256]{2,1,0:T(8,128)(2,1)S(1)} %get-tuple-element.95), channel_id=1, source_target_pairs={{0,8},{2,10},{4,12},{6,14},{8,0},{10,2},{12,4},{14,6},{1,9},{3,11}... | collective-permute-start | bytes 294920 | tf_op jit(solution)/shard_map/ppermute | solution.py:485
  49.8 16.3 %collective-permute-start.19 = (bf16[2,96,256]{2,1,0:T(8,128)(2,1)S(1)}, bf16[2,96,256]{2,1,0:T(8,128)(2,1)S(1)}, u32[]{:S(2)}, u32[]{:S(2)}) collective-permute-start(bf16[2,96,256]{2,1,0:T(8,128)(2,1)S(1)} %get-tuple-element.96), channel_id=1, source_target_pairs={{0,10},{2,8},{4,14},{6,12},{8,2},{10,0},{12,6},{14,4},{1,11},{3,9}... | collective-permute-start | bytes 294920 | tf_op jit(solution)/shard_map/ppermute | solution.py:485
  52.1 14.1 %collective-permute-start.20 = (bf16[2,96,256]{2,1,0:T(8,128)(2,1)S(1)}, bf16[2,96,256]{2,1,0:T(8,128)(2,1)S(1)}, u32[]{:S(2)}, u32[]{:S(2)}) collective-permute-start(bf16[2,96,256]{2,1,0:T(8,128)(2,1)S(1)} %get-tuple-element.97), channel_id=1, source_target_pairs={{0,12},{2,14},{4,8},{6,10},{8,4},{10,6},{12,0},{14,2},{1,13},{3,15... | collective-permute-start | bytes 294920 | tf_op jit(solution)/shard_map/ppermute | solution.py:485
  54.0 12.1 %collective-permute-start.21 = (bf16[2,96,256]{2,1,0:T(8,128)(2,1)S(1)}, bf16[2,96,256]{2,1,0:T(8,128)(2,1)S(1)}, u32[]{:S(2)}, u32[]{:S(2)}) collective-permute-start(bf16[2,96,256]{2,1,0:T(8,128)(2,1)S(1)} %get-tuple-element.98), channel_id=1, source_target_pairs={{0,14},{2,12},{4,10},{6,8},{8,6},{10,4},{12,2},{14,0},{1,15},{3,13... | collective-permute-start | bytes 294920 | tf_op jit(solution)/shard_map/ppermute | solution.py:485

commit v5 on v4

--- a/solution.py
+++ b/solution.py
@@ -327,30 +327,90 @@
     )(mask, u_own, *arrived)
 
 
-def receiver_kernel(count_col, half, mask, mixing, own, u_own, *refs):
+def copy_quarters(pieces, half_place, turn, matrix, sems):
+    copies = []
+    quarter = matrix.shape[2] // 2
+    for n in range(2):
+        start = (turn ^ n) * quarter
+        for cut in range(len(pieces) // 2):
+            ref = pieces[cut * 2 + n]
+            at = pl.ds(pl.multiple_of(start, 16), ref.shape[2])
+            copies.append(pltpu.make_async_copy(ref, matrix.at[:, :, at, :], sems.at[cut * 2 + n]))
+            copies[-1].start()
+            start = start + ref.shape[2]
+    return copies
+
+
+def stack_other(column, arrived, mask, slot, coefs):
+    strip, columns = arrived[0].shape[1:]
+    vis = columns // 2
+    for d, ref in enumerate(arrived):
+        values = ref[slot] * mask[slot, pl.ds(pl.multiple_of((column ^ d) * strip, strip), strip), :]
+        coefs[0, column ^ d] = values
+        coefs[1, column ^ d] = jnp.concatenate([-values[:, vis:], values[:, :vis]], axis=1)
+
+
+def other_field(coefs, half_place, matrix):
+    rows, width = matrix.shape[1:]
+    left = coefs[:, pl.ds(2 * half_place, 2)].reshape(2 * rows, coefs.shape[3])
+    return dot(left, matrix.reshape(2 * rows, width), 0, 0)
+
+
+def near_kernel(count_col, half, mask, *refs):
     arrived = refs[:count_col]
-    u_other = refs[count_col : -2 * count_col - 5]
-    outs = refs[-2 * count_col - 5 : -5]
-    factors, coefs, field, windowed, sems = refs[-5:]
+    pieces = refs[count_col:-4]
+    near, partial, coefs, sems = refs[-4:]
     column = lax.axis_index("col")
-    place = lax.axis_index("grp") * 2 + lax.axis_index("rep")
-    rows, columns = coefs.shape[2:]
-    vis = columns // 2
-    copies = []
-    for n, ref in enumerate(u_other):
-        cuts = len(u_other) // 4
-        start = (place ^ (n // cuts)) * (rows // 4) + sum(ref.shape[2] for ref in u_other[: n % cuts])
-        at = pl.ds(pl.multiple_of(start, 16), ref.shape[2])
-        copies.append(pltpu.make_async_copy(ref, factors.at[:, :, at, :], sems.at[n]))
-        copies[n].start()
+    group = lax.axis_index("grp")
+    copies = copy_quarters(pieces, group, lax.axis_index("rep"), near, sems)
     for s in range(half):
-        stack_coefficients(column, arrived, vis, s, mask, coefs.at[s])
+        stack_other(column, arrived, mask, s, coefs.at[s])
     for copy in copies:
         copy.wait()
-    strip = arrived[0].shape[1]
     for s in range(half):
-        matrix = factors[:, s].reshape(2 * rows, TS)
-        field[s] = dot(coefs[s].reshape(2 * rows, columns), matrix, 0, 0).astype(jnp.bfloat16)
+        partial[s] = other_field(coefs.at[s], group, near[:, s])
+
+
+def near_products(count_col, half, mask, arrived, pieces):
+    strip, columns = arrived[0].shape[1:]
+    vmem = pl.BlockSpec(memory_space=pltpu.VMEM)
+    return pl.pallas_call(
+        functools.partial(near_kernel, count_col, half),
+        in_specs=[vmem] * (1 + count_col + len(pieces)),
+        out_specs=[vmem] * 2,
+        out_shape=[
+            jax.ShapeDtypeStruct((2, half, 2 * strip, TS), jnp.bfloat16),
+            jax.ShapeDtypeStruct((half, columns, TS), jnp.float32),
+        ],
+        scratch_shapes=[
+            pltpu.VMEM((half, 2, count_col, strip, columns), jnp.bfloat16),
+            pltpu.SemaphoreType.DMA((len(pieces),)),
+        ],
+        compiler_params=pltpu.CompilerParams(vmem_limit_bytes=16 * 2**20),
+        cost_estimate=pl.CostEstimate(
+            flops=8 * half * strip * columns * TS, bytes_accessed=8 * half * strip * TS, transcendentals=0
+        ),
+        name="near_products",
+    )(mask, *arrived, *pieces)
+
+
+def receiver_kernel(count_col, half, mask, mixing, own, u_own, near, partial, *refs):
+    arrived = refs[:count_col]
+    pieces = refs[count_col : -2 * count_col - 6]
+    outs = refs[-2 * count_col - 6 : -6]
+    far, coefs, field, windowed, adjoint, sems = refs[-6:]
+    column = lax.axis_index("col")
+    group = lax.axis_index("grp")
+    strip, columns = arrived[0].shape[1:]
+    rows = adjoint.shape[2]
+    vis = columns // 2
+    copies = copy_quarters(pieces, 1 - group, lax.axis_index("rep"), far, sems)
+    for s in range(half):
+        stack_other(column, arrived, mask, s, coefs.at[s])
+    for copy in copies:
+        copy.wait()
+    for s in range(half):
+        field[s] = (partial[s] + other_field(coefs.at[s], 1 - group, far[:, s])).astype(jnp.bfloat16)
     for s in range(half):
         high = 64
         for lane in range(0, TS, 128):
@@ -367,44 +427,45 @@
                         total = total + mix[4 * p + q : 4 * p + q + 1] * inputs[q]
                     windowed[s, p // 2, pl.ds((p % 2) * vis + row, high), at] = total.astype(jnp.bfloat16)
         for e in range(2):
-            if e == 0:
-                matrix = u_own[:, s].reshape(2 * rows, TS)
-            back = dot(matrix, windowed[s, e], 1, 1)
-            by_real, by_imag = back[:rows], back[rows:]
-            adjoint = jnp.concatenate(
-                [by_real[:, :vis] + by_imag[:, vis:], by_real[:, vis:] - by_imag[:, :vis]], axis=1
-            )
-            coefs[s, 0] = adjoint.astype(jnp.bfloat16) * mask[s]
+            parts = [(u_own, 0)] if e == 0 else [(near, group * 2 * strip), (far, (1 - group) * 2 * strip)]
+            for factors, start in parts:
+                here = factors.shape[2]
+                back = dot(factors[:, s].reshape(2 * here, TS), windowed[s, e], 1, 1)
+                by_real, by_imag = back[:here], back[here:]
+                values = jnp.concatenate(
+                    [by_real[:, :vis] + by_imag[:, vis:], by_real[:, vis:] - by_imag[:, :vis]], axis=1
+                )
+                at = pl.ds(start if e == 0 else pl.multiple_of(start, strip), here)
+                adjoint[s, e, at, :] = values.astype(jnp.bfloat16) * mask[s, at, :]
             for d in range(count_col):
                 start = pl.multiple_of((column ^ d) * strip, strip)
-                outs[2 * d + e][s] = coefs[s, 0, pl.ds(start, strip), :]
-            if e == 0:
-                matrix = factors[:, s].reshape(2 * rows, TS)
-
-
-def receiver_products(count_col, half, mask, mixing, own, arrived, u_own, u_other):
+                outs[2 * d + e][s] = adjoint[s, e, pl.ds(start, strip), :]
+
+
+def receiver_products(count_col, half, mask, mixing, own, arrived, u_own, near, partial, pieces):
     strip, columns = arrived[0].shape[1:]
     rows = u_own.shape[2]
     vmem = pl.BlockSpec(memory_space=pltpu.VMEM)
     out = jax.ShapeDtypeStruct((half, strip, columns), jnp.bfloat16)
     return pl.pallas_call(
         functools.partial(receiver_kernel, count_col, half),
-        in_specs=[vmem] * (4 + count_col + len(u_other)),
+        in_specs=[vmem] * (6 + count_col + len(pieces)),
         out_specs=[vmem] * (2 * count_col),
         out_shape=[out] * (2 * count_col),
         scratch_shapes=[
-            pltpu.VMEM((2, half, rows, TS), jnp.bfloat16),
-            pltpu.VMEM((half, 2, rows, columns), jnp.bfloat16),
+            pltpu.VMEM((2, half, 2 * strip, TS), jnp.bfloat16),
+            pltpu.VMEM((half, 2, count_col, strip, columns), jnp.bfloat16),
             pltpu.VMEM((half, columns, TS), jnp.bfloat16),
             pltpu.VMEM((half, 2, columns, TS), jnp.bfloat16),
-            pltpu.SemaphoreType.DMA((len(u_other),)),
+            pltpu.VMEM((half, 2, rows, columns), jnp.bfloat16),
+            pltpu.SemaphoreType.DMA((len(pieces),)),
         ],
         compiler_params=pltpu.CompilerParams(vmem_limit_bytes=24 * 2**20),
         cost_estimate=pl.CostEstimate(
             flops=12 * half * rows * columns * TS, bytes_accessed=8 * half * rows * TS, transcendentals=0
         ),
         name="receiver_products",
-    )(mask, mixing, own, u_own, *arrived, *u_other)
+    )(mask, mixing, own, u_own, near, partial, *arrived, *pieces)
 
 
 def update_kernel(count_col, half, owners, *refs):
@@ -514,22 +575,27 @@
     )
     first[0], _ = lax.optimization_barrier((first[0], outgoing[0]))
     second = [swap(first[0], "grp")]
-    for offset in (6, 4, 2):
+    for offset in (4, 7, 2):
         arrived[offset] = move(offset, arrived[offset])
     held = lax.optimization_barrier(tuple(arrived + first + [u_here, mixing] + second))
     arrived, (*first, u_here, mixing, head) = list(held[: 2 * count_col]), held[2 * count_col :]
     second = [head, swap(first[1], "grp")]
-    for offset in (7, 5, 3, 1):
+    for offset in (5, 6, 3, 1):
         arrived[offset] = move(offset, arrived[offset])
-    tied = lax.optimization_barrier(tuple(first + [arrived[n] for n in (7, 5)]))
+    tied = lax.optimization_barrier(tuple(first + [arrived[n] for n in (5,)]))
     first = list(tied[:2])
     mates = [swap(piece, "rep") for piece in first]
     own = own_field(count_col, half, mask, u_here, arrived[::2])
     held = lax.optimization_barrier(tuple(arrived + first + second + [u_here, own]))
     arrived, (*pieces, u_here, own) = list(held[: 2 * count_col]), held[2 * count_col :]
     first, second = pieces[:2], pieces[2:4]
-    gathered = first + mates + second + [swap(piece, "rep") for piece in second]
-    back = receiver_products(count_col, half, mask, mixing, own, arrived[1::2], u_here, gathered)
+    near, partial = near_products(
+        count_col, half, mask, arrived[1::2], [first[0], mates[0], first[1], mates[1]]
+    )
+    pieces = []
+    for piece in second:
+        pieces.extend([piece, swap(piece, "rep")])
+    back = receiver_products(count_col, half, mask, mixing, own, arrived[1::2], u_here, near, partial, pieces)
     returned = exchange(back, count_col)
     return update_products(count_col, half, owners, returned, focus_here, v_here)
 
@@ -541,7 +607,7 @@
         and lax.axis_size("grp") == 2
         and lax.axis_size("rep") == 2
         and focusing.shape[0] == 1
-        and count_col & (count_col - 1) == 0
+        and count_col == 4
         and u_factors.shape[2] % 2 == 0
         and u_factors.shape[2] * count_col == NR // TS
         and focusing.shape[2] % 128 == 0

time: 70.8 us -> 69.6 us (0.983)
  waiting for transfers between devices: 21.1 us -> 19.6 us
  Pallas kernels: 17.3 us -> 18.1 us
    ppermute x8, waiting for transfers between devices: 3.35 us -> 2.19 us  [swap(): return lax.ppermute(array, axis, [(0, 1), (1, 0)])]
    pallas_call x0 -> x1, Pallas kernels: none -> 1.12 us  [near_products(): pl.pallas_call(functools.partial(near_kernel, count_col, half), in_specs=...]
  transfers between devices with their start and end apart: 22 -> 22, of which waited for: 10 -> 10; matrix products, arithmetic and copies ran while one was open for 0% -> 0% of each run, Pallas kernels for 15% -> 16%
where the time goes in v5:
time: 69.6 us; the launch traced here: 68.4 us
  starting transfers between devices  28.5 us (41%)
  waiting for transfers between devices  19.6 us (28%)
  Pallas kernels  18.1 us (26%)
  local copies, waits for them, and re-layouts  2.06 us (3%)
    ppermute x7, starting transfers between devices, exchange(): lax.ppermute(arrays[offset], ('col', 'freq'), [(i, i ^ offset) for i in r...  11.2 us
    ppermute x7, starting transfers between devices, move(): lax.ppermute(payload, ('col', 'freq'), [(i, i ^ offset) for i in range(2...  11.1 us
    ppermute x7, waiting for transfers between devices, exchange(): lax.ppermute(arrays[offset], ('col', 'freq'), [(i, i ^ offset) for i in r...  9.35 us
    ppermute x7, waiting for transfers between devices, move(): lax.ppermute(payload, ('col', 'freq'), [(i, i ^ offset) for i in range(2...  8.07 us
    pallas_call x1, Pallas kernels, forward_products(): pl.pallas_call(functools.partial(forward_kernel, count_col, half), in_spe...  7.48 us
    ppermute x8, starting transfers between devices, swap(): return lax.ppermute(array, axis, [(0, 1), (1, 0)])  6.23 us
    pallas_call x1, Pallas kernels, receiver_products(): pl.pallas_call(functools.partial(receiver_kernel, count_col, half), in_sp...  3.45 us
    pallas_call x1, Pallas kernels, update_products(): pl.pallas_call(functools.partial(update_kernel, count_col, half), in_spec...  3.45 us
  transfers between devices with their start and end apart: 22, of which 10 were waited for; matrix products, arithmetic and copies ran while one was open for 0% of the time, Pallas kernels for 16%

profile of v5, /device:TPU:0, one launch (start us, length us, event | category | flops | bytes accessed | tf_op | source)
XLA Modules:
  0.0 68.4 jit_solution(8325438877180237235)
XLA Ops:
  0.0 1.2 %dynamic-slice_bitcast_fusion = bf16[2,2,96,1024]{3,2,1,0:T(8,128)(2,1)S(1)} fusion(bf16[1,2,4,384,1024]{4,3,2,1,0:T(8,128)(2,1)} %u_factors, s32[]{:T(128)S(6)} %select_n.6, s32[]{:T(128)S(6)} %select_n.7), kind=kLoop, calls=%fused_computation | loop fusion | bytes 1572872 | tf_op jit(solution)/shard_map/reshape | solution.py:566
  1.2 0.0 slice-start
  1.2 0.1 fusion
  1.3 3.0 %collective-permute-start.3 = (bf16[2,2,48,1024]{3,2,1,0:T(8,128)(2,1)S(1)}, bf16[2,2,48,1024]{3,2,1,0:T(8,128)(2,1)S(1)}, u32[]{:S(2)}, u32[]{:S(2)}) collective-permute-start(bf16[2,2,48,1024]{3,2,1,0:T(8,128)(2,1)S(1)} %get-tuple-element.106), channel_id=1, source_target_pairs={{0,2},{2,0},{1,3},{3,1},{4,6},{6,4},{5,7},{7,5},{8,10},{10,8},{9,1... | collective-permute-start | bytes 1179656 | tf_op jit(solution)/shard_map/ppermute | solution.py:537
  4.3 0.0 slice-start.1
  4.3 0.0 copy-start
  4.3 0.0 copy-start.1
  4.3 0.1 collective-permute-start.4
  4.4 0.8 %copy-done.3 = s32[16]{0:T(128)S(1)} copy-done((s32[16]{0:T(128)S(1)}, s32[16]{0:T(128)}, u32[]{:S(2)}) %copy-start.3) | copy-done | bytes 88
  5.2 7.5 %forward_products.1 = (bf16[2,96,256]{2,1,0:T(8,128)(2,1)S(1)}, bf16[2,96,256]{2,1,0:T(8,128)(2,1)S(1)}, bf16[2,96,256]{2,1,0:T(8,128)(2,1)S(1)}, bf16[2,96,256]...) custom-call(s32[16]{0:T(128)S(1)} %copy-done.3, ...), custom_call_target="tpu_custom_call" | custom-call | flops 1610612736 | bytes 10485760 | tf_op jit(solution)/shard_map/forward_products/pallas_call | solution.py:226
  12.7 1.5 %collective-permute-done.3.refs_4_ = bf16[2,2,48,1024]{3,2,1,0:T(8,128)(2,1)S(1)} collective-permute-done((bf16[2,2,48,1024]{3,2,1,0:T(8,128)(2,1)S(1)}, bf16[2,2,48,1024]{3,2,1,0:T(8,128)(2,1)S(1)}, u32[]{:S(2)}, u32[]{:S(2)}) %collective-permute-start.3) | collective-permute-done | bytes 393248 | tf_op jit(solution)/shard_map/ppermute | solution.py:537
  14.2 2.1 %collective-permute-start.5 = (bf16[2,2,48,1024]{3,2,1,0:T(8,128)(2,1)S(1)}, bf16[2,2,48,1024]{3,2,1,0:T(8,128)(2,1)S(1)}, u32[]{:S(2)}, u32[]{:S(2)}) collective-permute-start(bf16[2,2,48,1024]{3,2,1,0:T(8,128)(2,1)S(1)} %collective-permute-done.3.refs_4_), channel_id=1, source_target_pairs={{0,16},{16,0},{1,17},{17,1},{2,18},{18,2},{3,19},{19,3},{4,20},{20... | collective-permute-start | bytes 1179656 | tf_op jit(solution)/shard_map/ppermute | solution.py:537
  16.3 1.6 %collective-permute-start = (bf16[2,96,256]{2,1,0:T(8,128)(2,1)S(1)}, bf16[2,96,256]{2,1,0:T(8,128)(2,1)S(1)}, u32[]{:S(2)}, u32[]{:S(2)}) collective-permute-start(bf16[2,96,256]{2,1,0:T(8,128)(2,1)S(1)} %get-tuple-element.59), channel_id=1, source_target_pairs={{0,4},{2,6},{4,0},{6,2},{8,12},{10,14},{12,8},{14,10},{1,5},{3,7},... | collective-permute-start | bytes 294920 | tf_op jit(solution)/shard_map/ppermute | solution.py:570
  17.9 2.6 %collective-permute-start.1 = (bf16[2,96,256]{2,1,0:T(8,128)(2,1)S(1)}, bf16[2,96,256]{2,1,0:T(8,128)(2,1)S(1)}, u32[]{:S(2)}, u32[]{:S(2)}) collective-permute-start(bf16[2,96,256]{2,1,0:T(8,128)(2,1)S(1)} %get-tuple-element.61), channel_id=1, source_target_pairs={{0,8},{2,10},{4,12},{6,14},{8,0},{10,2},{12,4},{14,6},{1,9},{3,11}... | collective-permute-start | bytes 294920 | tf_op jit(solution)/shard_map/ppermute | solution.py:570
  20.5 1.1 %collective-permute-start.2 = (bf16[2,96,256]{2,1,0:T(8,128)(2,1)S(1)}, bf16[2,96,256]{2,1,0:T(8,128)(2,1)S(1)}, u32[]{:S(2)}, u32[]{:S(2)}) collective-permute-start(bf16[2,96,256]{2,1,0:T(8,128)(2,1)S(1)} %get-tuple-element.64), channel_id=1, source_target_pairs={{0,14},{2,12},{4,10},{6,8},{8,6},{10,4},{12,2},{14,0},{1,15},{3,13... | collective-permute-start | bytes 294920 | tf_op jit(solution)/shard_map/ppermute | solution.py:570
  21.6 0.0 slice-done
  21.6 0.0 slice-done.1
  21.6 0.0 copy-done
  21.6 0.0 copy-done.1
  21.6 0.0 copy-done.2
  21.6 1.5 %prepare.1 = (bf16[2,2,384,1024]{3,2,1,0:T(8,128)(2,1)S(1)}, f32[2,16,1024]{2,1,0:T(8,128)S(1)}, bf16[2,384,256]{2,1,0:T(8,128)(2,1)S(1)}) custom-call(s32[16]{0:T(128)S(1)} %copy-done.3, s32[16,16]{1,0:T(8,128)S(1)} %copy-done.2, s32[16,1,1024]{2,1,0:T(1,128)S(1)} %bitcast.7, bf16[2,48,512]{2,1,0:T(8,128)(2,1)S(1)} %copy-done, ...), custom_call_target="tpu_custom_call" | custom-call | bytes 6291456 | tf_op jit(solution)/shard_map/prepare/pallas_call | solution.py:272
  23.2 0.0 collective-permute-done.refs_1_
  23.2 2.3 %collective-permute-done.1.refs_2_ = bf16[2,96,256]{2,1,0:T(8,128)(2,1)S(1)} collective-permute-done((bf16[2,96,256]{2,1,0:T(8,128)(2,1)S(1)}, bf16[2,96,256]{2,1,0:T(8,128)(2,1)S(1)}, u32[]{:S(2)}, u32[]{:S(2)}) %collective-permute-start.1) | collective-permute-done | bytes 98336 | tf_op jit(solution)/shard_map/ppermute | solution.py:570
  25.5 2.4 %collective-permute-done.2.refs_3_ = bf16[2,96,256]{2,1,0:T(8,128)(2,1)S(1)} collective-permute-done((bf16[2,96,256]{2,1,0:T(8,128)(2,1)S(1)}, bf16[2,96,256]{2,1,0:T(8,128)(2,1)S(1)}, u32[]{:S(2)}, u32[]{:S(2)}) %collective-permute-start.2) | collective-permute-done | bytes 98336 | tf_op jit(solution)/shard_map/ppermute | solution.py:570
  27.9 0.0 collective-permute-done.4.refs_6_
  27.9 0.0 collective-permute-done.5.refs_4_
  27.9 0.5 collective-permute-start.10
  28.4 1.6 %collective-permute-start.8 = (bf16[2,96,256]{2,1,0:T(8,128)(2,1)S(1)}, bf16[2,96,256]{2,1,0:T(8,128)(2,1)S(1)}, u32[]{:S(2)}, u32[]{:S(2)}) collective-permute-start(bf16[2,96,256]{2,1,0:T(8,128)(2,1)S(1)} %get-tuple-element.74), channel_id=1, source_target_pairs={{0,10},{2,8},{4,14},{6,12},{8,2},{10,0},{12,6},{14,4},{1,11},{3,9}... | collective-permute-start | bytes 294920 | tf_op jit(solution)/shard_map/ppermute | solution.py:570
  30.0 0.8 %collective-permute-start.9 = (bf16[2,96,256]{2,1,0:T(8,128)(2,1)S(1)}, bf16[2,96,256]{2,1,0:T(8,128)(2,1)S(1)}, u32[]{:S(2)}, u32[]{:S(2)}) collective-permute-start(bf16[2,96,256]{2,1,0:T(8,128)(2,1)S(1)} %get-tuple-element.75), channel_id=1, source_target_pairs={{0,12},{2,14},{4,8},{6,10},{8,4},{10,6},{12,0},{14,2},{1,13},{3,15... | collective-permute-start | bytes 294920 | tf_op jit(solution)/shard_map/ppermute | solution.py:570
  30.9 2.2 %collective-permute-start.6 = (bf16[2,96,256]{2,1,0:T(8,128)(2,1)S(1)}, bf16[2,96,256]{2,1,0:T(8,128)(2,1)S(1)}, u32[]{:S(2)}, u32[]{:S(2)}) collective-permute-start(bf16[2,96,256]{2,1,0:T(8,128)(2,1)S(1)} %get-tuple-element.70), channel_id=1, source_target_pairs={{0,2},{2,0},{4,6},{6,4},{8,10},{10,8},{12,14},{14,12},{1,3},{3,1},... | collective-permute-start | bytes 294920 | tf_op jit(solution)/shard_map/ppermute | solution.py:570
  33.1 1.0 %collective-permute-start.7 = (bf16[2,96,256]{2,1,0:T(8,128)(2,1)S(1)}, bf16[2,96,256]{2,1,0:T(8,128)(2,1)S(1)}, u32[]{:S(2)}, u32[]{:S(2)}) collective-permute-start(bf16[2,96,256]{2,1,0:T(8,128)(2,1)S(1)} %get-tuple-element.72), channel_id=1, source_target_pairs={{0,6},{2,4},{4,2},{6,0},{8,14},{10,12},{12,10},{14,8},{1,7},{3,5},... | collective-permute-start | bytes 294920 | tf_op jit(solution)/shard_map/ppermute | solution.py:570
  34.2 1.8 %collective-permute-done.8.refs_2_ = bf16[2,96,256]{2,1,0:T(8,128)(2,1)S(1)} collective-permute-done((bf16[2,96,256]{2,1,0:T(8,128)(2,1)S(1)}, bf16[2,96,256]{2,1,0:T(8,128)(2,1)S(1)}, u32[]{:S(2)}, u32[]{:S(2)}) %collective-permute-start.8) | collective-permute-done | bytes 98336 | tf_op jit(solution)/shard_map/ppermute | solution.py:570
  36.0 0.0 collective-permute-start.11
  36.0 0.6 collective-permute-done.9.refs_3_
  36.6 0.0 collective-permute-start.12
  36.6 1.1 %own_field.1.own = bf16[2,256,1024]{2,1,0:T(8,128)(2,1)S(1)} custom-call(bf16[2,384,256]{2,1,0:T(8,128)(2,1)S(1)} %get-tuple-element.57.mask, bf16[2,2,384,1024]{3,2,1,0:T(8,128)(2,1)S(1)} %get-tuple-element.84.u_own, bf16[2,96,256]{2,1,0:T(8,128)(2,1)S(1)} %get-tuple-element.69.refs_0_, bf16[2,96,256]{2,1,0:T(8,128)(2,1)S(1)} %collective-permute-done.refs_1_, ...), custom_call_target="tpu_custom_call" | custom-call | flops 805306368 | bytes 1572864 | tf_op jit(solution)/shard_map/own_field/pallas_call | solution.py:316
  37.7 0.0 collective-permute-done.6.refs_0_
  37.7 0.9 %collective-permute-done.7.refs_1_ = bf16[2,96,256]{2,1,0:T(8,128)(2,1)S(1)} collective-permute-done((bf16[2,96,256]{2,1,0:T(8,128)(2,1)S(1)}, bf16[2,96,256]{2,1,0:T(8,128)(2,1)S(1)}, u32[]{:S(2)}, u32[]{:S(2)}) %collective-permute-start.7) | collective-permute-done | bytes 98336 | tf_op jit(solution)/shard_map/ppermute | solution.py:570
  38.6 0.0 collective-permute-done.10.refs_6_
  38.6 0.0 collective-permute-start.13
  38.6 0.5 collective-permute-start.14
  39.2 0.0 collective-permute-done.11.refs_5_
  39.2 0.0 collective-permute-done.12.refs_7_
  39.2 1.1 %near_products.1 = (bf16[2,2,192,1024]{3,2,1,0:T(8,128)(2,1)S(1)}, f32[2,256,1024]{2,1,0:T(8,128)S(1)}) custom-call(bf16[2,384,256]{2,1,0:T(8,128)(2,1)S(1)} %get-tuple-element.57.mask, bf16[2,96,256]{2,1,0:T(8,128)(2,1)S(1)} %collective-permute-done.6.refs_0_, bf16[2,96,256]{2,1,0:T(8,128)(2,1)S(1)} %collective-permute-done.7.refs_1_, ...), custom_call_target="tpu_custom_call" | custom-call | flops 402653184 | bytes 1572864 | tf_op jit(solution)/shard_map/near_products/pallas_call | solution.py:377
  40.3 0.1 collective-permute-done.13.refs_5_
  40.4 0.6 collective-permute-done.14.refs_7_
  40.9 3.4 %receiver_products.1 = (bf16[2,96,256]{2,1,0:T(8,128)(2,1)S(1)}, bf16[2,96,256]{2,1,0:T(8,128)(2,1)S(1)}, bf16[2,96,256]{2,1,0:T(8,128)(2,1)S(1)}, bf16[2,96,256...) custom-call(bf16[2,384,256]{2,1,0:T(8,128)(2,1)S(1)} %get-tuple-elem, ...), custom_call_target="tpu_custom_call" | custom-call | flops 2415919104 | bytes 6291456 | tf_op jit(solution)/shard_map/receiver_products/pallas_call | solution.py:450
  44.4 0.8 %collective-permute-start.15 = (bf16[2,96,256]{2,1,0:T(8,128)(2,1)S(1)}, bf16[2,96,256]{2,1,0:T(8,128)(2,1)S(1)}, u32[]{:S(2)}, u32[]{:S(2)}) collective-permute-start(bf16[2,96,256]{2,1,0:T(8,128)(2,1)S(1)} %get-tuple-element.96), channel_id=1, source_target_pairs={{0,2},{2,0},{4,6},{6,4},{8,10},{10,8},{12,14},{14,12},{1,3},{3,1},... | collective-permute-start | bytes 294920 | tf_op jit(solution)/shard_map/ppermute | solution.py:546
  45.2 1.0 %collective-permute-start.16 = (bf16[2,96,256]{2,1,0:T(8,128)(2,1)S(1)}, bf16[2,96,256]{2,1,0:T(8,128)(2,1)S(1)}, u32[]{:S(2)}, u32[]{:S(2)}) collective-permute-start(bf16[2,96,256]{2,1,0:T(8,128)(2,1)S(1)} %get-tuple-element.97), channel_id=1, source_target_pairs={{0,4},{2,6},{4,0},{6,2},{8,12},{10,14},{12,8},{14,10},{1,5},{3,7},... | collective-permute-start | bytes 294920 | tf_op jit(solution)/shard_map/ppermute | solution.py:546
  46.2 1.7 %collective-permute-start.17 = (bf16[2,96,256]{2,1,0:T(8,128)(2,1)S(1)}, bf16[2,96,256]{2,1,0:T(8,128)(2,1)S(1)}, u32[]{:S(2)}, u32[]{:S(2)}) collective-permute-start(bf16[2,96,256]{2,1,0:T(8,128)(2,1)S(1)} %get-tuple-element.98), channel_id=1, source_target_pairs={{0,6},{2,4},{4,2},{6,0},{8,14},{10,12},{12,10},{14,8},{1,7},{3,5},... | collective-permute-start | bytes 294920 | tf_op jit(solution)/shard_map/ppermute | solution.py:546
  47.9 1.4 %collective-permute-start.18 = (bf16[2,96,256]{2,1,0:T(8,128)(2,1)S(1)}, bf16[2,96,256]{2,1,0:T(8,128)(2,1)S(1)}, u32[]{:S(2)}, u32[]{:S(2)}) collective-permute-start(bf16[2,96,256]{2,1,0:T(8,128)(2,1)S(1)} %get-tuple-element.99), channel_id=1, source_target_pairs={{0,8},{2,10},{4,12},{6,14},{8,0},{10,2},{12,4},{14,6},{1,9},{3,11}... | collective-permute-start | bytes 294920 | tf_op jit(solution)/shard_map/ppermute | solution.py:546
  49.4 1.7 %collective-permute-start.19 = (bf16[2,96,256]{2,1,0:T(8,128)(2,1)S(1)}, bf16[2,96,256]{2,1,0:T(8,128)(2,1)S(1)}, u32[]{:S(2)}, u32[]{:S(2)}) collective-permute-start(bf16[2,96,256]{2,1,0:T(8,128)(2,1)S(1)} %get-tuple-element.100), channel_id=1, source_target_pairs={{0,10},{2,8},{4,14},{6,12},{8,2},{10,0},{12,6},{14,4},{1,11},{3,9}... | collective-permute-start | bytes 294920 | tf_op jit(solution)/shard_map/ppermute | solution.py:546
  51.1 0.0 collective-permute-done.15.refs_1_
  51.1 2.5 %collective-permute-start.20 = (bf16[2,96,256]{2,1,0:T(8,128)(2,1)S(1)}, bf16[2,96,256]{2,1,0:T(8,128)(2,1)S(1)}, u32[]{:S(2)}, u32[]{:S(2)}) collective-permute-start(bf16[2,96,256]{2,1,0:T(8,128)(2,1)S(1)} %get-tuple-element.101), channel_id=1, source_target_pairs={{0,12},{2,14},{4,8},{6,10},{8,4},{10,6},{12,0},{14,2},{1,13},{3,15... | collective-permute-start | bytes 294920 | tf_op jit(solution)/shard_map/ppermute | solution.py:546
  53.6 0.0 collective-permute-done.16.refs_2_
  53.6 2.0 %collective-permute-start.21 = (bf16[2,96,256]{2,1,0:T(8,128)(2,1)S(1)}, bf16[2,96,256]{2,1,0:T(8,128)(2,1)S(1)}, u32[]{:S(2)}, u32[]{:S(2)}) collective-permute-start(bf16[2,96,256]{2,1,0:T(8,128)(2,1)S(1)} %get-tuple-element.102), channel_id=1, source_target_pairs={{0,14},{2,12},{4,10},{6,8},{8,6},{10,4},{12,2},{14,0},{1,15},{3,13... | collective-permute-start | bytes 294920 | tf_op jit(solution)/shard_map/ppermute | solution.py:546
  55.6 0.0 collective-permute-done.17.refs_3_
  55.6 6.9 %collective-permute-done.18.refs_4_ = bf16[2,96,256]{2,1,0:T(8,128)(2,1)S(1)} collective-permute-done((bf16[2,96,256]{2,1,0:T(8,128)(2,1)S(1)}, bf16[2,96,256]{2,1,0:T(8,128)(2,1)S(1)}, u32[]{:S(2)}, u32[]{:S(2)}) %collective-permute-start.18) | collective-permute-done | bytes 98336 | tf_op jit(solution)/shard_map/ppermute | solution.py:546
  62.6 2.4 %collective-permute-done.19.refs_5_ = bf16[2,96,256]{2,1,0:T(8,128)(2,1)S(1)} collective-permute-done((bf16[2,96,256]{2,1,0:T(8,128)(2,1)S(1)}, bf16[2,96,256]{2,1,0:T(8,128)(2,1)S(1)}, u32[]{:S(2)}, u32[]{:S(2)}) %collective-permute-start.19) | collective-permute-done | bytes 98336 | tf_op jit(solution)/shard_map/ppermute | solution.py:546
  64.9 0.0 collective-permute-done.20.refs_6_
  64.9 0.0 collective-permute-done.21.refs_7_
  64.9 0.0 slice-done.2
  65.0 0.0 slice-done.3
  65.0 3.4 %update_products.1 = f32[1,2,128,4096]{3,2,1,0:T(8,128)} custom-call(s32[16]{0:T(128)S(1)} %copy-done.3, bf16[2,96,256]{2,1,0:T(8,128)(2,1)S(1)} %get-tuple-element.95.refs_0_, bf16[2,96,256]{2,1,0:T(8,128)(2,1)S(1)} %collective-permute-done.15.refs_1_, bf16[2,96,256]{2,1,0:T(8,128)(2,1)S(1)} %collective-permute-done.16.refs_2_, ...), custom_call_target="tpu_custom_call" | custom-call | flops 1610612736 | bytes 14680064 | tf_op jit(solution)/shard_map/update_products/pallas_call | solution.py:515
  (6 shorter events, 0.0 us)
Async XLA Ops:
  1.2 20.4 %slice-start = ((s8[6291456]{0:T(1024)(128)(4,1)}), s8[4194304]{0:T(1024)(128)(4,1)S(1)}, s32[]{:S(2)}) async-start(s8[6291456]{0:T(1024)(128)(4,1)} %bitcast.3), calls=%async_computation | async-start | bytes 8388608
  1.3 12.9 %collective-permute-start.3 = (bf16[2,2,48,1024]{3,2,1,0:T(8,128)(2,1)S(1)}, bf16[2,2,48,1024]{3,2,1,0:T(8,128)(2,1)S(1)}, u32[]{:S(2)}, u32[]{:S(2)}) collective-permute-start(bf16[2,2,48,1024]{3,2,1,0:T(8,128)(2,1)S(1)} %get-tuple-element.106), channel_id=1, source_target_pairs={{0,2},{2,0},{1,3},{3,1},{4,6},{6,4},{5,7},{7,5},{8,10},{10,8},{9,1... | collective-permute-start | bytes 1179656 | tf_op jit(solution)/shard_map/ppermute | solution.py:537
  4.3 17.4 %slice-start.1 = ((s8[6291456]{0:T(1024)(128)(4,1)}), s8[2097152]{0:T(1024)(128)(4,1)S(1)}, s32[]{:S(2)}) async-start(s8[6291456]{0:T(1024)(128)(4,1)} %bitcast.3), calls=%async_computation.1 | async-start | bytes 4194304
  4.3 17.4 %copy-start = (bf16[2,48,512]{2,1,0:T(8,128)(2,1)S(1)}, bf16[2,48,512]{2,1,0:T(8,128)(2,1)}, u32[]{:S(2)}) copy-start(bf16[2,48,512]{2,1,0:T(8,128)(2,1)} %constant.24.clone.table) | copy-start | bytes 294916
  4.3 17.4 %copy-start.1 = (s32[16384]{0:T(1024)S(1)}, s32[16384]{0:T(1024)}, u32[]{:S(2)}) copy-start(s32[16384]{0:T(1024)} %param.12) | copy-start | bytes 196612
  4.3 17.4 %copy-start.2 = (s32[16,16]{1,0:T(8,128)S(1)}, s32[16,16]{1,0:T(8,128)}, u32[]{:S(2)}) copy-start(s32[16,16]{1,0:T(8,128)} %ranks.1) | copy-start | bytes 3076
  4.3 23.6 %collective-permute-start.4 = (bf16[2,2,48,1024]{3,2,1,0:T(8,128)(2,1)S(1)}, bf16[2,2,48,1024]{3,2,1,0:T(8,128)(2,1)S(1)}, u32[]{:S(2)}, u32[]{:S(2)}) collective-permute-start(bf16[2,2,48,1024]{3,2,1,0:T(8,128)(2,1)S(1)} %get-tuple-element.105), channel_id=1, source_target_pairs={{0,2},{2,0},{1,3},{3,1},{4,6},{6,4},{5,7},{7,5},{8,10},{10,8},{9,1... | collective-permute-start | bytes 1179656 | tf_op jit(solution)/shard_map/ppermute | solution.py:537
  4.4 0.8 %copy-start.3 = (s32[16]{0:T(128)S(1)}, s32[16]{0:T(128)}, u32[]{:S(2)}) copy-start(s32[16]{0:T(128)} %owners.3) | copy-start | bytes 196
  14.2 13.7 %collective-permute-start.5 = (bf16[2,2,48,1024]{3,2,1,0:T(8,128)(2,1)S(1)}, bf16[2,2,48,1024]{3,2,1,0:T(8,128)(2,1)S(1)}, u32[]{:S(2)}, u32[]{:S(2)}) collective-permute-start(bf16[2,2,48,1024]{3,2,1,0:T(8,128)(2,1)S(1)} %collective-permute-done.3.refs_4_), channel_id=1, source_target_pairs={{0,16},{16,0},{1,17},{17,1},{2,18},{18,2},{3,19},{19,3},{4,20},{20... | collective-permute-start | bytes 1179656 | tf_op jit(solution)/shard_map/ppermute | solution.py:537
  16.3 6.9 %collective-permute-start = (bf16[2,96,256]{2,1,0:T(8,128)(2,1)S(1)}, bf16[2,96,256]{2,1,0:T(8,128)(2,1)S(1)}, u32[]{:S(2)}, u32[]{:S(2)}) collective-permute-start(bf16[2,96,256]{2,1,0:T(8,128)(2,1)S(1)} %get-tuple-element.59), channel_id=1, source_target_pairs={{0,4},{2,6},{4,0},{6,2},{8,12},{10,14},{12,8},{14,10},{1,5},{3,7},... | collective-permute-start | bytes 294920 | tf_op jit(solution)/shard_map/ppermute | solution.py:570
  17.9 7.6 %collective-permute-start.1 = (bf16[2,96,256]{2,1,0:T(8,128)(2,1)S(1)}, bf16[2,96,256]{2,1,0:T(8,128)(2,1)S(1)}, u32[]{:S(2)}, u32[]{:S(2)}) collective-permute-start(bf16[2,96,256]{2,1,0:T(8,128)(2,1)S(1)} %get-tuple-element.61), channel_id=1, source_target_pairs={{0,8},{2,10},{4,12},{6,14},{8,0},{10,2},{12,4},{14,6},{1,9},{3,11}... | collective-permute-start | bytes 294920 | tf_op jit(solution)/shard_map/ppermute | solution.py:570
  20.5 7.4 %collective-permute-start.2 = (bf16[2,96,256]{2,1,0:T(8,128)(2,1)S(1)}, bf16[2,96,256]{2,1,0:T(8,128)(2,1)S(1)}, u32[]{:S(2)}, u32[]{:S(2)}) collective-permute-start(bf16[2,96,256]{2,1,0:T(8,128)(2,1)S(1)} %get-tuple-element.64), channel_id=1, source_target_pairs={{0,14},{2,12},{4,10},{6,8},{8,6},{10,4},{12,2},{14,0},{1,15},{3,13... | collective-permute-start | bytes 294920 | tf_op jit(solution)/shard_map/ppermute | solution.py:570
  27.9 10.8 %collective-permute-start.10 = (bf16[2,2,48,1024]{3,2,1,0:T(8,128)(2,1)S(1)}, bf16[2,2,48,1024]{3,2,1,0:T(8,128)(2,1)S(1)}, u32[]{:S(2)}, u32[]{:S(2)}) collective-permute-start(bf16[2,2,48,1024]{3,2,1,0:T(8,128)(2,1)S(1)} %collective-permute-done.4.refs_6_), channel_id=1, source_target_pairs={{0,16},{16,0},{1,17},{17,1},{2,18},{18,2},{3,19},{19,3},{4,20},{20... | collective-permute-start | bytes 1179656 | tf_op jit(solution)/shard_map/ppermute | solution.py:537
  28.4 7.6 %collective-permute-start.8 = (bf16[2,96,256]{2,1,0:T(8,128)(2,1)S(1)}, bf16[2,96,256]{2,1,0:T(8,128)(2,1)S(1)}, u32[]{:S(2)}, u32[]{:S(2)}) collective-permute-start(bf16[2,96,256]{2,1,0:T(8,128)(2,1)S(1)} %get-tuple-element.74), channel_id=1, source_target_pairs={{0,10},{2,8},{4,14},{6,12},{8,2},{10,0},{12,6},{14,4},{1,11},{3,9}... | collective-permute-start | bytes 294920 | tf_op jit(solution)/shard_map/ppermute | solution.py:570
  30.0 6.6 %collective-permute-start.9 = (bf16[2,96,256]{2,1,0:T(8,128)(2,1)S(1)}, bf16[2,96,256]{2,1,0:T(8,128)(2,1)S(1)}, u32[]{:S(2)}, u32[]{:S(2)}) collective-permute-start(bf16[2,96,256]{2,1,0:T(8,128)(2,1)S(1)} %get-tuple-element.75), channel_id=1, source_target_pairs={{0,12},{2,14},{4,8},{6,10},{8,4},{10,6},{12,0},{14,2},{1,13},{3,15... | collective-permute-start | bytes 294920 | tf_op jit(solution)/shard_map/ppermute | solution.py:570
  30.9 6.8 %collective-permute-start.6 = (bf16[2,96,256]{2,1,0:T(8,128)(2,1)S(1)}, bf16[2,96,256]{2,1,0:T(8,128)(2,1)S(1)}, u32[]{:S(2)}, u32[]{:S(2)}) collective-permute-start(bf16[2,96,256]{2,1,0:T(8,128)(2,1)S(1)} %get-tuple-element.70), channel_id=1, source_target_pairs={{0,2},{2,0},{4,6},{6,4},{8,10},{10,8},{12,14},{14,12},{1,3},{3,1},... | collective-permute-start | bytes 294920 | tf_op jit(solution)/shard_map/ppermute | solution.py:570
  33.1 5.5 %collective-permute-start.7 = (bf16[2,96,256]{2,1,0:T(8,128)(2,1)S(1)}, bf16[2,96,256]{2,1,0:T(8,128)(2,1)S(1)}, u32[]{:S(2)}, u32[]{:S(2)}) collective-permute-start(bf16[2,96,256]{2,1,0:T(8,128)(2,1)S(1)} %get-tuple-element.72), channel_id=1, source_target_pairs={{0,6},{2,4},{4,2},{6,0},{8,14},{10,12},{12,10},{14,8},{1,7},{3,5},... | collective-permute-start | bytes 294920 | tf_op jit(solution)/shard_map/ppermute | solution.py:570
  36.0 3.2 %collective-permute-start.11 = (bf16[2,2,48,1024]{3,2,1,0:T(8,128)(2,1)S(1)}, bf16[2,2,48,1024]{3,2,1,0:T(8,128)(2,1)S(1)}, u32[]{:S(2)}, u32[]{:S(2)}) collective-permute-start(bf16[2,2,48,1024]{3,2,1,0:T(8,128)(2,1)S(1)} %collective-permute-done.3.refs_4_), channel_id=1, source_target_pairs={{0,1},{1,0},{2,3},{3,2},{4,5},{5,4},{6,7},{7,6},{8,9},{9,8},{10,11... | collective-permute-start | bytes 1179656 | tf_op jit(solution)/shard_map/ppermute | solution.py:537
  36.6 2.6 %collective-permute-start.12 = (bf16[2,2,48,1024]{3,2,1,0:T(8,128)(2,1)S(1)}, bf16[2,2,48,1024]{3,2,1,0:T(8,128)(2,1)S(1)}, u32[]{:S(2)}, u32[]{:S(2)}) collective-permute-start(bf16[2,2,48,1024]{3,2,1,0:T(8,128)(2,1)S(1)} %collective-permute-done.4.refs_6_), channel_id=1, source_target_pairs={{0,1},{1,0},{2,3},{3,2},{4,5},{5,4},{6,7},{7,6},{8,9},{9,8},{10,11... | collective-permute-start | bytes 1179656 | tf_op jit(solution)/shard_map/ppermute | solution.py:537
  38.6 1.7 %collective-permute-start.13 = (bf16[2,2,48,1024]{3,2,1,0:T(8,128)(2,1)S(1)}, bf16[2,2,48,1024]{3,2,1,0:T(8,128)(2,1)S(1)}, u32[]{:S(2)}, u32[]{:S(2)}) collective-permute-start(bf16[2,2,48,1024]{3,2,1,0:T(8,128)(2,1)S(1)} %collective-permute-done.5.refs_4_), channel_id=1, source_target_pairs={{0,1},{1,0},{2,3},{3,2},{4,5},{5,4},{6,7},{7,6},{8,9},{9,8},{10,11... | collective-permute-start | bytes 1179656 | tf_op jit(solution)/shard_map/ppermute | solution.py:537
  38.6 2.3 %collective-permute-start.14 = (bf16[2,2,48,1024]{3,2,1,0:T(8,128)(2,1)S(1)}, bf16[2,2,48,1024]{3,2,1,0:T(8,128)(2,1)S(1)}, u32[]{:S(2)}, u32[]{:S(2)}) collective-permute-start(bf16[2,2,48,1024]{3,2,1,0:T(8,128)(2,1)S(1)} %collective-permute-done.10.refs_6_), channel_id=1, source_target_pairs={{0,1},{1,0},{2,3},{3,2},{4,5},{5,4},{6,7},{7,6},{8,9},{9,8},{10,11... | collective-permute-start | bytes 1179656 | tf_op jit(solution)/shard_map/ppermute | solution.py:537
  39.2 25.8 %slice-start.2 = ((s8[6291456]{0:T(1024)(128)(4,1)}), s8[4194304]{0:T(1024)(128)(4,1)S(1)}, s32[]{:S(2)}) async-start(s8[6291456]{0:T(1024)(128)(4,1)} %bitcast.5), calls=%async_computation.2 | async-start | bytes 8388608
  40.9 24.0 %slice-start.3 = ((s8[6291456]{0:T(1024)(128)(4,1)}), s8[2097152]{0:T(1024)(128)(4,1)S(1)}, s32[]{:S(2)}) async-start(s8[6291456]{0:T(1024)(128)(4,1)} %bitcast.5), calls=%async_computation.3 | async-start | bytes 4194304
  44.4 6.7 %collective-permute-start.15 = (bf16[2,96,256]{2,1,0:T(8,128)(2,1)S(1)}, bf16[2,96,256]{2,1,0:T(8,128)(2,1)S(1)}, u32[]{:S(2)}, u32[]{:S(2)}) collective-permute-start(bf16[2,96,256]{2,1,0:T(8,128)(2,1)S(1)} %get-tuple-element.96), channel_id=1, source_target_pairs={{0,2},{2,0},{4,6},{6,4},{8,10},{10,8},{12,14},{14,12},{1,3},{3,1},... | collective-permute-start | bytes 294920 | tf_op jit(solution)/shard_map/ppermute | solution.py:546
  45.2 8.3 %collective-permute-start.16 = (bf16[2,96,256]{2,1,0:T(8,128)(2,1)S(1)}, bf16[2,96,256]{2,1,0:T(8,128)(2,1)S(1)}, u32[]{:S(2)}, u32[]{:S(2)}) collective-permute-start(bf16[2,96,256]{2,1,0:T(8,128)(2,1)S(1)} %get-tuple-element.97), channel_id=1, source_target_pairs={{0,4},{2,6},{4,0},{6,2},{8,12},{10,14},{12,8},{14,10},{1,5},{3,7},... | collective-permute-start | bytes 294920 | tf_op jit(solution)/shard_map/ppermute | solution.py:546
  46.2 9.4 %collective-permute-start.17 = (bf16[2,96,256]{2,1,0:T(8,128)(2,1)S(1)}, bf16[2,96,256]{2,1,0:T(8,128)(2,1)S(1)}, u32[]{:S(2)}, u32[]{:S(2)}) collective-permute-start(bf16[2,96,256]{2,1,0:T(8,128)(2,1)S(1)} %get-tuple-element.98), channel_id=1, source_target_pairs={{0,6},{2,4},{4,2},{6,0},{8,14},{10,12},{12,10},{14,8},{1,7},{3,5},... | collective-permute-start | bytes 294920 | tf_op jit(solution)/shard_map/ppermute | solution.py:546
  47.9 14.6 %collective-permute-start.18 = (bf16[2,96,256]{2,1,0:T(8,128)(2,1)S(1)}, bf16[2,96,256]{2,1,0:T(8,128)(2,1)S(1)}, u32[]{:S(2)}, u32[]{:S(2)}) collective-permute-start(bf16[2,96,256]{2,1,0:T(8,128)(2,1)S(1)} %get-tuple-element.99), channel_id=1, source_target_pairs={{0,8},{2,10},{4,12},{6,14},{8,0},{10,2},{12,4},{14,6},{1,9},{3,11}... | collective-permute-start | bytes 294920 | tf_op jit(solution)/shard_map/ppermute | solution.py:546
  49.4 15.5 %collective-permute-start.19 = (bf16[2,96,256]{2,1,0:T(8,128)(2,1)S(1)}, bf16[2,96,256]{2,1,0:T(8,128)(2,1)S(1)}, u32[]{:S(2)}, u32[]{:S(2)}) collective-permute-start(bf16[2,96,256]{2,1,0:T(8,128)(2,1)S(1)} %get-tuple-element.100), channel_id=1, source_target_pairs={{0,10},{2,8},{4,14},{6,12},{8,2},{10,0},{12,6},{14,4},{1,11},{3,9}... | collective-permute-start | bytes 294920 | tf_op jit(solution)/shard_map/ppermute | solution.py:546
  51.1 13.8 %collective-permute-start.20 = (bf16[2,96,256]{2,1,0:T(8,128)(2,1)S(1)}, bf16[2,96,256]{2,1,0:T(8,128)(2,1)S(1)}, u32[]{:S(2)}, u32[]{:S(2)}) collective-permute-start(bf16[2,96,256]{2,1,0:T(8,128)(2,1)S(1)} %get-tuple-element.101), channel_id=1, source_target_pairs={{0,12},{2,14},{4,8},{6,10},{8,4},{10,6},{12,0},{14,2},{1,13},{3,15... | collective-permute-start | bytes 294920 | tf_op jit(solution)/shard_map/ppermute | solution.py:546
  53.6 11.4 %collective-permute-start.21 = (bf16[2,96,256]{2,1,0:T(8,128)(2,1)S(1)}, bf16[2,96,256]{2,1,0:T(8,128)(2,1)S(1)}, u32[]{:S(2)}, u32[]{:S(2)}) collective-permute-start(bf16[2,96,256]{2,1,0:T(8,128)(2,1)S(1)} %get-tuple-element.102), channel_id=1, source_target_pairs={{0,14},{2,12},{4,10},{6,8},{8,6},{10,4},{12,2},{14,0},{1,15},{3,13... | collective-permute-start | bytes 294920 | tf_op jit(solution)/shard_map/ppermute | solution.py:546

commit v6 on v5

--- a/solution.py
+++ b/solution.py
@@ -537,18 +537,6 @@
     return lax.ppermute(array, axis, [(0, 1), (1, 0)])
 
 
-def exchange(arrays, count_col):
-    moved = list(arrays)
-    for d in range(count_col - 1, -1, -1):
-        for e in (1, 0):
-            offset = 2 * d + e
-            if offset:
-                moved[offset] = lax.ppermute(
-                    arrays[offset], ("col", "freq"), [(i, i ^ offset) for i in range(2 * count_col)]
-                )
-    return moved
-
-
 def per_device_paired(focusing, v_factors, u_factors, tile_ranks, owners, onsets):
     count_col = lax.axis_size("col")
     mine = lax.axis_index("freq")
@@ -596,7 +584,12 @@
     for piece in second:
         pieces.extend([piece, swap(piece, "rep")])
     back = receiver_products(count_col, half, mask, mixing, own, arrived[1::2], u_here, near, partial, pieces)
-    returned = exchange(back, count_col)
+    returned = list(back)
+    for offset in (4, 5, 6, 7, 1):
+        returned[offset] = move(offset, back[offset])
+    *rest, returned[(4, 5, 6, 7, 1)[0]] = lax.optimization_barrier(tuple([back[n] for n in (2, 3)] + [returned[(4, 5, 6, 7, 1)[0]]]))
+    for offset, payload in zip((2, 3), rest):
+        returned[offset] = move(offset, payload)
     return update_products(count_col, half, owners, returned, focus_here, v_here)
 
 

time: 69.6 us -> 69.3 us (level); the launches traced: 68.4 us -> 69.1 us
  waiting for transfers between devices: 19.6 us -> 20.3 us
    ppermute x7 -> x14, starting transfers between devices: 11.1 us -> 22.3 us  [move(): lax.ppermute(payload, ('col', 'freq'), [(i, i ^ offset) for i in range(2...]
    ppermute x7 -> x0, starting transfers between devices: 11.2 us -> none  [exchange(): lax.ppermute(arrays[offset], ('col', 'freq'), [(i, i ^ offset) for i in r...]
    ppermute x7 -> x14, waiting for transfers between devices: 8.07 us -> 18.1 us  [move(): lax.ppermute(payload, ('col', 'freq'), [(i, i ^ offset) for i in range(2...]
    ppermute x7 -> x0, waiting for transfers between devices: 9.35 us -> none  [exchange(): lax.ppermute(arrays[offset], ('col', 'freq'), [(i, i ^ offset) for i in r...]
  transfers between devices with their start and end apart: 22 -> 22, of which waited for: 10 -> 12; matrix products, arithmetic and copies ran while one was open for 0% -> 0% of each run, Pallas kernels for 16% -> 16%
where the time goes in v6:
time: 69.3 us; the launch traced here: 69.1 us
  starting transfers between devices  28.5 us (41%)
  waiting for transfers between devices  20.3 us (29%)
  Pallas kernels  18.1 us (26%)
  local copies, waits for them, and re-layouts  2.06 us (3%)
    ppermute x14, starting transfers between devices, move(): lax.ppermute(payload, ('col', 'freq'), [(i, i ^ offset) for i in range(2...  22.3 us
    ppermute x14, waiting for transfers between devices, move(): lax.ppermute(payload, ('col', 'freq'), [(i, i ^ offset) for i in range(2...  18.1 us
    pallas_call x1, Pallas kernels, forward_products(): pl.pallas_call(functools.partial(forward_kernel, count_col, half), in_spe...  7.48 us
    ppermute x8, starting transfers between devices, swap(): return lax.ppermute(array, axis, [(0, 1), (1, 0)])  6.23 us
    pallas_call x1, Pallas kernels, receiver_products(): pl.pallas_call(functools.partial(receiver_kernel, count_col, half), in_sp...  3.45 us
    pallas_call x1, Pallas kernels, update_products(): pl.pallas_call(functools.partial(update_kernel, count_col, half), in_spec...  3.44 us
    ppermute x8, waiting for transfers between devices, swap(): return lax.ppermute(array, axis, [(0, 1), (1, 0)])  2.19 us
    pallas_call x1, Pallas kernels, prepare(): pl.pallas_call(functools.partial(prepare_kernel, count_col, half), in_spe...  1.5 us
  transfers between devices with their start and end apart: 22, of which 12 were waited for; matrix products, arithmetic and copies ran while one was open for 0% of the time, Pallas kernels for 16%

profile of v6, /device:TPU:0, one launch (start us, length us, event | category | flops | bytes accessed | tf_op | source)
XLA Modules:
  0.0 69.1 jit_solution(2630259733704047905)
XLA Ops:
  0.0 1.2 %dynamic-slice_bitcast_fusion = bf16[2,2,96,1024]{3,2,1,0:T(8,128)(2,1)S(1)} fusion(bf16[1,2,4,384,1024]{4,3,2,1,0:T(8,128)(2,1)} %u_factors, s32[]{:T(128)S(6)} %select_n.6, s32[]{:T(128)S(6)} %select_n.7), kind=kLoop, calls=%fused_computation | loop fusion | bytes 1572872 | tf_op jit(solution)/shard_map/reshape | solution.py:554
  1.2 0.0 slice-start
  1.2 0.1 fusion
  1.3 3.0 %collective-permute-start.3 = (bf16[2,2,48,1024]{3,2,1,0:T(8,128)(2,1)S(1)}, bf16[2,2,48,1024]{3,2,1,0:T(8,128)(2,1)S(1)}, u32[]{:S(2)}, u32[]{:S(2)}) collective-permute-start(bf16[2,2,48,1024]{3,2,1,0:T(8,128)(2,1)S(1)} %get-tuple-element.112), channel_id=1, source_target_pairs={{0,2},{2,0},{1,3},{3,1},{4,6},{6,4},{5,7},{7,5},{8,10},{10,8},{9,1... | collective-permute-start | bytes 1179656 | tf_op jit(solution)/shard_map/ppermute | solution.py:537
  4.3 0.0 slice-start.1
  4.3 0.0 copy-start
  4.3 0.0 copy-start.1
  4.3 0.1 collective-permute-start.4
  4.4 0.8 %copy-done.3 = s32[16]{0:T(128)S(1)} copy-done((s32[16]{0:T(128)S(1)}, s32[16]{0:T(128)}, u32[]{:S(2)}) %copy-start.3) | copy-done | bytes 88
  5.2 7.5 %forward_products.1 = (bf16[2,96,256]{2,1,0:T(8,128)(2,1)S(1)}, bf16[2,96,256]{2,1,0:T(8,128)(2,1)S(1)}, bf16[2,96,256]{2,1,0:T(8,128)(2,1)S(1)}, bf16[2,96,256]...) custom-call(s32[16]{0:T(128)S(1)} %copy-done.3, ...), custom_call_target="tpu_custom_call" | custom-call | flops 1610612736 | bytes 10485760 | tf_op jit(solution)/shard_map/forward_products/pallas_call | solution.py:226
  12.7 1.5 %collective-permute-done.3.refs_4_ = bf16[2,2,48,1024]{3,2,1,0:T(8,128)(2,1)S(1)} collective-permute-done((bf16[2,2,48,1024]{3,2,1,0:T(8,128)(2,1)S(1)}, bf16[2,2,48,1024]{3,2,1,0:T(8,128)(2,1)S(1)}, u32[]{:S(2)}, u32[]{:S(2)}) %collective-permute-start.3) | collective-permute-done | bytes 393248 | tf_op jit(solution)/shard_map/ppermute | solution.py:537
  14.2 2.1 %collective-permute-start.5 = (bf16[2,2,48,1024]{3,2,1,0:T(8,128)(2,1)S(1)}, bf16[2,2,48,1024]{3,2,1,0:T(8,128)(2,1)S(1)}, u32[]{:S(2)}, u32[]{:S(2)}) collective-permute-start(bf16[2,2,48,1024]{3,2,1,0:T(8,128)(2,1)S(1)} %collective-permute-done.3.refs_4_), channel_id=1, source_target_pairs={{0,16},{16,0},{1,17},{17,1},{2,18},{18,2},{3,19},{19,3},{4,20},{20... | collective-permute-start | bytes 1179656 | tf_op jit(solution)/shard_map/ppermute | solution.py:537
  16.3 1.6 %collective-permute-start = (bf16[2,96,256]{2,1,0:T(8,128)(2,1)S(1)}, bf16[2,96,256]{2,1,0:T(8,128)(2,1)S(1)}, u32[]{:S(2)}, u32[]{:S(2)}) collective-permute-start(bf16[2,96,256]{2,1,0:T(8,128)(2,1)S(1)} %get-tuple-element.62), channel_id=1, source_target_pairs={{0,4},{2,6},{4,0},{6,2},{8,12},{10,14},{12,8},{14,10},{1,5},{3,7},... | collective-permute-start | bytes 294920 | tf_op jit(solution)/shard_map/ppermute | solution.py:558
  17.9 2.6 %collective-permute-start.1 = (bf16[2,96,256]{2,1,0:T(8,128)(2,1)S(1)}, bf16[2,96,256]{2,1,0:T(8,128)(2,1)S(1)}, u32[]{:S(2)}, u32[]{:S(2)}) collective-permute-start(bf16[2,96,256]{2,1,0:T(8,128)(2,1)S(1)} %get-tuple-element.64), channel_id=1, source_target_pairs={{0,8},{2,10},{4,12},{6,14},{8,0},{10,2},{12,4},{14,6},{1,9},{3,11}... | collective-permute-start | bytes 294920 | tf_op jit(solution)/shard_map/ppermute | solution.py:558
  20.5 1.1 %collective-permute-start.2 = (bf16[2,96,256]{2,1,0:T(8,128)(2,1)S(1)}, bf16[2,96,256]{2,1,0:T(8,128)(2,1)S(1)}, u32[]{:S(2)}, u32[]{:S(2)}) collective-permute-start(bf16[2,96,256]{2,1,0:T(8,128)(2,1)S(1)} %get-tuple-element.67), channel_id=1, source_target_pairs={{0,14},{2,12},{4,10},{6,8},{8,6},{10,4},{12,2},{14,0},{1,15},{3,13... | collective-permute-start | bytes 294920 | tf_op jit(solution)/shard_map/ppermute | solution.py:558
  21.6 0.0 slice-done
  21.6 0.0 slice-done.1
  21.6 0.0 copy-done
  21.6 0.0 copy-done.1
  21.6 0.0 copy-done.2
  21.6 1.5 %prepare.1 = (bf16[2,2,384,1024]{3,2,1,0:T(8,128)(2,1)S(1)}, f32[2,16,1024]{2,1,0:T(8,128)S(1)}, bf16[2,384,256]{2,1,0:T(8,128)(2,1)S(1)}) custom-call(s32[16]{0:T(128)S(1)} %copy-done.3, s32[16,16]{1,0:T(8,128)S(1)} %copy-done.2, s32[16,1,1024]{2,1,0:T(1,128)S(1)} %bitcast.7, bf16[2,48,512]{2,1,0:T(8,128)(2,1)S(1)} %copy-done, ...), custom_call_target="tpu_custom_call" | custom-call | bytes 6291456 | tf_op jit(solution)/shard_map/prepare/pallas_call | solution.py:272
  23.2 0.0 collective-permute-done.refs_1_
  23.2 2.3 %collective-permute-done.1.refs_2_ = bf16[2,96,256]{2,1,0:T(8,128)(2,1)S(1)} collective-permute-done((bf16[2,96,256]{2,1,0:T(8,128)(2,1)S(1)}, bf16[2,96,256]{2,1,0:T(8,128)(2,1)S(1)}, u32[]{:S(2)}, u32[]{:S(2)}) %collective-permute-start.1) | collective-permute-done | bytes 98336 | tf_op jit(solution)/shard_map/ppermute | solution.py:558
  25.5 2.4 %collective-permute-done.2.refs_3_ = bf16[2,96,256]{2,1,0:T(8,128)(2,1)S(1)} collective-permute-done((bf16[2,96,256]{2,1,0:T(8,128)(2,1)S(1)}, bf16[2,96,256]{2,1,0:T(8,128)(2,1)S(1)}, u32[]{:S(2)}, u32[]{:S(2)}) %collective-permute-start.2) | collective-permute-done | bytes 98336 | tf_op jit(solution)/shard_map/ppermute | solution.py:558
  27.9 0.0 collective-permute-done.4.refs_6_
  27.9 0.0 collective-permute-done.5.refs_4_
  27.9 0.5 collective-permute-start.10
  28.4 1.6 %collective-permute-start.8 = (bf16[2,96,256]{2,1,0:T(8,128)(2,1)S(1)}, bf16[2,96,256]{2,1,0:T(8,128)(2,1)S(1)}, u32[]{:S(2)}, u32[]{:S(2)}) collective-permute-start(bf16[2,96,256]{2,1,0:T(8,128)(2,1)S(1)} %get-tuple-element.77), channel_id=1, source_target_pairs={{0,10},{2,8},{4,14},{6,12},{8,2},{10,0},{12,6},{14,4},{1,11},{3,9}... | collective-permute-start | bytes 294920 | tf_op jit(solution)/shard_map/ppermute | solution.py:558
  30.0 0.8 %collective-permute-start.9 = (bf16[2,96,256]{2,1,0:T(8,128)(2,1)S(1)}, bf16[2,96,256]{2,1,0:T(8,128)(2,1)S(1)}, u32[]{:S(2)}, u32[]{:S(2)}) collective-permute-start(bf16[2,96,256]{2,1,0:T(8,128)(2,1)S(1)} %get-tuple-element.78), channel_id=1, source_target_pairs={{0,12},{2,14},{4,8},{6,10},{8,4},{10,6},{12,0},{14,2},{1,13},{3,15... | collective-permute-start | bytes 294920 | tf_op jit(solution)/shard_map/ppermute | solution.py:558
  30.9 2.2 %collective-permute-start.6 = (bf16[2,96,256]{2,1,0:T(8,128)(2,1)S(1)}, bf16[2,96,256]{2,1,0:T(8,128)(2,1)S(1)}, u32[]{:S(2)}, u32[]{:S(2)}) collective-permute-start(bf16[2,96,256]{2,1,0:T(8,128)(2,1)S(1)} %get-tuple-element.73), channel_id=1, source_target_pairs={{0,2},{2,0},{4,6},{6,4},{8,10},{10,8},{12,14},{14,12},{1,3},{3,1},... | collective-permute-start | bytes 294920 | tf_op jit(solution)/shard_map/ppermute | solution.py:558
  33.1 1.0 %collective-permute-start.7 = (bf16[2,96,256]{2,1,0:T(8,128)(2,1)S(1)}, bf16[2,96,256]{2,1,0:T(8,128)(2,1)S(1)}, u32[]{:S(2)}, u32[]{:S(2)}) collective-permute-start(bf16[2,96,256]{2,1,0:T(8,128)(2,1)S(1)} %get-tuple-element.75), channel_id=1, source_target_pairs={{0,6},{2,4},{4,2},{6,0},{8,14},{10,12},{12,10},{14,8},{1,7},{3,5},... | collective-permute-start | bytes 294920 | tf_op jit(solution)/shard_map/ppermute | solution.py:558
  34.2 1.8 %collective-permute-done.8.refs_2_ = bf16[2,96,256]{2,1,0:T(8,128)(2,1)S(1)} collective-permute-done((bf16[2,96,256]{2,1,0:T(8,128)(2,1)S(1)}, bf16[2,96,256]{2,1,0:T(8,128)(2,1)S(1)}, u32[]{:S(2)}, u32[]{:S(2)}) %collective-permute-start.8) | collective-permute-done | bytes 98336 | tf_op jit(solution)/shard_map/ppermute | solution.py:558
  36.0 0.0 collective-permute-start.11
  36.0 0.6 collective-permute-done.9.refs_3_
  36.6 0.0 collective-permute-start.12
  36.6 1.1 %own_field.1.own = bf16[2,256,1024]{2,1,0:T(8,128)(2,1)S(1)} custom-call(bf16[2,384,256]{2,1,0:T(8,128)(2,1)S(1)} %get-tuple-element.60.mask, bf16[2,2,384,1024]{3,2,1,0:T(8,128)(2,1)S(1)} %get-tuple-element.87.u_own, bf16[2,96,256]{2,1,0:T(8,128)(2,1)S(1)} %get-tuple-element.72.refs_0_, bf16[2,96,256]{2,1,0:T(8,128)(2,1)S(1)} %collective-permute-done.refs_1_, ...), custom_call_target="tpu_custom_call" | custom-call | flops 805306368 | bytes 1572864 | tf_op jit(solution)/shard_map/own_field/pallas_call | solution.py:316
  37.7 0.0 collective-permute-done.6.refs_0_
  37.7 0.9 %collective-permute-done.7.refs_1_ = bf16[2,96,256]{2,1,0:T(8,128)(2,1)S(1)} collective-permute-done((bf16[2,96,256]{2,1,0:T(8,128)(2,1)S(1)}, bf16[2,96,256]{2,1,0:T(8,128)(2,1)S(1)}, u32[]{:S(2)}, u32[]{:S(2)}) %collective-permute-start.7) | collective-permute-done | bytes 98336 | tf_op jit(solution)/shard_map/ppermute | solution.py:558
  38.6 0.0 collective-permute-done.10.refs_6_
  38.6 0.0 collective-permute-start.13
  38.6 0.5 collective-permute-start.14
  39.2 0.0 collective-permute-done.11.refs_5_
  39.2 0.0 collective-permute-done.12.refs_7_
  39.2 1.1 %near_products.1 = (bf16[2,2,192,1024]{3,2,1,0:T(8,128)(2,1)S(1)}, f32[2,256,1024]{2,1,0:T(8,128)S(1)}) custom-call(bf16[2,384,256]{2,1,0:T(8,128)(2,1)S(1)} %get-tuple-element.60.mask, bf16[2,96,256]{2,1,0:T(8,128)(2,1)S(1)} %collective-permute-done.6.refs_0_, bf16[2,96,256]{2,1,0:T(8,128)(2,1)S(1)} %collective-permute-done.7.refs_1_, ...), custom_call_target="tpu_custom_call" | custom-call | flops 402653184 | bytes 1572864 | tf_op jit(solution)/shard_map/near_products/pallas_call | solution.py:377
  40.3 0.1 collective-permute-done.13.refs_5_
  40.4 0.6 collective-permute-done.14.refs_7_
  40.9 3.4 %receiver_products.1 = (bf16[2,96,256]{2,1,0:T(8,128)(2,1)S(1)}, bf16[2,96,256]{2,1,0:T(8,128)(2,1)S(1)}, bf16[2,96,256]{2,1,0:T(8,128)(2,1)S(1)}, bf16[2,96,256...) custom-call(bf16[2,384,256]{2,1,0:T(8,128)(2,1)S(1)} %get-tuple-elem, ...), custom_call_target="tpu_custom_call" | custom-call | flops 2415919104 | bytes 6291456 | tf_op jit(solution)/shard_map/receiver_products/pallas_call | solution.py:450
  44.4 1.5 %collective-permute-start.16 = (bf16[2,96,256]{2,1,0:T(8,128)(2,1)S(1)}, bf16[2,96,256]{2,1,0:T(8,128)(2,1)S(1)}, u32[]{:S(2)}, u32[]{:S(2)}) collective-permute-start(bf16[2,96,256]{2,1,0:T(8,128)(2,1)S(1)} %get-tuple-element.102), channel_id=1, source_target_pairs={{0,8},{2,10},{4,12},{6,14},{8,0},{10,2},{12,4},{14,6},{1,9},{3,11}... | collective-permute-start | bytes 294920 | tf_op jit(solution)/shard_map/ppermute | solution.py:558
  45.9 0.6 collective-permute-start.15
  46.5 2.4 %collective-permute-start.19 = (bf16[2,96,256]{2,1,0:T(8,128)(2,1)S(1)}, bf16[2,96,256]{2,1,0:T(8,128)(2,1)S(1)}, u32[]{:S(2)}, u32[]{:S(2)}) collective-permute-start(bf16[2,96,256]{2,1,0:T(8,128)(2,1)S(1)} %get-tuple-element.106), channel_id=1, source_target_pairs={{0,10},{2,8},{4,14},{6,12},{8,2},{10,0},{12,6},{14,4},{1,11},{3,9}... | collective-permute-start | bytes 294920 | tf_op jit(solution)/shard_map/ppermute | solution.py:558
  48.8 2.3 %collective-permute-start.20 = (bf16[2,96,256]{2,1,0:T(8,128)(2,1)S(1)}, bf16[2,96,256]{2,1,0:T(8,128)(2,1)S(1)}, u32[]{:S(2)}, u32[]{:S(2)}) collective-permute-start(bf16[2,96,256]{2,1,0:T(8,128)(2,1)S(1)} %get-tuple-element.107), channel_id=1, source_target_pairs={{0,12},{2,14},{4,8},{6,10},{8,4},{10,6},{12,0},{14,2},{1,13},{3,15... | collective-permute-start | bytes 294920 | tf_op jit(solution)/shard_map/ppermute | solution.py:558
  51.1 1.8 %collective-permute-start.21 = (bf16[2,96,256]{2,1,0:T(8,128)(2,1)S(1)}, bf16[2,96,256]{2,1,0:T(8,128)(2,1)S(1)}, u32[]{:S(2)}, u32[]{:S(2)}) collective-permute-start(bf16[2,96,256]{2,1,0:T(8,128)(2,1)S(1)} %get-tuple-element.108), channel_id=1, source_target_pairs={{0,14},{2,12},{4,10},{6,8},{8,6},{10,4},{12,2},{14,0},{1,15},{3,13... | collective-permute-start | bytes 294920 | tf_op jit(solution)/shard_map/ppermute | solution.py:558
  52.9 6.0 %collective-permute-done.16.refs_4_ = bf16[2,96,256]{2,1,0:T(8,128)(2,1)S(1)} collective-permute-done((bf16[2,96,256]{2,1,0:T(8,128)(2,1)S(1)}, bf16[2,96,256]{2,1,0:T(8,128)(2,1)S(1)}, u32[]{:S(2)}, u32[]{:S(2)}) %collective-permute-start.16) | collective-permute-done | bytes 98336 | tf_op jit(solution)/shard_map/ppermute | solution.py:558
  58.9 0.0 collective-permute-start.17
  58.9 0.0 collective-permute-done.15.refs_1_
  58.9 2.7 %collective-permute-start.18 = (bf16[2,96,256]{2,1,0:T(8,128)(2,1)S(1)}, bf16[2,96,256]{2,1,0:T(8,128)(2,1)S(1)}, u32[]{:S(2)}, u32[]{:S(2)}) collective-permute-start(bf16[2,96,256]{2,1,0:T(8,128)(2,1)S(1)} %get-tuple-element.104), channel_id=1, source_target_pairs={{0,6},{2,4},{4,2},{6,0},{8,14},{10,12},{12,10},{14,8},{1,7},{3,5},... | collective-permute-start | bytes 294920 | tf_op jit(solution)/shard_map/ppermute | solution.py:558
  61.6 0.1 collective-permute-done.19.refs_5_
  61.7 0.0 collective-permute-done.20.refs_6_
  61.7 0.0 collective-permute-done.21.refs_7_
  61.7 2.6 %collective-permute-done.17.refs_2_ = bf16[2,96,256]{2,1,0:T(8,128)(2,1)S(1)} collective-permute-done((bf16[2,96,256]{2,1,0:T(8,128)(2,1)S(1)}, bf16[2,96,256]{2,1,0:T(8,128)(2,1)S(1)}, u32[]{:S(2)}, u32[]{:S(2)}) %collective-permute-start.17) | collective-permute-done | bytes 98336 | tf_op jit(solution)/shard_map/ppermute | solution.py:558
  64.2 1.4 %collective-permute-done.18.refs_3_ = bf16[2,96,256]{2,1,0:T(8,128)(2,1)S(1)} collective-permute-done((bf16[2,96,256]{2,1,0:T(8,128)(2,1)S(1)}, bf16[2,96,256]{2,1,0:T(8,128)(2,1)S(1)}, u32[]{:S(2)}, u32[]{:S(2)}) %collective-permute-start.18) | collective-permute-done | bytes 98336 | tf_op jit(solution)/shard_map/ppermute | solution.py:558
  65.7 0.0 slice-done.2
  65.7 0.0 slice-done.3
  65.7 3.4 %update_products.1 = f32[1,2,128,4096]{3,2,1,0:T(8,128)} custom-call(s32[16]{0:T(128)S(1)} %copy-done.3, bf16[2,96,256]{2,1,0:T(8,128)(2,1)S(1)} %get-tuple-element.98.refs_0_, bf16[2,96,256]{2,1,0:T(8,128)(2,1)S(1)} %collective-permute-done.15.refs_1_, bf16[2,96,256]{2,1,0:T(8,128)(2,1)S(1)} %collective-permute-done.17.refs_2_, ...), custom_call_target="tpu_custom_call" | custom-call | flops 1610612736 | bytes 14680064 | tf_op jit(solution)/shard_map/update_products/pallas_call | solution.py:515
  (6 shorter events, 0.0 us)
Async XLA Ops:
  1.2 20.4 %slice-start = ((s8[6291456]{0:T(1024)(128)(4,1)}), s8[4194304]{0:T(1024)(128)(4,1)S(1)}, s32[]{:S(2)}) async-start(s8[6291456]{0:T(1024)(128)(4,1)} %bitcast.3), calls=%async_computation | async-start | bytes 8388608
  1.3 12.9 %collective-permute-start.3 = (bf16[2,2,48,1024]{3,2,1,0:T(8,128)(2,1)S(1)}, bf16[2,2,48,1024]{3,2,1,0:T(8,128)(2,1)S(1)}, u32[]{:S(2)}, u32[]{:S(2)}) collective-permute-start(bf16[2,2,48,1024]{3,2,1,0:T(8,128)(2,1)S(1)} %get-tuple-element.112), channel_id=1, source_target_pairs={{0,2},{2,0},{1,3},{3,1},{4,6},{6,4},{5,7},{7,5},{8,10},{10,8},{9,1... | collective-permute-start | bytes 1179656 | tf_op jit(solution)/shard_map/ppermute | solution.py:537
  4.3 17.4 %slice-start.1 = ((s8[6291456]{0:T(1024)(128)(4,1)}), s8[2097152]{0:T(1024)(128)(4,1)S(1)}, s32[]{:S(2)}) async-start(s8[6291456]{0:T(1024)(128)(4,1)} %bitcast.3), calls=%async_computation.1 | async-start | bytes 4194304
  4.3 17.4 %copy-start = (bf16[2,48,512]{2,1,0:T(8,128)(2,1)S(1)}, bf16[2,48,512]{2,1,0:T(8,128)(2,1)}, u32[]{:S(2)}) copy-start(bf16[2,48,512]{2,1,0:T(8,128)(2,1)} %constant.24.clone.table) | copy-start | bytes 294916
  4.3 17.4 %copy-start.1 = (s32[16384]{0:T(1024)S(1)}, s32[16384]{0:T(1024)}, u32[]{:S(2)}) copy-start(s32[16384]{0:T(1024)} %param.12) | copy-start | bytes 196612
  4.3 17.4 %copy-start.2 = (s32[16,16]{1,0:T(8,128)S(1)}, s32[16,16]{1,0:T(8,128)}, u32[]{:S(2)}) copy-start(s32[16,16]{1,0:T(8,128)} %ranks.1) | copy-start | bytes 3076
  4.3 23.6 %collective-permute-start.4 = (bf16[2,2,48,1024]{3,2,1,0:T(8,128)(2,1)S(1)}, bf16[2,2,48,1024]{3,2,1,0:T(8,128)(2,1)S(1)}, u32[]{:S(2)}, u32[]{:S(2)}) collective-permute-start(bf16[2,2,48,1024]{3,2,1,0:T(8,128)(2,1)S(1)} %get-tuple-element.111), channel_id=1, source_target_pairs={{0,2},{2,0},{1,3},{3,1},{4,6},{6,4},{5,7},{7,5},{8,10},{10,8},{9,1... | collective-permute-start | bytes 1179656 | tf_op jit(solution)/shard_map/ppermute | solution.py:537
  4.4 0.8 %copy-start.3 = (s32[16]{0:T(128)S(1)}, s32[16]{0:T(128)}, u32[]{:S(2)}) copy-start(s32[16]{0:T(128)} %owners.3) | copy-start | bytes 196
  14.2 13.7 %collective-permute-start.5 = (bf16[2,2,48,1024]{3,2,1,0:T(8,128)(2,1)S(1)}, bf16[2,2,48,1024]{3,2,1,0:T(8,128)(2,1)S(1)}, u32[]{:S(2)}, u32[]{:S(2)}) collective-permute-start(bf16[2,2,48,1024]{3,2,1,0:T(8,128)(2,1)S(1)} %collective-permute-done.3.refs_4_), channel_id=1, source_target_pairs={{0,16},{16,0},{1,17},{17,1},{2,18},{18,2},{3,19},{19,3},{4,20},{20... | collective-permute-start | bytes 1179656 | tf_op jit(solution)/shard_map/ppermute | solution.py:537
  16.3 6.9 %collective-permute-start = (bf16[2,96,256]{2,1,0:T(8,128)(2,1)S(1)}, bf16[2,96,256]{2,1,0:T(8,128)(2,1)S(1)}, u32[]{:S(2)}, u32[]{:S(2)}) collective-permute-start(bf16[2,96,256]{2,1,0:T(8,128)(2,1)S(1)} %get-tuple-element.62), channel_id=1, source_target_pairs={{0,4},{2,6},{4,0},{6,2},{8,12},{10,14},{12,8},{14,10},{1,5},{3,7},... | collective-permute-start | bytes 294920 | tf_op jit(solution)/shard_map/ppermute | solution.py:558
  17.9 7.6 %collective-permute-start.1 = (bf16[2,96,256]{2,1,0:T(8,128)(2,1)S(1)}, bf16[2,96,256]{2,1,0:T(8,128)(2,1)S(1)}, u32[]{:S(2)}, u32[]{:S(2)}) collective-permute-start(bf16[2,96,256]{2,1,0:T(8,128)(2,1)S(1)} %get-tuple-element.64), channel_id=1, source_target_pairs={{0,8},{2,10},{4,12},{6,14},{8,0},{10,2},{12,4},{14,6},{1,9},{3,11}... | collective-permute-start | bytes 294920 | tf_op jit(solution)/shard_map/ppermute | solution.py:558
  20.5 7.4 %collective-permute-start.2 = (bf16[2,96,256]{2,1,0:T(8,128)(2,1)S(1)}, bf16[2,96,256]{2,1,0:T(8,128)(2,1)S(1)}, u32[]{:S(2)}, u32[]{:S(2)}) collective-permute-start(bf16[2,96,256]{2,1,0:T(8,128)(2,1)S(1)} %get-tuple-element.67), channel_id=1, source_target_pairs={{0,14},{2,12},{4,10},{6,8},{8,6},{10,4},{12,2},{14,0},{1,15},{3,13... | collective-permute-start | bytes 294920 | tf_op jit(solution)/shard_map/ppermute | solution.py:558
  27.9 10.8 %collective-permute-start.10 = (bf16[2,2,48,1024]{3,2,1,0:T(8,128)(2,1)S(1)}, bf16[2,2,48,1024]{3,2,1,0:T(8,128)(2,1)S(1)}, u32[]{:S(2)}, u32[]{:S(2)}) collective-permute-start(bf16[2,2,48,1024]{3,2,1,0:T(8,128)(2,1)S(1)} %collective-permute-done.4.refs_6_), channel_id=1, source_target_pairs={{0,16},{16,0},{1,17},{17,1},{2,18},{18,2},{3,19},{19,3},{4,20},{20... | collective-permute-start | bytes 1179656 | tf_op jit(solution)/shard_map/ppermute | solution.py:537
  28.4 7.6 %collective-permute-start.8 = (bf16[2,96,256]{2,1,0:T(8,128)(2,1)S(1)}, bf16[2,96,256]{2,1,0:T(8,128)(2,1)S(1)}, u32[]{:S(2)}, u32[]{:S(2)}) collective-permute-start(bf16[2,96,256]{2,1,0:T(8,128)(2,1)S(1)} %get-tuple-element.77), channel_id=1, source_target_pairs={{0,10},{2,8},{4,14},{6,12},{8,2},{10,0},{12,6},{14,4},{1,11},{3,9}... | collective-permute-start | bytes 294920 | tf_op jit(solution)/shard_map/ppermute | solution.py:558
  30.0 6.6 %collective-permute-start.9 = (bf16[2,96,256]{2,1,0:T(8,128)(2,1)S(1)}, bf16[2,96,256]{2,1,0:T(8,128)(2,1)S(1)}, u32[]{:S(2)}, u32[]{:S(2)}) collective-permute-start(bf16[2,96,256]{2,1,0:T(8,128)(2,1)S(1)} %get-tuple-element.78), channel_id=1, source_target_pairs={{0,12},{2,14},{4,8},{6,10},{8,4},{10,6},{12,0},{14,2},{1,13},{3,15... | collective-permute-start | bytes 294920 | tf_op jit(solution)/shard_map/ppermute | solution.py:558
  30.9 6.8 %collective-permute-start.6 = (bf16[2,96,256]{2,1,0:T(8,128)(2,1)S(1)}, bf16[2,96,256]{2,1,0:T(8,128)(2,1)S(1)}, u32[]{:S(2)}, u32[]{:S(2)}) collective-permute-start(bf16[2,96,256]{2,1,0:T(8,128)(2,1)S(1)} %get-tuple-element.73), channel_id=1, source_target_pairs={{0,2},{2,0},{4,6},{6,4},{8,10},{10,8},{12,14},{14,12},{1,3},{3,1},... | collective-permute-start | bytes 294920 | tf_op jit(solution)/shard_map/ppermute | solution.py:558
  33.1 5.5 %collective-permute-start.7 = (bf16[2,96,256]{2,1,0:T(8,128)(2,1)S(1)}, bf16[2,96,256]{2,1,0:T(8,128)(2,1)S(1)}, u32[]{:S(2)}, u32[]{:S(2)}) collective-permute-start(bf16[2,96,256]{2,1,0:T(8,128)(2,1)S(1)} %get-tuple-element.75), channel_id=1, source_target_pairs={{0,6},{2,4},{4,2},{6,0},{8,14},{10,12},{12,10},{14,8},{1,7},{3,5},... | collective-permute-start | bytes 294920 | tf_op jit(solution)/shard_map/ppermute | solution.py:558
  36.0 3.2 %collective-permute-start.11 = (bf16[2,2,48,1024]{3,2,1,0:T(8,128)(2,1)S(1)}, bf16[2,2,48,1024]{3,2,1,0:T(8,128)(2,1)S(1)}, u32[]{:S(2)}, u32[]{:S(2)}) collective-permute-start(bf16[2,2,48,1024]{3,2,1,0:T(8,128)(2,1)S(1)} %collective-permute-done.3.refs_4_), channel_id=1, source_target_pairs={{0,1},{1,0},{2,3},{3,2},{4,5},{5,4},{6,7},{7,6},{8,9},{9,8},{10,11... | collective-permute-start | bytes 1179656 | tf_op jit(solution)/shard_map/ppermute | solution.py:537
  36.6 2.6 %collective-permute-start.12 = (bf16[2,2,48,1024]{3,2,1,0:T(8,128)(2,1)S(1)}, bf16[2,2,48,1024]{3,2,1,0:T(8,128)(2,1)S(1)}, u32[]{:S(2)}, u32[]{:S(2)}) collective-permute-start(bf16[2,2,48,1024]{3,2,1,0:T(8,128)(2,1)S(1)} %collective-permute-done.4.refs_6_), channel_id=1, source_target_pairs={{0,1},{1,0},{2,3},{3,2},{4,5},{5,4},{6,7},{7,6},{8,9},{9,8},{10,11... | collective-permute-start | bytes 1179656 | tf_op jit(solution)/shard_map/ppermute | solution.py:537
  38.6 1.7 %collective-permute-start.13 = (bf16[2,2,48,1024]{3,2,1,0:T(8,128)(2,1)S(1)}, bf16[2,2,48,1024]{3,2,1,0:T(8,128)(2,1)S(1)}, u32[]{:S(2)}, u32[]{:S(2)}) collective-permute-start(bf16[2,2,48,1024]{3,2,1,0:T(8,128)(2,1)S(1)} %collective-permute-done.5.refs_4_), channel_id=1, source_target_pairs={{0,1},{1,0},{2,3},{3,2},{4,5},{5,4},{6,7},{7,6},{8,9},{9,8},{10,11... | collective-permute-start | bytes 1179656 | tf_op jit(solution)/shard_map/ppermute | solution.py:537
  38.6 2.3 %collective-permute-start.14 = (bf16[2,2,48,1024]{3,2,1,0:T(8,128)(2,1)S(1)}, bf16[2,2,48,1024]{3,2,1,0:T(8,128)(2,1)S(1)}, u32[]{:S(2)}, u32[]{:S(2)}) collective-permute-start(bf16[2,2,48,1024]{3,2,1,0:T(8,128)(2,1)S(1)} %collective-permute-done.10.refs_6_), channel_id=1, source_target_pairs={{0,1},{1,0},{2,3},{3,2},{4,5},{5,4},{6,7},{7,6},{8,9},{9,8},{10,11... | collective-permute-start | bytes 1179656 | tf_op jit(solution)/shard_map/ppermute | solution.py:537
  39.2 26.5 %slice-start.2 = ((s8[6291456]{0:T(1024)(128)(4,1)}), s8[4194304]{0:T(1024)(128)(4,1)S(1)}, s32[]{:S(2)}) async-start(s8[6291456]{0:T(1024)(128)(4,1)} %bitcast.5), calls=%async_computation.2 | async-start | bytes 8388608
  40.9 24.8 %slice-start.3 = ((s8[6291456]{0:T(1024)(128)(4,1)}), s8[2097152]{0:T(1024)(128)(4,1)S(1)}, s32[]{:S(2)}) async-start(s8[6291456]{0:T(1024)(128)(4,1)} %bitcast.5), calls=%async_computation.3 | async-start | bytes 4194304
  44.4 14.5 %collective-permute-start.16 = (bf16[2,96,256]{2,1,0:T(8,128)(2,1)S(1)}, bf16[2,96,256]{2,1,0:T(8,128)(2,1)S(1)}, u32[]{:S(2)}, u32[]{:S(2)}) collective-permute-start(bf16[2,96,256]{2,1,0:T(8,128)(2,1)S(1)} %get-tuple-element.102), channel_id=1, source_target_pairs={{0,8},{2,10},{4,12},{6,14},{8,0},{10,2},{12,4},{14,6},{1,9},{3,11}... | collective-permute-start | bytes 294920 | tf_op jit(solution)/shard_map/ppermute | solution.py:558
  45.9 13.0 %collective-permute-start.15 = (bf16[2,96,256]{2,1,0:T(8,128)(2,1)S(1)}, bf16[2,96,256]{2,1,0:T(8,128)(2,1)S(1)}, u32[]{:S(2)}, u32[]{:S(2)}) collective-permute-start(bf16[2,96,256]{2,1,0:T(8,128)(2,1)S(1)} %get-tuple-element.99), channel_id=1, source_target_pairs={{0,2},{2,0},{4,6},{6,4},{8,10},{10,8},{12,14},{14,12},{1,3},{3,1},... | collective-permute-start | bytes 294920 | tf_op jit(solution)/shard_map/ppermute | solution.py:558
  46.5 15.2 %collective-permute-start.19 = (bf16[2,96,256]{2,1,0:T(8,128)(2,1)S(1)}, bf16[2,96,256]{2,1,0:T(8,128)(2,1)S(1)}, u32[]{:S(2)}, u32[]{:S(2)}) collective-permute-start(bf16[2,96,256]{2,1,0:T(8,128)(2,1)S(1)} %get-tuple-element.106), channel_id=1, source_target_pairs={{0,10},{2,8},{4,14},{6,12},{8,2},{10,0},{12,6},{14,4},{1,11},{3,9}... | collective-permute-start | bytes 294920 | tf_op jit(solution)/shard_map/ppermute | solution.py:558
  48.8 12.8 %collective-permute-start.20 = (bf16[2,96,256]{2,1,0:T(8,128)(2,1)S(1)}, bf16[2,96,256]{2,1,0:T(8,128)(2,1)S(1)}, u32[]{:S(2)}, u32[]{:S(2)}) collective-permute-start(bf16[2,96,256]{2,1,0:T(8,128)(2,1)S(1)} %get-tuple-element.107), channel_id=1, source_target_pairs={{0,12},{2,14},{4,8},{6,10},{8,4},{10,6},{12,0},{14,2},{1,13},{3,15... | collective-permute-start | bytes 294920 | tf_op jit(solution)/shard_map/ppermute | solution.py:558
  51.1 10.5 %collective-permute-start.21 = (bf16[2,96,256]{2,1,0:T(8,128)(2,1)S(1)}, bf16[2,96,256]{2,1,0:T(8,128)(2,1)S(1)}, u32[]{:S(2)}, u32[]{:S(2)}) collective-permute-start(bf16[2,96,256]{2,1,0:T(8,128)(2,1)S(1)} %get-tuple-element.108), channel_id=1, source_target_pairs={{0,14},{2,12},{4,10},{6,8},{8,6},{10,4},{12,2},{14,0},{1,15},{3,13... | collective-permute-start | bytes 294920 | tf_op jit(solution)/shard_map/ppermute | solution.py:558
  58.9 5.4 %collective-permute-start.17 = (bf16[2,96,256]{2,1,0:T(8,128)(2,1)S(1)}, bf16[2,96,256]{2,1,0:T(8,128)(2,1)S(1)}, u32[]{:S(2)}, u32[]{:S(2)}) collective-permute-start(bf16[2,96,256]{2,1,0:T(8,128)(2,1)S(1)} %get-tuple-element.103), channel_id=1, source_target_pairs={{0,4},{2,6},{4,0},{6,2},{8,12},{10,14},{12,8},{14,10},{1,5},{3,7},... | collective-permute-start | bytes 294920 | tf_op jit(solution)/shard_map/ppermute | solution.py:558
  58.9 6.8 %collective-permute-start.18 = (bf16[2,96,256]{2,1,0:T(8,128)(2,1)S(1)}, bf16[2,96,256]{2,1,0:T(8,128)(2,1)S(1)}, u32[]{:S(2)}, u32[]{:S(2)}) collective-permute-start(bf16[2,96,256]{2,1,0:T(8,128)(2,1)S(1)} %get-tuple-element.104), channel_id=1, source_target_pairs={{0,6},{2,4},{4,2},{6,0},{8,14},{10,12},{12,10},{14,8},{1,7},{3,5},... | collective-permute-start | bytes 294920 | tf_op jit(solution)/shard_map/ppermute | solution.py:558

commit v7 on v5

--- a/solution.py
+++ b/solution.py
@@ -582,8 +582,8 @@
     second = [head, swap(first[1], "grp")]
     for offset in (5, 6, 3, 1):
         arrived[offset] = move(offset, arrived[offset])
-    tied = lax.optimization_barrier(tuple(first + [arrived[n] for n in (5,)]))
-    first = list(tied[:2])
+    first[0], _ = lax.optimization_barrier((first[0], arrived[5]))
+    first[1], _ = lax.optimization_barrier((first[1], arrived[1]))
     mates = [swap(piece, "rep") for piece in first]
     own = own_field(count_col, half, mask, u_here, arrived[::2])
     held = lax.optimization_barrier(tuple(arrived + first + second + [u_here, own]))

time: 69.6 us -> 69.3 us (level)
  transfers between devices with their start and end apart: 22 -> 22, of which waited for: 10 -> 9; matrix products, arithmetic and copies ran while one was open for 0% -> 0% of each run, Pallas kernels for 16% -> 16%
where the time goes in v7:
time: 69.3 us; the launch traced here: 68.7 us
  starting transfers between devices  29.1 us (42%)
  waiting for transfers between devices  19.3 us (28%)
  Pallas kernels  18.1 us (26%)
  local copies, waits for them, and re-layouts  2.06 us (3%)
    ppermute x7, starting transfers between devices, exchange(): lax.ppermute(arrays[offset], ('col', 'freq'), [(i, i ^ offset) for i in r...  11.2 us
    ppermute x7, starting transfers between devices, move(): lax.ppermute(payload, ('col', 'freq'), [(i, i ^ offset) for i in range(2...  11.1 us
    ppermute x7, waiting for transfers between devices, exchange(): lax.ppermute(arrays[offset], ('col', 'freq'), [(i, i ^ offset) for i in r...  8.96 us
    ppermute x7, waiting for transfers between devices, move(): lax.ppermute(payload, ('col', 'freq'), [(i, i ^ offset) for i in range(2...  8.11 us
    pallas_call x1, Pallas kernels, forward_products(): pl.pallas_call(functools.partial(forward_kernel, count_col, half), in_spe...  7.48 us
    ppermute x8, starting transfers between devices, swap(): return lax.ppermute(array, axis, [(0, 1), (1, 0)])  6.8 us
    pallas_call x1, Pallas kernels, update_products(): pl.pallas_call(functools.partial(update_kernel, count_col, half), in_spec...  3.46 us
    pallas_call x1, Pallas kernels, receiver_products(): pl.pallas_call(functools.partial(receiver_kernel, count_col, half), in_sp...  3.45 us
  transfers between devices with their start and end apart: 22, of which 9 were waited for; matrix products, arithmetic and copies ran while one was open for 0% of the time, Pallas kernels for 16%

profile of v7, /device:TPU:0, one launch (start us, length us, event | category | flops | bytes accessed | tf_op | source)
XLA Modules:
  0.0 68.7 jit_solution(9355504842122986862)
XLA Ops:
  0.0 1.2 %dynamic-slice_bitcast_fusion = bf16[2,2,96,1024]{3,2,1,0:T(8,128)(2,1)S(1)} fusion(bf16[1,2,4,384,1024]{4,3,2,1,0:T(8,128)(2,1)} %u_factors, s32[]{:T(128)S(6)} %select_n.6, s32[]{:T(128)S(6)} %select_n.7), kind=kLoop, calls=%fused_computation | loop fusion | bytes 1572872 | tf_op jit(solution)/shard_map/reshape | solution.py:566
  1.2 0.0 slice-start
  1.2 0.1 fusion
  1.3 3.0 %collective-permute-start.3 = (bf16[2,2,48,1024]{3,2,1,0:T(8,128)(2,1)S(1)}, bf16[2,2,48,1024]{3,2,1,0:T(8,128)(2,1)S(1)}, u32[]{:S(2)}, u32[]{:S(2)}) collective-permute-start(bf16[2,2,48,1024]{3,2,1,0:T(8,128)(2,1)S(1)} %get-tuple-element.106), channel_id=1, source_target_pairs={{0,2},{2,0},{1,3},{3,1},{4,6},{6,4},{5,7},{7,5},{8,10},{10,8},{9,1... | collective-permute-start | bytes 1179656 | tf_op jit(solution)/shard_map/ppermute | solution.py:537
  4.3 0.0 slice-start.1
  4.3 0.0 copy-start
  4.3 0.0 copy-start.1
  4.3 0.1 collective-permute-start.4
  4.4 0.8 %copy-done.3 = s32[16]{0:T(128)S(1)} copy-done((s32[16]{0:T(128)S(1)}, s32[16]{0:T(128)}, u32[]{:S(2)}) %copy-start.3) | copy-done | bytes 88
  5.2 7.5 %forward_products.1 = (bf16[2,96,256]{2,1,0:T(8,128)(2,1)S(1)}, bf16[2,96,256]{2,1,0:T(8,128)(2,1)S(1)}, bf16[2,96,256]{2,1,0:T(8,128)(2,1)S(1)}, bf16[2,96,256]...) custom-call(s32[16]{0:T(128)S(1)} %copy-done.3, ...), custom_call_target="tpu_custom_call" | custom-call | flops 1610612736 | bytes 10485760 | tf_op jit(solution)/shard_map/forward_products/pallas_call | solution.py:226
  12.7 1.5 %collective-permute-done.3.refs_4_ = bf16[2,2,48,1024]{3,2,1,0:T(8,128)(2,1)S(1)} collective-permute-done((bf16[2,2,48,1024]{3,2,1,0:T(8,128)(2,1)S(1)}, bf16[2,2,48,1024]{3,2,1,0:T(8,128)(2,1)S(1)}, u32[]{:S(2)}, u32[]{:S(2)}) %collective-permute-start.3) | collective-permute-done | bytes 393248 | tf_op jit(solution)/shard_map/ppermute | solution.py:537
  14.2 2.1 %collective-permute-start.5 = (bf16[2,2,48,1024]{3,2,1,0:T(8,128)(2,1)S(1)}, bf16[2,2,48,1024]{3,2,1,0:T(8,128)(2,1)S(1)}, u32[]{:S(2)}, u32[]{:S(2)}) collective-permute-start(bf16[2,2,48,1024]{3,2,1,0:T(8,128)(2,1)S(1)} %collective-permute-done.3.refs_4_), channel_id=1, source_target_pairs={{0,16},{16,0},{1,17},{17,1},{2,18},{18,2},{3,19},{19,3},{4,20},{20... | collective-permute-start | bytes 1179656 | tf_op jit(solution)/shard_map/ppermute | solution.py:537
  16.3 1.6 %collective-permute-start = (bf16[2,96,256]{2,1,0:T(8,128)(2,1)S(1)}, bf16[2,96,256]{2,1,0:T(8,128)(2,1)S(1)}, u32[]{:S(2)}, u32[]{:S(2)}) collective-permute-start(bf16[2,96,256]{2,1,0:T(8,128)(2,1)S(1)} %get-tuple-element.59), channel_id=1, source_target_pairs={{0,4},{2,6},{4,0},{6,2},{8,12},{10,14},{12,8},{14,10},{1,5},{3,7},... | collective-permute-start | bytes 294920 | tf_op jit(solution)/shard_map/ppermute | solution.py:570
  17.9 2.6 %collective-permute-start.1 = (bf16[2,96,256]{2,1,0:T(8,128)(2,1)S(1)}, bf16[2,96,256]{2,1,0:T(8,128)(2,1)S(1)}, u32[]{:S(2)}, u32[]{:S(2)}) collective-permute-start(bf16[2,96,256]{2,1,0:T(8,128)(2,1)S(1)} %get-tuple-element.61), channel_id=1, source_target_pairs={{0,8},{2,10},{4,12},{6,14},{8,0},{10,2},{12,4},{14,6},{1,9},{3,11}... | collective-permute-start | bytes 294920 | tf_op jit(solution)/shard_map/ppermute | solution.py:570
  20.5 1.1 %collective-permute-start.2 = (bf16[2,96,256]{2,1,0:T(8,128)(2,1)S(1)}, bf16[2,96,256]{2,1,0:T(8,128)(2,1)S(1)}, u32[]{:S(2)}, u32[]{:S(2)}) collective-permute-start(bf16[2,96,256]{2,1,0:T(8,128)(2,1)S(1)} %get-tuple-element.64), channel_id=1, source_target_pairs={{0,14},{2,12},{4,10},{6,8},{8,6},{10,4},{12,2},{14,0},{1,15},{3,13... | collective-permute-start | bytes 294920 | tf_op jit(solution)/shard_map/ppermute | solution.py:570
  21.6 0.0 slice-done
  21.6 0.0 slice-done.1
  21.6 0.0 copy-done
  21.6 0.0 copy-done.1
  21.6 0.0 copy-done.2
  21.6 1.5 %prepare.1 = (bf16[2,2,384,1024]{3,2,1,0:T(8,128)(2,1)S(1)}, f32[2,16,1024]{2,1,0:T(8,128)S(1)}, bf16[2,384,256]{2,1,0:T(8,128)(2,1)S(1)}) custom-call(s32[16]{0:T(128)S(1)} %copy-done.3, s32[16,16]{1,0:T(8,128)S(1)} %copy-done.2, s32[16,1,1024]{2,1,0:T(1,128)S(1)} %bitcast.7, bf16[2,48,512]{2,1,0:T(8,128)(2,1)S(1)} %copy-done, ...), custom_call_target="tpu_custom_call" | custom-call | bytes 6291456 | tf_op jit(solution)/shard_map/prepare/pallas_call | solution.py:272
  23.2 0.0 collective-permute-done.refs_1_
  23.2 2.3 %collective-permute-done.1.refs_2_ = bf16[2,96,256]{2,1,0:T(8,128)(2,1)S(1)} collective-permute-done((bf16[2,96,256]{2,1,0:T(8,128)(2,1)S(1)}, bf16[2,96,256]{2,1,0:T(8,128)(2,1)S(1)}, u32[]{:S(2)}, u32[]{:S(2)}) %collective-permute-start.1) | collective-permute-done | bytes 98336 | tf_op jit(solution)/shard_map/ppermute | solution.py:570
  25.5 2.4 %collective-permute-done.2.refs_3_ = bf16[2,96,256]{2,1,0:T(8,128)(2,1)S(1)} collective-permute-done((bf16[2,96,256]{2,1,0:T(8,128)(2,1)S(1)}, bf16[2,96,256]{2,1,0:T(8,128)(2,1)S(1)}, u32[]{:S(2)}, u32[]{:S(2)}) %collective-permute-start.2) | collective-permute-done | bytes 98336 | tf_op jit(solution)/shard_map/ppermute | solution.py:570
  27.9 0.0 collective-permute-done.4.refs_6_
  27.9 0.0 collective-permute-done.5.refs_4_
  27.9 0.5 collective-permute-start.10
  28.4 1.6 %collective-permute-start.8 = (bf16[2,96,256]{2,1,0:T(8,128)(2,1)S(1)}, bf16[2,96,256]{2,1,0:T(8,128)(2,1)S(1)}, u32[]{:S(2)}, u32[]{:S(2)}) collective-permute-start(bf16[2,96,256]{2,1,0:T(8,128)(2,1)S(1)} %get-tuple-element.74), channel_id=1, source_target_pairs={{0,10},{2,8},{4,14},{6,12},{8,2},{10,0},{12,6},{14,4},{1,11},{3,9}... | collective-permute-start | bytes 294920 | tf_op jit(solution)/shard_map/ppermute | solution.py:570
  30.0 1.5 %collective-permute-start.6 = (bf16[2,96,256]{2,1,0:T(8,128)(2,1)S(1)}, bf16[2,96,256]{2,1,0:T(8,128)(2,1)S(1)}, u32[]{:S(2)}, u32[]{:S(2)}) collective-permute-start(bf16[2,96,256]{2,1,0:T(8,128)(2,1)S(1)} %get-tuple-element.70), channel_id=1, source_target_pairs={{0,2},{2,0},{4,6},{6,4},{8,10},{10,8},{12,14},{14,12},{1,3},{3,1},... | collective-permute-start | bytes 294920 | tf_op jit(solution)/shard_map/ppermute | solution.py:570
  31.6 1.6 %collective-permute-start.9 = (bf16[2,96,256]{2,1,0:T(8,128)(2,1)S(1)}, bf16[2,96,256]{2,1,0:T(8,128)(2,1)S(1)}, u32[]{:S(2)}, u32[]{:S(2)}) collective-permute-start(bf16[2,96,256]{2,1,0:T(8,128)(2,1)S(1)} %get-tuple-element.75), channel_id=1, source_target_pairs={{0,12},{2,14},{4,8},{6,10},{8,4},{10,6},{12,0},{14,2},{1,13},{3,15... | collective-permute-start | bytes 294920 | tf_op jit(solution)/shard_map/ppermute | solution.py:570
  33.1 1.0 %collective-permute-start.7 = (bf16[2,96,256]{2,1,0:T(8,128)(2,1)S(1)}, bf16[2,96,256]{2,1,0:T(8,128)(2,1)S(1)}, u32[]{:S(2)}, u32[]{:S(2)}) collective-permute-start(bf16[2,96,256]{2,1,0:T(8,128)(2,1)S(1)} %get-tuple-element.72), channel_id=1, source_target_pairs={{0,6},{2,4},{4,2},{6,0},{8,14},{10,12},{12,10},{14,8},{1,7},{3,5},... | collective-permute-start | bytes 294920 | tf_op jit(solution)/shard_map/ppermute | solution.py:570
  34.2 1.7 %collective-permute-done.8.refs_2_ = bf16[2,96,256]{2,1,0:T(8,128)(2,1)S(1)} collective-permute-done((bf16[2,96,256]{2,1,0:T(8,128)(2,1)S(1)}, bf16[2,96,256]{2,1,0:T(8,128)(2,1)S(1)}, u32[]{:S(2)}, u32[]{:S(2)}) %collective-permute-start.8) | collective-permute-done | bytes 98336 | tf_op jit(solution)/shard_map/ppermute | solution.py:570
  35.9 0.0 collective-permute-done.6.refs_0_
  35.9 0.0 collective-permute-start.11
  35.9 0.5 collective-permute-start.12
  36.4 1.7 %collective-permute-done.9.refs_3_ = bf16[2,96,256]{2,1,0:T(8,128)(2,1)S(1)} collective-permute-done((bf16[2,96,256]{2,1,0:T(8,128)(2,1)S(1)}, bf16[2,96,256]{2,1,0:T(8,128)(2,1)S(1)}, u32[]{:S(2)}, u32[]{:S(2)}) %collective-permute-start.9) | collective-permute-done | bytes 98336 | tf_op jit(solution)/shard_map/ppermute | solution.py:570
  38.1 1.1 %own_field.1.own = bf16[2,256,1024]{2,1,0:T(8,128)(2,1)S(1)} custom-call(bf16[2,384,256]{2,1,0:T(8,128)(2,1)S(1)} %get-tuple-element.57.mask, bf16[2,2,384,1024]{3,2,1,0:T(8,128)(2,1)S(1)} %get-tuple-element.84.u_own, bf16[2,96,256]{2,1,0:T(8,128)(2,1)S(1)} %get-tuple-element.69.refs_0_, bf16[2,96,256]{2,1,0:T(8,128)(2,1)S(1)} %collective-permute-done.refs_1_, ...), custom_call_target="tpu_custom_call" | custom-call | flops 805306368 | bytes 1572864 | tf_op jit(solution)/shard_map/own_field/pallas_call | solution.py:316
  39.2 0.0 collective-permute-done.7.refs_1_
  39.2 0.0 collective-permute-done.10.refs_6_
  39.2 0.1 collective-permute-start.13
  39.3 0.5 collective-permute-start.14
  39.8 0.0 collective-permute-done.11.refs_5_
  39.8 0.0 collective-permute-done.12.refs_7_
  39.8 1.1 %near_products.1 = (bf16[2,2,192,1024]{3,2,1,0:T(8,128)(2,1)S(1)}, f32[2,256,1024]{2,1,0:T(8,128)S(1)}) custom-call(bf16[2,384,256]{2,1,0:T(8,128)(2,1)S(1)} %get-tuple-element.57.mask, bf16[2,96,256]{2,1,0:T(8,128)(2,1)S(1)} %collective-permute-done.6.refs_0_, bf16[2,96,256]{2,1,0:T(8,128)(2,1)S(1)} %collective-permute-done.7.refs_1_, ...), custom_call_target="tpu_custom_call" | custom-call | flops 402653184 | bytes 1572864 | tf_op jit(solution)/shard_map/near_products/pallas_call | solution.py:377
  40.9 0.1 collective-permute-done.13.refs_5_
  41.0 0.6 collective-permute-done.14.refs_7_
  41.6 3.4 %receiver_products.1 = (bf16[2,96,256]{2,1,0:T(8,128)(2,1)S(1)}, bf16[2,96,256]{2,1,0:T(8,128)(2,1)S(1)}, bf16[2,96,256]{2,1,0:T(8,128)(2,1)S(1)}, bf16[2,96,256...) custom-call(bf16[2,384,256]{2,1,0:T(8,128)(2,1)S(1)} %get-tuple-elem, ...), custom_call_target="tpu_custom_call" | custom-call | flops 2415919104 | bytes 6291456 | tf_op jit(solution)/shard_map/receiver_products/pallas_call | solution.py:450
  45.0 0.6 collective-permute-start.15
  45.6 0.6 collective-permute-start.16
  46.1 2.4 %collective-permute-start.17 = (bf16[2,96,256]{2,1,0:T(8,128)(2,1)S(1)}, bf16[2,96,256]{2,1,0:T(8,128)(2,1)S(1)}, u32[]{:S(2)}, u32[]{:S(2)}) collective-permute-start(bf16[2,96,256]{2,1,0:T(8,128)(2,1)S(1)} %get-tuple-element.98), channel_id=1, source_target_pairs={{0,6},{2,4},{4,2},{6,0},{8,14},{10,12},{12,10},{14,8},{1,7},{3,5},... | collective-permute-start | bytes 294920 | tf_op jit(solution)/shard_map/ppermute | solution.py:546
  48.6 0.7 collective-permute-start.18
  49.2 2.2 %collective-permute-start.19 = (bf16[2,96,256]{2,1,0:T(8,128)(2,1)S(1)}, bf16[2,96,256]{2,1,0:T(8,128)(2,1)S(1)}, u32[]{:S(2)}, u32[]{:S(2)}) collective-permute-start(bf16[2,96,256]{2,1,0:T(8,128)(2,1)S(1)} %get-tuple-element.100), channel_id=1, source_target_pairs={{0,10},{2,8},{4,14},{6,12},{8,2},{10,0},{12,6},{14,4},{1,11},{3,9}... | collective-permute-start | bytes 294920 | tf_op jit(solution)/shard_map/ppermute | solution.py:546
  51.4 0.0 collective-permute-done.15.refs_1_
  51.4 2.4 %collective-permute-start.20 = (bf16[2,96,256]{2,1,0:T(8,128)(2,1)S(1)}, bf16[2,96,256]{2,1,0:T(8,128)(2,1)S(1)}, u32[]{:S(2)}, u32[]{:S(2)}) collective-permute-start(bf16[2,96,256]{2,1,0:T(8,128)(2,1)S(1)} %get-tuple-element.101), channel_id=1, source_target_pairs={{0,12},{2,14},{4,8},{6,10},{8,4},{10,6},{12,0},{14,2},{1,13},{3,15... | collective-permute-start | bytes 294920 | tf_op jit(solution)/shard_map/ppermute | solution.py:546
  53.9 0.0 collective-permute-done.16.refs_2_
  53.9 2.4 %collective-permute-start.21 = (bf16[2,96,256]{2,1,0:T(8,128)(2,1)S(1)}, bf16[2,96,256]{2,1,0:T(8,128)(2,1)S(1)}, u32[]{:S(2)}, u32[]{:S(2)}) collective-permute-start(bf16[2,96,256]{2,1,0:T(8,128)(2,1)S(1)} %get-tuple-element.102), channel_id=1, source_target_pairs={{0,14},{2,12},{4,10},{6,8},{8,6},{10,4},{12,2},{14,0},{1,15},{3,13... | collective-permute-start | bytes 294920 | tf_op jit(solution)/shard_map/ppermute | solution.py:546
  56.2 0.0 collective-permute-done.17.refs_3_
  56.2 7.0 %collective-permute-done.18.refs_4_ = bf16[2,96,256]{2,1,0:T(8,128)(2,1)S(1)} collective-permute-done((bf16[2,96,256]{2,1,0:T(8,128)(2,1)S(1)}, bf16[2,96,256]{2,1,0:T(8,128)(2,1)S(1)}, u32[]{:S(2)}, u32[]{:S(2)}) %collective-permute-start.18) | collective-permute-done | bytes 98336 | tf_op jit(solution)/shard_map/ppermute | solution.py:546
  63.2 2.0 %collective-permute-done.19.refs_5_ = bf16[2,96,256]{2,1,0:T(8,128)(2,1)S(1)} collective-permute-done((bf16[2,96,256]{2,1,0:T(8,128)(2,1)S(1)}, bf16[2,96,256]{2,1,0:T(8,128)(2,1)S(1)}, u32[]{:S(2)}, u32[]{:S(2)}) %collective-permute-start.19) | collective-permute-done | bytes 98336 | tf_op jit(solution)/shard_map/ppermute | solution.py:546
  65.2 0.0 collective-permute-done.20.refs_6_
  65.2 0.0 collective-permute-done.21.refs_7_
  65.2 0.0 slice-done.2
  65.2 0.0 slice-done.3
  65.2 3.5 %update_products.1 = f32[1,2,128,4096]{3,2,1,0:T(8,128)} custom-call(s32[16]{0:T(128)S(1)} %copy-done.3, bf16[2,96,256]{2,1,0:T(8,128)(2,1)S(1)} %get-tuple-element.95.refs_0_, bf16[2,96,256]{2,1,0:T(8,128)(2,1)S(1)} %collective-permute-done.15.refs_1_, bf16[2,96,256]{2,1,0:T(8,128)(2,1)S(1)} %collective-permute-done.16.refs_2_, ...), custom_call_target="tpu_custom_call" | custom-call | flops 1610612736 | bytes 14680064 | tf_op jit(solution)/shard_map/update_products/pallas_call | solution.py:515
  (6 shorter events, 0.0 us)
Async XLA Ops:
  1.2 20.4 %slice-start = ((s8[6291456]{0:T(1024)(128)(4,1)}), s8[4194304]{0:T(1024)(128)(4,1)S(1)}, s32[]{:S(2)}) async-start(s8[6291456]{0:T(1024)(128)(4,1)} %bitcast.3), calls=%async_computation | async-start | bytes 8388608
  1.3 12.9 %collective-permute-start.3 = (bf16[2,2,48,1024]{3,2,1,0:T(8,128)(2,1)S(1)}, bf16[2,2,48,1024]{3,2,1,0:T(8,128)(2,1)S(1)}, u32[]{:S(2)}, u32[]{:S(2)}) collective-permute-start(bf16[2,2,48,1024]{3,2,1,0:T(8,128)(2,1)S(1)} %get-tuple-element.106), channel_id=1, source_target_pairs={{0,2},{2,0},{1,3},{3,1},{4,6},{6,4},{5,7},{7,5},{8,10},{10,8},{9,1... | collective-permute-start | bytes 1179656 | tf_op jit(solution)/shard_map/ppermute | solution.py:537
  4.3 17.4 %slice-start.1 = ((s8[6291456]{0:T(1024)(128)(4,1)}), s8[2097152]{0:T(1024)(128)(4,1)S(1)}, s32[]{:S(2)}) async-start(s8[6291456]{0:T(1024)(128)(4,1)} %bitcast.3), calls=%async_computation.1 | async-start | bytes 4194304
  4.3 17.4 %copy-start = (bf16[2,48,512]{2,1,0:T(8,128)(2,1)S(1)}, bf16[2,48,512]{2,1,0:T(8,128)(2,1)}, u32[]{:S(2)}) copy-start(bf16[2,48,512]{2,1,0:T(8,128)(2,1)} %constant.24.clone.table) | copy-start | bytes 294916
  4.3 17.4 %copy-start.1 = (s32[16384]{0:T(1024)S(1)}, s32[16384]{0:T(1024)}, u32[]{:S(2)}) copy-start(s32[16384]{0:T(1024)} %param.12) | copy-start | bytes 196612
  4.3 17.4 %copy-start.2 = (s32[16,16]{1,0:T(8,128)S(1)}, s32[16,16]{1,0:T(8,128)}, u32[]{:S(2)}) copy-start(s32[16,16]{1,0:T(8,128)} %ranks.1) | copy-start | bytes 3076
  4.3 23.6 %collective-permute-start.4 = (bf16[2,2,48,1024]{3,2,1,0:T(8,128)(2,1)S(1)}, bf16[2,2,48,1024]{3,2,1,0:T(8,128)(2,1)S(1)}, u32[]{:S(2)}, u32[]{:S(2)}) collective-permute-start(bf16[2,2,48,1024]{3,2,1,0:T(8,128)(2,1)S(1)} %get-tuple-element.105), channel_id=1, source_target_pairs={{0,2},{2,0},{1,3},{3,1},{4,6},{6,4},{5,7},{7,5},{8,10},{10,8},{9,1... | collective-permute-start | bytes 1179656 | tf_op jit(solution)/shard_map/ppermute | solution.py:537
  4.4 0.8 %copy-start.3 = (s32[16]{0:T(128)S(1)}, s32[16]{0:T(128)}, u32[]{:S(2)}) copy-start(s32[16]{0:T(128)} %owners.3) | copy-start | bytes 196
  14.2 13.7 %collective-permute-start.5 = (bf16[2,2,48,1024]{3,2,1,0:T(8,128)(2,1)S(1)}, bf16[2,2,48,1024]{3,2,1,0:T(8,128)(2,1)S(1)}, u32[]{:S(2)}, u32[]{:S(2)}) collective-permute-start(bf16[2,2,48,1024]{3,2,1,0:T(8,128)(2,1)S(1)} %collective-permute-done.3.refs_4_), channel_id=1, source_target_pairs={{0,16},{16,0},{1,17},{17,1},{2,18},{18,2},{3,19},{19,3},{4,20},{20... | collective-permute-start | bytes 1179656 | tf_op jit(solution)/shard_map/ppermute | solution.py:537
  16.3 6.9 %collective-permute-start = (bf16[2,96,256]{2,1,0:T(8,128)(2,1)S(1)}, bf16[2,96,256]{2,1,0:T(8,128)(2,1)S(1)}, u32[]{:S(2)}, u32[]{:S(2)}) collective-permute-start(bf16[2,96,256]{2,1,0:T(8,128)(2,1)S(1)} %get-tuple-element.59), channel_id=1, source_target_pairs={{0,4},{2,6},{4,0},{6,2},{8,12},{10,14},{12,8},{14,10},{1,5},{3,7},... | collective-permute-start | bytes 294920 | tf_op jit(solution)/shard_map/ppermute | solution.py:570
  17.9 7.6 %collective-permute-start.1 = (bf16[2,96,256]{2,1,0:T(8,128)(2,1)S(1)}, bf16[2,96,256]{2,1,0:T(8,128)(2,1)S(1)}, u32[]{:S(2)}, u32[]{:S(2)}) collective-permute-start(bf16[2,96,256]{2,1,0:T(8,128)(2,1)S(1)} %get-tuple-element.61), channel_id=1, source_target_pairs={{0,8},{2,10},{4,12},{6,14},{8,0},{10,2},{12,4},{14,6},{1,9},{3,11}... | collective-permute-start | bytes 294920 | tf_op jit(solution)/shard_map/ppermute | solution.py:570
  20.5 7.4 %collective-permute-start.2 = (bf16[2,96,256]{2,1,0:T(8,128)(2,1)S(1)}, bf16[2,96,256]{2,1,0:T(8,128)(2,1)S(1)}, u32[]{:S(2)}, u32[]{:S(2)}) collective-permute-start(bf16[2,96,256]{2,1,0:T(8,128)(2,1)S(1)} %get-tuple-element.64), channel_id=1, source_target_pairs={{0,14},{2,12},{4,10},{6,8},{8,6},{10,4},{12,2},{14,0},{1,15},{3,13... | collective-permute-start | bytes 294920 | tf_op jit(solution)/shard_map/ppermute | solution.py:570
  27.9 11.3 %collective-permute-start.10 = (bf16[2,2,48,1024]{3,2,1,0:T(8,128)(2,1)S(1)}, bf16[2,2,48,1024]{3,2,1,0:T(8,128)(2,1)S(1)}, u32[]{:S(2)}, u32[]{:S(2)}) collective-permute-start(bf16[2,2,48,1024]{3,2,1,0:T(8,128)(2,1)S(1)} %collective-permute-done.4.refs_6_), channel_id=1, source_target_pairs={{0,16},{16,0},{1,17},{17,1},{2,18},{18,2},{3,19},{19,3},{4,20},{20... | collective-permute-start | bytes 1179656 | tf_op jit(solution)/shard_map/ppermute | solution.py:537
  28.4 7.5 %collective-permute-start.8 = (bf16[2,96,256]{2,1,0:T(8,128)(2,1)S(1)}, bf16[2,96,256]{2,1,0:T(8,128)(2,1)S(1)}, u32[]{:S(2)}, u32[]{:S(2)}) collective-permute-start(bf16[2,96,256]{2,1,0:T(8,128)(2,1)S(1)} %get-tuple-element.74), channel_id=1, source_target_pairs={{0,10},{2,8},{4,14},{6,12},{8,2},{10,0},{12,6},{14,4},{1,11},{3,9}... | collective-permute-start | bytes 294920 | tf_op jit(solution)/shard_map/ppermute | solution.py:570
  30.0 5.8 %collective-permute-start.6 = (bf16[2,96,256]{2,1,0:T(8,128)(2,1)S(1)}, bf16[2,96,256]{2,1,0:T(8,128)(2,1)S(1)}, u32[]{:S(2)}, u32[]{:S(2)}) collective-permute-start(bf16[2,96,256]{2,1,0:T(8,128)(2,1)S(1)} %get-tuple-element.70), channel_id=1, source_target_pairs={{0,2},{2,0},{4,6},{6,4},{8,10},{10,8},{12,14},{14,12},{1,3},{3,1},... | collective-permute-start | bytes 294920 | tf_op jit(solution)/shard_map/ppermute | solution.py:570
  31.6 6.5 %collective-permute-start.9 = (bf16[2,96,256]{2,1,0:T(8,128)(2,1)S(1)}, bf16[2,96,256]{2,1,0:T(8,128)(2,1)S(1)}, u32[]{:S(2)}, u32[]{:S(2)}) collective-permute-start(bf16[2,96,256]{2,1,0:T(8,128)(2,1)S(1)} %get-tuple-element.75), channel_id=1, source_target_pairs={{0,12},{2,14},{4,8},{6,10},{8,4},{10,6},{12,0},{14,2},{1,13},{3,15... | collective-permute-start | bytes 294920 | tf_op jit(solution)/shard_map/ppermute | solution.py:570
  33.1 6.1 %collective-permute-start.7 = (bf16[2,96,256]{2,1,0:T(8,128)(2,1)S(1)}, bf16[2,96,256]{2,1,0:T(8,128)(2,1)S(1)}, u32[]{:S(2)}, u32[]{:S(2)}) collective-permute-start(bf16[2,96,256]{2,1,0:T(8,128)(2,1)S(1)} %get-tuple-element.72), channel_id=1, source_target_pairs={{0,6},{2,4},{4,2},{6,0},{8,14},{10,12},{12,10},{14,8},{1,7},{3,5},... | collective-permute-start | bytes 294920 | tf_op jit(solution)/shard_map/ppermute | solution.py:570
  35.9 3.9 %collective-permute-start.11 = (bf16[2,2,48,1024]{3,2,1,0:T(8,128)(2,1)S(1)}, bf16[2,2,48,1024]{3,2,1,0:T(8,128)(2,1)S(1)}, u32[]{:S(2)}, u32[]{:S(2)}) collective-permute-start(bf16[2,2,48,1024]{3,2,1,0:T(8,128)(2,1)S(1)} %collective-permute-done.3.refs_4_), channel_id=1, source_target_pairs={{0,1},{1,0},{2,3},{3,2},{4,5},{5,4},{6,7},{7,6},{8,9},{9,8},{10,11... | collective-permute-start | bytes 1179656 | tf_op jit(solution)/shard_map/ppermute | solution.py:537
  35.9 3.9 %collective-permute-start.12 = (bf16[2,2,48,1024]{3,2,1,0:T(8,128)(2,1)S(1)}, bf16[2,2,48,1024]{3,2,1,0:T(8,128)(2,1)S(1)}, u32[]{:S(2)}, u32[]{:S(2)}) collective-permute-start(bf16[2,2,48,1024]{3,2,1,0:T(8,128)(2,1)S(1)} %collective-permute-done.4.refs_6_), channel_id=1, source_target_pairs={{0,1},{1,0},{2,3},{3,2},{4,5},{5,4},{6,7},{7,6},{8,9},{9,8},{10,11... | collective-permute-start | bytes 1179656 | tf_op jit(solution)/shard_map/ppermute | solution.py:537
  39.2 1.8 %collective-permute-start.13 = (bf16[2,2,48,1024]{3,2,1,0:T(8,128)(2,1)S(1)}, bf16[2,2,48,1024]{3,2,1,0:T(8,128)(2,1)S(1)}, u32[]{:S(2)}, u32[]{:S(2)}) collective-permute-start(bf16[2,2,48,1024]{3,2,1,0:T(8,128)(2,1)S(1)} %collective-permute-done.5.refs_4_), channel_id=1, source_target_pairs={{0,1},{1,0},{2,3},{3,2},{4,5},{5,4},{6,7},{7,6},{8,9},{9,8},{10,11... | collective-permute-start | bytes 1179656 | tf_op jit(solution)/shard_map/ppermute | solution.py:537
  39.3 2.3 %collective-permute-start.14 = (bf16[2,2,48,1024]{3,2,1,0:T(8,128)(2,1)S(1)}, bf16[2,2,48,1024]{3,2,1,0:T(8,128)(2,1)S(1)}, u32[]{:S(2)}, u32[]{:S(2)}) collective-permute-start(bf16[2,2,48,1024]{3,2,1,0:T(8,128)(2,1)S(1)} %collective-permute-done.10.refs_6_), channel_id=1, source_target_pairs={{0,1},{1,0},{2,3},{3,2},{4,5},{5,4},{6,7},{7,6},{8,9},{9,8},{10,11... | collective-permute-start | bytes 1179656 | tf_op jit(solution)/shard_map/ppermute | solution.py:537
  39.8 25.4 %slice-start.2 = ((s8[6291456]{0:T(1024)(128)(4,1)}), s8[4194304]{0:T(1024)(128)(4,1)S(1)}, s32[]{:S(2)}) async-start(s8[6291456]{0:T(1024)(128)(4,1)} %bitcast.5), calls=%async_computation.2 | async-start | bytes 8388608
  41.6 23.6 %slice-start.3 = ((s8[6291456]{0:T(1024)(128)(4,1)}), s8[2097152]{0:T(1024)(128)(4,1)S(1)}, s32[]{:S(2)}) async-start(s8[6291456]{0:T(1024)(128)(4,1)} %bitcast.5), calls=%async_computation.3 | async-start | bytes 4194304
  45.0 6.4 %collective-permute-start.15 = (bf16[2,96,256]{2,1,0:T(8,128)(2,1)S(1)}, bf16[2,96,256]{2,1,0:T(8,128)(2,1)S(1)}, u32[]{:S(2)}, u32[]{:S(2)}) collective-permute-start(bf16[2,96,256]{2,1,0:T(8,128)(2,1)S(1)} %get-tuple-element.96), channel_id=1, source_target_pairs={{0,2},{2,0},{4,6},{6,4},{8,10},{10,8},{12,14},{14,12},{1,3},{3,1},... | collective-permute-start | bytes 294920 | tf_op jit(solution)/shard_map/ppermute | solution.py:546
  45.6 8.3 %collective-permute-start.16 = (bf16[2,96,256]{2,1,0:T(8,128)(2,1)S(1)}, bf16[2,96,256]{2,1,0:T(8,128)(2,1)S(1)}, u32[]{:S(2)}, u32[]{:S(2)}) collective-permute-start(bf16[2,96,256]{2,1,0:T(8,128)(2,1)S(1)} %get-tuple-element.97), channel_id=1, source_target_pairs={{0,4},{2,6},{4,0},{6,2},{8,12},{10,14},{12,8},{14,10},{1,5},{3,7},... | collective-permute-start | bytes 294920 | tf_op jit(solution)/shard_map/ppermute | solution.py:546
  46.1 10.1 %collective-permute-start.17 = (bf16[2,96,256]{2,1,0:T(8,128)(2,1)S(1)}, bf16[2,96,256]{2,1,0:T(8,128)(2,1)S(1)}, u32[]{:S(2)}, u32[]{:S(2)}) collective-permute-start(bf16[2,96,256]{2,1,0:T(8,128)(2,1)S(1)} %get-tuple-element.98), channel_id=1, source_target_pairs={{0,6},{2,4},{4,2},{6,0},{8,14},{10,12},{12,10},{14,8},{1,7},{3,5},... | collective-permute-start | bytes 294920 | tf_op jit(solution)/shard_map/ppermute | solution.py:546
  48.6 14.6 %collective-permute-start.18 = (bf16[2,96,256]{2,1,0:T(8,128)(2,1)S(1)}, bf16[2,96,256]{2,1,0:T(8,128)(2,1)S(1)}, u32[]{:S(2)}, u32[]{:S(2)}) collective-permute-start(bf16[2,96,256]{2,1,0:T(8,128)(2,1)S(1)} %get-tuple-element.99), channel_id=1, source_target_pairs={{0,8},{2,10},{4,12},{6,14},{8,0},{10,2},{12,4},{14,6},{1,9},{3,11}... | collective-permute-start | bytes 294920 | tf_op jit(solution)/shard_map/ppermute | solution.py:546
  49.2 15.9 %collective-permute-start.19 = (bf16[2,96,256]{2,1,0:T(8,128)(2,1)S(1)}, bf16[2,96,256]{2,1,0:T(8,128)(2,1)S(1)}, u32[]{:S(2)}, u32[]{:S(2)}) collective-permute-start(bf16[2,96,256]{2,1,0:T(8,128)(2,1)S(1)} %get-tuple-element.100), channel_id=1, source_target_pairs={{0,10},{2,8},{4,14},{6,12},{8,2},{10,0},{12,6},{14,4},{1,11},{3,9}... | collective-permute-start | bytes 294920 | tf_op jit(solution)/shard_map/ppermute | solution.py:546
  51.4 13.8 %collective-permute-start.20 = (bf16[2,96,256]{2,1,0:T(8,128)(2,1)S(1)}, bf16[2,96,256]{2,1,0:T(8,128)(2,1)S(1)}, u32[]{:S(2)}, u32[]{:S(2)}) collective-permute-start(bf16[2,96,256]{2,1,0:T(8,128)(2,1)S(1)} %get-tuple-element.101), channel_id=1, source_target_pairs={{0,12},{2,14},{4,8},{6,10},{8,4},{10,6},{12,0},{14,2},{1,13},{3,15... | collective-permute-start | bytes 294920 | tf_op jit(solution)/shard_map/ppermute | solution.py:546
  53.9 11.3 %collective-permute-start.21 = (bf16[2,96,256]{2,1,0:T(8,128)(2,1)S(1)}, bf16[2,96,256]{2,1,0:T(8,128)(2,1)S(1)}, u32[]{:S(2)}, u32[]{:S(2)}) collective-permute-start(bf16[2,96,256]{2,1,0:T(8,128)(2,1)S(1)} %get-tuple-element.102), channel_id=1, source_target_pairs={{0,14},{2,12},{4,10},{6,8},{8,6},{10,4},{12,2},{14,0},{1,15},{3,13... | collective-permute-start | bytes 294920 | tf_op jit(solution)/shard_map/ppermute | solution.py:546
